TPU v7x, 256 devices: a whole 4x4x8 slice. The times are simulated.
256 devices in a mesh: dp: 32 (over x, y, core), expert: 8 (over z).
Axes of the slice: x: 4, y: 4, z: 8, core: 2. Of those that a mesh axis runs over, the one named last changes fastest.
Arguments:
- grad: bfloat16 [8, 32, 256, 8192], P('expert', 'dp'), may hold values from -23 to 23, as said below
- error: bfloat16 [8, 32, 256, 8192], P('expert', 'dp'), may hold values from -3 to 3
- q_init: bfloat16 [8, 32, 8192], P('expert'), may hold values from -4 to 4
Outputs:
- basis_out: float32 [8, 256, 32], P('expert')
- q_factor: float32 [8, 32, 8192], P('expert', None, 'dp')
- new_error: bfloat16 [8, 32, 256, 8192], P('expert', 'dp')
- error_norm: float32 [], replicated
Inputs may be any that keep to these rules, and one draw needn't show every extreme that they name: `grad`: entries of each expert's gradient.
All inputs are finite; a program needn't handle non-finite values.
Results may differ from a plain program's by a relative error of at most 0.02.
Values may be sent and summed in bfloat16 or wider, within the bound.
No kernel may reach another device: no remote copies, remote signals or barrier semaphores. Data moves between devices by JAX's collectives and lax.ppermute only.
A program may use at most 64 MiB of HBM per device.

v0:
```python
import jax
import jax.numpy as jnp
from jax import lax
from jax.sharding import PartitionSpec as P

ITERS = 2


def make_orthonormal(lower_factor, projected):
    solved = jax.scipy.linalg.solve_triangular(
        lower_factor, jnp.swapaxes(projected, 1, 2), lower=True
    )
    return jnp.swapaxes(solved, 1, 2)


def gram_of(projected):
    return jnp.einsum("erk,erj->ekj", projected, projected, precision=lax.Precision.HIGHEST)


def local(grad, error, q_init):
    combined = (grad[:, 0].astype(jnp.float32) + error[:, 0].astype(jnp.float32)).astype(
        jnp.bfloat16
    )
    replicas = lax.axis_size("dp")
    groups = lax.axis_size("expert")
    share_width = combined.shape[2] // replicas
    factor_low = q_init
    orthonormal = jnp.zeros((combined.shape[0], combined.shape[1], q_init.shape[1]), jnp.float32)
    ortho_low = orthonormal.astype(jnp.bfloat16)
    factor_share = jnp.zeros((q_init.shape[0], q_init.shape[1], share_width), jnp.float32)
    for step in range(ITERS):
        partial_value = jnp.einsum(
            "erf,ekf->erk", combined, factor_low, preferred_element_type=jnp.float32
        )
        projected = lax.psum(partial_value, "dp") / replicas
        lower_factor = jnp.linalg.cholesky(gram_of(projected))
        orthonormal = make_orthonormal(lower_factor, projected)
        ortho_low = orthonormal.astype(jnp.bfloat16)
        right_part = jnp.einsum(
            "erk,erf->ekf", ortho_low, combined, preferred_element_type=jnp.float32
        )
        factor_full = lax.psum(right_part.astype(jnp.bfloat16), "dp").astype(jnp.float32) / replicas
        factor_low = factor_full.astype(jnp.bfloat16)
        factor_share = lax.dynamic_slice_in_dim(
            factor_full, lax.axis_index("dp") * share_width, share_width, 2
        )
    approx = jnp.einsum("erk,ekf->erf", ortho_low, factor_low, preferred_element_type=jnp.float32)
    new_error = (combined.astype(jnp.float32) - approx).astype(jnp.bfloat16)
    local_sum = jnp.sum(jnp.square(new_error.astype(jnp.float32)))
    total = lax.psum(local_sum, ("dp", "expert"))
    count = combined.shape[0] * combined.shape[1] * combined.shape[2] * replicas * groups
    error_norm = jnp.sqrt(total / count)
    return (orthonormal, factor_share, new_error[:, None], error_norm)


def solution(mesh):
    placed = (P("expert", "dp", None, None), P("expert", "dp", None, None), P("expert", None, None))
    return jax.shard_map(
        local,
        mesh=mesh,
        in_specs=placed,
        out_specs=(
            P("expert", None, None),
            P("expert", None, "dp"),
            P("expert", "dp", None, None),
            P(),
        ),
        check_vma=False,
    )
```

profile of v0, /device:TPU:1, one launch (start us, length us, event | category | flops | bytes accessed | tf_op | source)
XLA Modules:
  0.0 612.2 jit_solution(11681528760471083051)
XLA Ops:
  7.2 0.0 all-reduce.3.cloned.1.call-start
  7.2 5.1 fusion.3
  12.3 2.0 copy-done.1
  14.3 1.4 convolution_bitcast_fusion.3
  15.7 124.2 %psum.35 = f32[1,256,32]{1,2,0:T(8,128)S(1)} all-reduce(f32[1,256,32]{1,2,0:T(8,128)S(1)} %convolution_bitcast_fusion.3), channel_id=1, replica_groups=mesh['dp'=32,'expert'=8] {'dp'}, use_global_device_ids=true, to_apply=%region_0.0 | all-reduce | flops 8192 | bytes 65536 | tf_op jit(solution)/shard_map/psum | solution.py:35
  139.9 0.2 fusion.16
  140.1 0.1 copy.8
  140.2 2.9 custom-call.8
  143.1 0.6 compare_reduce_fusion.1
  143.8 0.7 select_select_fusion.1
  144.4 2.4 custom-call.9
  146.8 0.2 fusion.5
  147.1 3.8 fusion.1
  150.9 0.0 all-reduce.3.cloned.1.call-update
  151.0 0.0 all-reduce.5.cloned.1.call-start
  151.0 116.5 %all-reduce.3.cloned.1.call-done = bf16[1,32,8192]{2,1,0:T(8,128)(2,1)} async-done(((bf16[1,32,8192]{2,1,0:T(8,128)(2,1)}), bf16[1,32,8192]{2,1,0:T(8,128)(2,1)}) %all-reduce.3.cloned.1.call-update) | async-done | bytes 524304 | tf_op jit(solution)/shard_map/psum | solution.py:42
  267.5 3.7 convolution_bitcast_fusion.1
  271.2 122.2 %psum.37 = f32[1,256,32]{1,2,0:T(8,128)S(1)} all-reduce(f32[1,256,32]{1,2,0:T(8,128)S(1)} %convolution_bitcast_fusion.1), channel_id=1, replica_groups=mesh['dp'=32,'expert'=8] {'dp'}, use_global_device_ids=true, to_apply=%region_4.0 | all-reduce | flops 8192 | bytes 65536 | tf_op jit(solution)/shard_map/psum | solution.py:35
  393.4 0.2 fusion.14
  393.6 0.1 copy.10
  393.7 2.9 custom-call.10
  396.6 0.6 compare_reduce_fusion
  397.3 0.7 select_select_fusion
  397.9 2.4 custom-call.11
  400.4 0.2 convolution_bitcast_fusion
  400.6 3.8 fusion.2
  404.5 0.0 all-reduce.5.cloned.1.call-update
  404.5 115.1 %all-reduce.5.cloned.1.call-done = bf16[1,32,8192]{2,1,0:T(8,128)(2,1)} async-done(((bf16[1,32,8192]{2,1,0:T(8,128)(2,1)}), bf16[1,32,8192]{2,1,0:T(8,128)(2,1)}) %all-reduce.5.cloned.1.call-update) | async-done | bytes 524304 | tf_op jit(solution)/shard_map/psum | solution.py:42
  519.6 6.4 %multiply_reduce_fusion = (f32[]{:T(128)}, bf16[256,8192]{1,0:T(8,128)(2,1)}) fusion(bf16[1,32,8192]{2,1,0:T(8,128)(2,1)} %all-reduce.5.cloned.1.call-done, f32[1,256,32]{1,2,0:T(8,128)S(1)} %convolution_bitcast_fusion, bf16[256,8192]{1,0:T(8,128)(2,1)} %copy-done.1), kind=kOutput, calls=%fused_computation.6 | convolution fusion | flops 147595264 | bytes 8945668 | tf_op jit(solution)/shard_map/erk,ekf->erf/dot_general | solution.py:47
  526.0 76.8 %psum.39 = f32[]{:T(128)} all-reduce(f32[]{:T(128)} %get-tuple-element.6), channel_id=1, replica_groups=mesh['dp'=32,'expert'=8] {'dp','expert'}, use_global_device_ids=true, to_apply=%region_7.10 | all-reduce | flops 1 | bytes 8 | tf_op jit(solution)/shard_map/psum | solution.py:50
  603.5 0.1 convert_multiply_fusion
  603.6 0.6 constant_dynamic-slice_fusion
  (11 shorter events, 0.1 us)
Async XLA Ops:
  7.2 7.1 %copy-start = (bf16[1,32,8192]{2,1,0:T(8,128)(2,1)S(1)}, bf16[1,32,8192]{2,1,0:T(8,128)(2,1)}, u32[]{:S(2)}) copy-start(bf16[1,32,8192]{2,1,0:T(8,128)(2,1)} %param.8) | copy-start | bytes 1572868
  7.2 260.3 %all-reduce.3.cloned.1.call-start = ((), (), s32[]{:S(2)}) async-start(), calls=%async_computation | async-start | bytes 1048576 | tf_op jit(solution)/shard_map/psum | solution.py:42
  12.3 2.0 copy-start.1
  151.0 368.6 %all-reduce.5.cloned.1.call-start = ((), (), s32[]{:S(2)}) async-start(), calls=%async_computation.1 | async-start | bytes 1048576 | tf_op jit(solution)/shard_map/psum | solution.py:42
  400.6 125.4 %copy-start.3 = (f32[1,256,32]{1,2,0:T(8,128)}, f32[1,256,32]{1,2,0:T(8,128)S(1)}, u32[]{:S(2)}) copy-start(f32[1,256,32]{1,2,0:T(8,128)S(1)} %convolution_bitcast_fusion) | copy-start | bytes 98308
  519.6 83.9 %copy-start.2 = (bf16[1,32,8192]{2,1,0:T(8,128)(2,1)S(1)}, bf16[1,32,8192]{2,1,0:T(8,128)(2,1)}, u32[]{:S(2)}) copy-start(bf16[1,32,8192]{2,1,0:T(8,128)(2,1)} %all-reduce.5.cloned.1.call-done) | copy-start | bytes 1572868
Sparse Core Ops, SparseCore 0:
  151.1 116.3 all-reduce.2
  404.6 114.9 all-reduce.4
where the time goes:
time: 613 us; the launch traced here: 612 us
  blocking collectives  323 us (53%)
  waiting for transfers between devices  232 us (38%)
  matrix products  19.9 us (3%)
  other arithmetic  18.5 us (3%)
  between operations  16 us (3%)
    psum x2, blocking collectives, local(): projected = lax.psum(partial_value, 'dp') / replicas  246 us
    psum x2, waiting for transfers between devices, local(): lax.psum(right_part.astype(jnp.bfloat16), 'dp').astype(jnp.float32)  232 us
    psum x1, blocking collectives, local(): total = lax.psum(local_sum, ('dp', 'expert'))  76.8 us
  transfers between devices with their start and end apart: 2, of which 2 were waited for; matrix products, arithmetic and copies ran while one was open for 0% of the time, Pallas kernels for 0%

commit v1 on v0

v1 whole, which is shorter than its diff:
```python
import functools

import jax
import jax.numpy as jnp
import numpy as np
from jax import lax
from jax.experimental import pallas as pl
from jax.experimental.pallas import tpu as pltpu
from jax.sharding import Mesh
from jax.sharding import PartitionSpec as P

F32 = jnp.float32
BF16 = jnp.bfloat16
HIGHEST = lax.Precision.HIGHEST
CHIPS = ("x", "y")
ALL = ("x", "y", "core", "expert")
VMEM_LIMIT = 48 * 1024 * 1024

NN = (((1,), (0,)), ((), ()))
NT = (((1,), (1,)), ((), ()))
TN = (((0,), (0,)), ((), ()))


def call(body, name, flops, moved, **kw):
    return pl.pallas_call(
        body,
        name=name,
        compiler_params=pltpu.CompilerParams(vmem_limit_bytes=VMEM_LIMIT),
        cost_estimate=pl.CostEstimate(flops=flops, bytes_accessed=moved, transcendentals=0),
        **kw,
    )


def combine(grad, error, q_init, parity, name):
    rows, ff = grad.shape
    rank = q_init.shape[0]
    width = 256
    pairs = ff // (2 * width)
    per = 2
    parity = jnp.reshape(parity, (1,)).astype(jnp.int32)

    def body(par_ref, *refs):
        g, e, q = refs[:per], refs[per : 2 * per], refs[2 * per : 3 * per]
        c_ref, p_ref = refs[3 * per :]
        step = pl.program_id(0)
        part = jnp.zeros((rank, rows), F32)
        for i in range(per):
            c = (g[i][...].astype(F32) + e[i][...].astype(F32)).astype(BF16)
            c_ref[i] = c
            part += lax.dot_general(q[i][...], c, NT, preferred_element_type=F32)

        @pl.when(step == 0)
        def _():
            p_ref[...] = part

        @pl.when(step > 0)
        def _():
            p_ref[...] += part

    def block(height, i):
        return pl.BlockSpec((height, width), lambda s, par: (0, 2 * (s * per + i) + par[0]))

    return call(
        body,
        name,
        2 * rows * rank * ff // 2,
        6 * rows * ff // 2,
        grid_spec=pltpu.PrefetchScalarGridSpec(
            num_scalar_prefetch=1,
            grid=(pairs // per,),
            in_specs=[block(rows, i) for i in range(per)] * 2 + [block(rank, i) for i in range(per)],
            out_specs=[
                pl.BlockSpec((per, rows, width), lambda s, par: (s, 0, 0)),
                pl.BlockSpec((rank, rows), lambda s, par: (0, 0)),
            ],
        ),
        out_shape=(
            jax.ShapeDtypeStruct((pairs, rows, width), BF16),
            jax.ShapeDtypeStruct((rank, rows), F32),
        ),
    )(parity, *([grad] * per), *([error] * per), *([q_init] * per))


def lanes_of(x):
    x = x.reshape(x.shape[0] // 8, 8, x.shape[1])
    x = jnp.sum(x, axis=0)
    return x[:, :128] + x[:, 128:]


def pair_sum(mine, other):
    pairs, rows, width = mine.shape
    per = 4

    def body(a_ref, b_ref, s_ref, d_ref):
        step = pl.program_id(0)
        part = jnp.zeros((8, 128), F32)
        for i in range(per):
            a, b = a_ref[i].astype(F32), b_ref[i].astype(F32)
            s_ref[i] = (a + b).astype(BF16)
            d = a - b
            part += lanes_of(d * d)
        part = 0.5 * part

        @pl.when(step == 0)
        def _():
            d_ref[...] = part

        @pl.when(step > 0)
        def _():
            d_ref[...] += part

    spec = pl.BlockSpec((per, rows, width), lambda s: (s, 0, 0))
    return call(
        body,
        "pair_sum",
        6 * mine.size,
        6 * mine.size,
        grid=(pairs // per,),
        in_specs=[spec, spec],
        out_specs=[spec, pl.BlockSpec((8, 128), lambda s: (0, 0))],
        out_shape=(
            jax.ShapeDtypeStruct(mine.shape, BF16),
            jax.ShapeDtypeStruct((8, 128), F32),
        ),
    )(mine, other)


def eliminate(p):
    rank = p.shape[0]
    g = lax.dot_general(p, p, NT, precision=HIGHEST, preferred_element_type=F32)
    row = lax.broadcasted_iota(jnp.int32, (rank, 1), 0)
    pivots = jnp.zeros((rank, 1), F32)
    for k in range(rank):
        column = g[:, k : k + 1]
        pivot = g[k : k + 1, k : k + 1]
        pivots = jnp.where(row == k, pivot, pivots)
        if k < rank - 1:
            factor = jnp.where(row > k, column / pivot, 0.0)
            g, p = g - factor * g[k : k + 1, :], p - factor * p[k : k + 1, :]
    return p / jnp.sqrt(pivots)


def orthonormal_of(parts, replicas):
    chips, rank, rows = parts.shape

    def body(p_ref, o_ref):
        o_ref[...] = eliminate(jnp.sum(p_ref[...], axis=0) * (1.0 / replicas))

    return call(
        body,
        "orthonormal",
        2 * rank * rank * rows,
        4 * parts.size,
        out_shape=jax.ShapeDtypeStruct((rank, rows), F32),
    )(parts)


def first_right(sums, ortho_t, replicas):
    chips, rows, width = sums.shape
    rank = ortho_t.shape[0]
    per = 4

    def body(s_ref, o_ref, mean_ref, p_ref):
        step = pl.program_id(0)
        total = jnp.sum(s_ref[...].astype(F32), axis=0)

        @pl.when(step == 0)
        def _():
            mean_ref[...] = total

        @pl.when(step > 0)
        def _():
            mean_ref[...] += total

        @pl.when(step == chips // per - 1)
        def _():
            mean = mean_ref[...] * (1.0 / replicas)
            mean_ref[...] = mean
            ortho_low = o_ref[...].astype(BF16).astype(F32)
            q = lax.dot_general(ortho_low, mean, NN, precision=HIGHEST, preferred_element_type=F32)
            low = q.astype(BF16).astype(F32)
            p_ref[...] = lax.dot_general(low, mean, NT, precision=HIGHEST, preferred_element_type=F32)

    return call(
        body,
        "first_right",
        4 * rank * rows * width,
        2 * sums.size,
        grid=(chips // per,),
        in_specs=[
            pl.BlockSpec((per, rows, width), lambda s: (s, 0, 0)),
            pl.BlockSpec((rank, rows), lambda s: (0, 0)),
        ],
        out_specs=[
            pl.BlockSpec((rows, width), lambda s: (0, 0)),
            pl.BlockSpec((rank, rows), lambda s: (0, 0)),
        ],
        out_shape=(
            jax.ShapeDtypeStruct((rows, width), F32),
            jax.ShapeDtypeStruct((rank, rows), F32),
        ),
    )(sums, ortho_t)


def second_right(parts, mean):
    chips, rank, rows = parts.shape
    width = mean.shape[1]

    def body(p_ref, m_ref, o_ref, low_ref, q_ref, f_ref):
        ortho_t = eliminate(jnp.sum(p_ref[...], axis=0))
        o_ref[...] = ortho_t
        low_t = ortho_t.astype(BF16)
        low_ref[...] = low_t.astype(F32).T.astype(BF16)
        q = lax.dot_general(low_t.astype(F32), m_ref[...], NN, precision=HIGHEST, preferred_element_type=F32)
        q_ref[...] = q
        f_ref[...] = jnp.broadcast_to(q.astype(BF16)[None], f_ref.shape)

    return call(
        body,
        "second_right",
        4 * rank * rows * width,
        4 * parts.size,
        out_shape=(
            jax.ShapeDtypeStruct((rank, rows), F32),
            jax.ShapeDtypeStruct((rows, rank), BF16),
            jax.ShapeDtypeStruct((rank, width), F32),
            jax.ShapeDtypeStruct((chips, rank, width), BF16),
        ),
    )(parts, mean)


def squares(sums, low, q, halves, copies):
    chips, rows, width = sums.shape
    per = 4

    def body(s_ref, low_ref, q_ref, h_ref, out_ref, a_ref, acc_ref):
        step = pl.program_id(0)

        @pl.when(step == 0)
        def _():
            a_ref[...] = 2.0 * lax.dot_general(
                low_ref[...], q_ref[...].astype(BF16), NN, preferred_element_type=F32
            )
            acc_ref[...] = h_ref[...]

        part = jnp.zeros((8, 128), F32)
        for i in range(per):
            d = s_ref[i].astype(F32) - a_ref[...]
            part += lanes_of(d * d)
        acc_ref[...] += 0.5 * part

        @pl.when(step == chips // per - 1)
        def _():
            out_ref[...] = jnp.broadcast_to(jnp.sum(acc_ref[...], axis=0, keepdims=True), out_ref.shape)

    return call(
        body,
        "squares",
        4 * sums.size,
        2 * sums.size,
        grid=(chips // per,),
        in_specs=[
            pl.BlockSpec((per, rows, width), lambda s: (s, 0, 0)),
            pl.BlockSpec(low.shape, lambda s: (0, 0)),
            pl.BlockSpec(q.shape, lambda s: (0, 0)),
            pl.BlockSpec((8, 128), lambda s: (0, 0)),
        ],
        out_specs=pl.BlockSpec((copies, 128), lambda s: (0, 0)),
        out_shape=jax.ShapeDtypeStruct((copies, 128), F32),
        scratch_shapes=[pltpu.VMEM((rows, width), F32), pltpu.VMEM((8, 128), F32)],
    )(sums, low, q, halves)


def residual(mine, other, low, f_mine, f_other, core):
    pairs, rows, width = mine.shape
    rank = low.shape[1]
    core = jnp.reshape(core, (1,)).astype(jnp.int32)
    per = 1

    def body(core_ref, a_ref, b_ref, low_ref, fa_ref, fb_ref, out_ref):
        low_v = low_ref[...]
        new_a = (
            a_ref[0].astype(F32)
            - lax.dot_general(low_v, fa_ref[0], NN, preferred_element_type=F32)
        ).astype(BF16)
        new_b = (
            b_ref[0].astype(F32)
            - lax.dot_general(low_v, fb_ref[0], NN, preferred_element_type=F32)
        ).astype(BF16)

        @pl.when(core_ref[0] == 0)
        def _():
            out_ref[:, :width] = new_a
            out_ref[:, width:] = new_b

        @pl.when(core_ref[0] != 0)
        def _():
            out_ref[:, :width] = new_b
            out_ref[:, width:] = new_a

    big = pl.BlockSpec((per, rows, width), lambda s, c: (s, 0, 0))
    small = pl.BlockSpec((per, rank, width), lambda s, c: (s, 0, 0))
    return call(
        body,
        "residual",
        4 * rank * rows * width * pairs,
        8 * mine.size,
        grid_spec=pltpu.PrefetchScalarGridSpec(
            num_scalar_prefetch=1,
            grid=(pairs // per,),
            in_specs=[big, big, pl.BlockSpec(low.shape, lambda s, c: (0, 0)), small, small],
            out_specs=pl.BlockSpec((rows, 2 * per * width), lambda s, c: (0, s)),
        ),
        out_shape=jax.ShapeDtypeStruct((rows, 2 * pairs * width), BF16),
    )(core, mine, other, low, f_mine, f_other)


def swap(x):
    return lax.ppermute(x, "core", [(0, 1), (1, 0)])


def to_chips(x, chips):
    return lax.all_to_all(jnp.broadcast_to(x[None], (chips,) + x.shape), CHIPS, 0, 0)


def local(grad, error, q_init):
    grad, error, q_init = grad[0, 0], error[0, 0], q_init[0]
    rows, ff = grad.shape
    chips = lax.axis_size(CHIPS)
    replicas = 2 * chips
    devices = lax.axis_size(ALL)
    core = lax.axis_index("core")

    sent, p_sent = combine(grad, error, q_init, 1 - core, "combine_sent")
    came = swap(sent)
    mine, p_mine = combine(grad, error, q_init, core, "combine_mine")

    left = p_sent + p_mine
    left = to_chips(left + swap(left), chips)

    pair, halves = pair_sum(mine, came)
    sums = lax.all_to_all(pair, CHIPS, 0, 0)

    ortho_t = orthonormal_of(left, replicas)
    mean, left = first_right(sums, ortho_t, replicas)
    left = to_chips(left + swap(left), chips)
    ortho_t, low, q, f = second_right(left, mean)

    f_mine = lax.all_to_all(f, CHIPS, 0, 0)
    f_other = swap(f_mine)
    total = lax.all_to_all(squares(sums, low, q, halves, devices), ALL, 0, 0)
    new_error = residual(mine, sent, low, f_mine, f_other, core)
    error_norm = jnp.sqrt(jnp.sum(total) / (rows * ff * devices))
    return (ortho_t.T[None], q[None], new_error[None, None], error_norm)


def solution(mesh):
    x = y = int(round(np.sqrt(mesh.shape["dp"] // 2)))
    fine = Mesh(mesh.devices.reshape(x, y, 2, mesh.shape["expert"]), ALL)
    dp = ("x", "y", "core")
    placed = (P("expert", dp, None, None), P("expert", dp, None, None), P("expert", None, None))
    return jax.shard_map(
        local,
        mesh=fine,
        in_specs=placed,
        out_specs=(
            P("expert", None, None),
            P("expert", None, dp),
            P("expert", dp, None, None),
            P(),
        ),
        check_vma=False,
    )
```

time: 613 us -> 145 us (0.24)
  blocking collectives: 323 us -> 48.3 us
  waiting for transfers between devices: 232 us -> 30.7 us
  Pallas kernels: 0 us -> 35.2 us
  starting transfers between devices: 0.08 us -> 20.7 us
  matrix products: 19.9 us -> 0 us
  other arithmetic: 18.5 us -> 0.89 us
  between operations: 16 us -> 2.59 us
    psum x3 -> x0, blocking collectives: 323 us -> none  [the longest x2 246 us: local(): projected = lax.psum(partial_value, 'dp') / replicas]
    psum x2 -> x0, waiting for transfers between devices: 232 us -> none  [local(): lax.psum(right_part.astype(jnp.bfloat16), 'dp').astype(jnp.float32)]
    all_to_all x0 -> x3, blocking collectives: none -> 48.3 us  [the longest x1 23.8 us: local(): total = lax.all_to_all(squares(sums, low, q, halves, devices), ALL, 0, 0)]
    pallas_call x0 -> x8, Pallas kernels: none -> 35.2 us  [the longest x2 12.5 us: combine(): call(body, name, 2 * rows * rank * ff // 2, 6 * rows * ff // 2, grid_spec...]
    all_to_all x0 -> x2, waiting for transfers between devices: none -> 28.6 us  [the longest x1 22.7 us: local(): sums = lax.all_to_all(pair, CHIPS, 0, 0)]
    dot_general x7 -> x0, matrix products: 19.4 us -> none  [the longest x2 7.68 us: local(): jnp.einsum('erk,erf->ekf', ortho_low, combined, preferred_element_type=jn...]
    another operation x10 -> x0, other arithmetic: 13.4 us -> none  [the longest x6 7.19 us: local(): lower_factor = jnp.linalg.cholesky(gram_of(projected))]
    ppermute x0 -> x4, starting transfers between devices: none -> 11.5 us  [swap(): return lax.ppermute(x, 'core', [(0, 1), (1, 0)])]
  transfers between devices with their start and end apart: 2 -> 6, of which waited for: 2 -> 4; matrix products, arithmetic and copies ran while one was open for 0% -> 1% of each run, Pallas kernels for 0% -> 8%
where the time goes in v1:
time: 145 us; the launch traced here: 144 us
  blocking collectives  48.3 us (33%)
  Pallas kernels  35.2 us (24%)
  waiting for transfers between devices  30.7 us (21%)
  starting transfers between devices  20.7 us (14%)
  local copies, waits for them, and re-layouts  5.6 us (4%)
  between operations  2.59 us (2%)
    all_to_all x1, blocking collectives, local(): total = lax.all_to_all(squares(sums, low, q, halves, devices), ALL, 0, 0)  23.8 us
    all_to_all x1, waiting for transfers between devices, local(): sums = lax.all_to_all(pair, CHIPS, 0, 0)  22.7 us
    all_to_all x1, blocking collectives, to_chips(): lax.all_to_all(jnp.broadcast_to(x[None], (chips,) + x.shape), CHIPS, 0, 0)  13.7 us
    pallas_call x2, Pallas kernels, combine(): call(body, name, 2 * rows * rank * ff // 2, 6 * rows * ff // 2, grid_spec...  12.5 us
    ppermute x4, starting transfers between devices, swap(): return lax.ppermute(x, 'core', [(0, 1), (1, 0)])  11.5 us
    pallas_call x1, Pallas kernels, residual(): call(body, 'residual', 4 * rank * rows * width * pairs, 8 * mine.size, gr...  11.2 us
    all_to_all x1, blocking collectives, local(): f_mine = lax.all_to_all(f, CHIPS, 0, 0)  10.9 us
    all_to_all x1, waiting for transfers between devices, to_chips(): lax.all_to_all(jnp.broadcast_to(x[None], (chips,) + x.shape), CHIPS, 0, 0)  5.97 us
  transfers between devices with their start and end apart: 6, of which 4 were waited for; matrix products, arithmetic and copies ran while one was open for 1% of the time, Pallas kernels for 8%

profile of v1, /device:TPU:1, one launch (start us, length us, event | category | flops | bytes accessed | tf_op | source)
XLA Modules:
  0.0 143.9 jit_solution(10090085665265442732)
XLA Ops:
  0.6 0.0 copy-start
  0.6 1.0 copy-done
  1.7 6.9 %combine_sent.1 = (bf16[16,256,256]{2,1,0:T(8,128)(2,1)}, f32[32,256]{1,0:T(8,128)S(1)}) custom-call(s32[1]{0:T(128)} %bitcast.4.par_ref, bf16[256,8192]{1,0:T(8,128)(2,1)} %bitcast.19, bf16[256,8192]{1,0:T(8,128)(2,1)} %bitcast.20, bf16[256,8192]{1,0:T(8,128)(2,1)} %bitcast.23, bf16[256,8192]{1,0:T(8,128)(2,1)} %bitcast.24, bf16[32,8192]{1,0:T(8,128)(2,1)S(1)} %bitcast.13, ...), custom_call_target="tpu_custom_call" | custom-call | flops 67108864 | bytes 6291456 | tf_op jit(solution)/shard_map/combine_sent/pallas_call | solution.py:63
  8.6 3.2 %collective-permute-start = (bf16[16,256,256]{2,1,0:T(8,128)(2,1)}, bf16[16,256,256]{2,1,0:T(8,128)(2,1)}, u32[]{:S(2)}, u32[]{:S(2)}) collective-permute-start(bf16[16,256,256]{2,1,0:T(8,128)(2,1)} %get-tuple-element.17.b_ref), channel_id=1, source_target_pairs={{0,8},{8,0},{1,9},{9,1},{2,10},{10,2},{3,11},{11,3},{4,12},{12,4},... | collective-permute-start | bytes 6291464 | tf_op jit(solution)/shard_map/ppermute | solution.py:319
  11.9 5.6 %combine_mine.1 = (bf16[16,256,256]{2,1,0:T(8,128)(2,1)S(1)}, f32[32,256]{1,0:T(8,128)S(1)}) custom-call(s32[1]{0:T(128)} %bitcast.par_ref.core_ref, bf16[256,8192]{1,0:T(8,128)(2,1)} %bitcast.21, bf16[256,8192]{1,0:T(8,128)(2,1)} %bitcast.22, bf16[256,8192]{1,0:T(8,128)(2,1)} %bitcast.25, bf16[256,8192]{1,0:T(8,128)(2,1)} %bitcast.26, ...), custom_call_target="tpu_custom_call" | custom-call | flops 67108864 | bytes 6291456 | tf_op jit(solution)/shard_map/combine_mine/pallas_call | solution.py:63
  17.5 0.1 collective-permute-start.1
  17.6 1.2 collective-permute-done.1
  18.8 0.9 broadcast_in_dim.10
  19.6 5.0 %all-to-all-start.1 = ((f32[16,32,256]{2,1,0:T(8,128)}), f32[16,32,256]{2,1,0:T(8,128)S(1)}, u32[]{:S(2)}, u32[]{:S(2)}) async-start(f32[16,32,256]{2,1,0:T(8,128)} %broadcast_in_dim.10), calls=%async_computation.1 | async-start | bytes 1048576 | tf_op jit(solution)/shard_map/all_to_all | solution.py:323
  24.6 0.0 collective-permute-done.b_ref
  24.7 2.9 %pair_sum.1 = (bf16[16,256,256]{2,1,0:T(8,128)(2,1)S(1)}, f32[8,128]{1,0:T(8,128)S(1)}) custom-call(bf16[16,256,256]{2,1,0:T(8,128)(2,1)S(1)} %get-tuple-element.16.a_ref, bf16[16,256,256]{2,1,0:T(8,128)(2,1)} %collective-permute-done.b_ref), custom_call_target="tpu_custom_call" | custom-call | flops 6291456 | bytes 6291456 | tf_op jit(solution)/shard_map/pair_sum/pallas_call | solution.py:113
  27.5 0.0 copy-start.4
  27.5 1.3 copy-done.4
  28.9 6.0 %all-to-all-done.1.p_ref = f32[16,32,256]{2,1,0:T(8,128)S(1)} async-done(((f32[16,32,256]{2,1,0:T(8,128)}), f32[16,32,256]{2,1,0:T(8,128)S(1)}, u32[]{:S(2)}, u32[]{:S(2)}) %all-to-all-start.1) | async-done | bytes 524320 | tf_op jit(solution)/shard_map/all_to_all | solution.py:323
  34.8 4.2 %all-to-all-start = ((bf16[16,256,256]{2,1,0:T(8,128)(2,1)}), bf16[16,256,256]{2,1,0:T(8,128)(2,1)S(1)}, u32[]{:S(2)}, u32[]{:S(2)}) async-start(bf16[16,256,256]{2,1,0:T(8,128)(2,1)} %copy-done.4), calls=%async_computation | async-start | bytes 4194304 | tf_op jit(solution)/shard_map/all_to_all | solution.py:342
  39.0 2.9 %orthonormal.1.o_ref = f32[32,256]{1,0:T(8,128)S(1)} custom-call(f32[16,32,256]{2,1,0:T(8,128)S(1)} %all-to-all-done.1.p_ref), custom_call_target="tpu_custom_call" | custom-call | flops 524288 | bytes 524288 | tf_op jit(solution)/shard_map/orthonormal/pallas_call | solution.py:149
  41.9 22.7 %all-to-all-done.s_ref = bf16[16,256,256]{2,1,0:T(8,128)(2,1)S(1)} async-done(((bf16[16,256,256]{2,1,0:T(8,128)(2,1)}), bf16[16,256,256]{2,1,0:T(8,128)(2,1)S(1)}, u32[]{:S(2)}, u32[]{:S(2)}) %all-to-all-start) | async-done | bytes 2097184 | tf_op jit(solution)/shard_map/all_to_all | solution.py:342
  64.6 1.2 first_right.1
  65.8 5.2 %collective-permute-start.2 = (f32[32,256]{1,0:T(8,128)S(1)}, f32[32,256]{1,0:T(8,128)S(1)}, u32[]{:S(2)}, u32[]{:S(2)}) collective-permute-start(f32[32,256]{1,0:T(8,128)S(1)} %get-tuple-element.21), channel_id=1, source_target_pairs={{0,8},{8,0},{1,9},{9,1},{2,10},{10,2},{3,11},{11,3},{4,12},{12,4},... | collective-permute-start | bytes 98312 | tf_op jit(solution)/shard_map/ppermute | solution.py:319
  70.9 0.9 collective-permute-done.2
  71.9 13.7 %all_to_all.29.p_ref = f32[16,32,256]{2,1,0:T(8,128)S(1)} all-to-all(f32[16,32,256]{2,1,0:T(8,128)S(1)} %broadcast_in_dim.22), channel_id=1, replica_groups=mesh['x'=4,'y'=4,'core'=2,'expert'=8] {'x','y'}, dimensions={0} | all-to-all | bytes 1048576 | tf_op jit(solution)/shard_map/all_to_all | solution.py:323
  85.6 3.8 %second_right.1 = (f32[32,256]{1,0:T(8,128)}, bf16[256,32]{1,0:T(8,128)(2,1)S(1)}, f32[32,256]{1,0:T(8,128)}, bf16[16,32,256]{2,1,0:T(8,128)(2,1)S(1)}) custom-call(f32[16,32,256]{2,1,0:T(8,128)S(1)} %all_to_all.29.p_ref, f32[256,256]{1,0:T(8,128)S(1)} %get-tuple-element.22.m_ref), custom_call_target="tpu_custom_call" | custom-call | flops 8388608 | bytes 524288 | tf_op jit(solution)/shard_map/second_right/pallas_call | solution.py:218
  89.3 10.9 %all_to_all.30.fa_ref = bf16[16,32,256]{2,1,0:T(8,128)(2,1)S(1)} all-to-all(bf16[16,32,256]{2,1,0:T(8,128)(2,1)S(1)} %get-tuple-element.26), channel_id=1, replica_groups=mesh['x'=4,'y'=4,'core'=2,'expert'=8] {'x','y'}, dimensions={0} | all-to-all | bytes 524288 | tf_op jit(solution)/shard_map/all_to_all | solution.py:349
  100.2 2.9 %collective-permute-start.3 = (bf16[16,32,256]{2,1,0:T(8,128)(2,1)S(1)}, bf16[16,32,256]{2,1,0:T(8,128)(2,1)S(1)}, u32[]{:S(2)}, u32[]{:S(2)}) collective-permute-start(bf16[16,32,256]{2,1,0:T(8,128)(2,1)S(1)} %all_to_all.30.fa_ref), channel_id=1, source_target_pairs={{0,8},{8,0},{1,9},{9,1},{2,10},{10,2},{3,11},{11,3},{4,12},{12,4},... | collective-permute-start | bytes 786440 | tf_op jit(solution)/shard_map/ppermute | solution.py:319
  103.1 0.8 copy-done.5
  103.9 0.8 squares.1
  104.7 23.8 %all_to_all.31 = f32[256,1,128]{2,1,0:T(1,128)S(1)} all-to-all(f32[256,1,128]{2,1,0:T(1,128)S(1)} %bitcast.17), channel_id=1, replica_groups=mesh['x'=4,'y'=4,'core'=2,'expert'=8] {'x','y','core','expert'}, dimensions={0} | all-to-all | bytes 262144 | tf_op jit(solution)/shard_map/all_to_all | solution.py:351
  128.4 0.9 reduce_sum.9
  130.0 0.0 collective-permute-done.3.fb_ref
  130.0 0.0 copy-start.3
  130.0 1.6 %copy-done.3 = bf16[16,256,256]{2,1,0:T(8,128)(2,1)S(1)} copy-done((bf16[16,256,256]{2,1,0:T(8,128)(2,1)S(1)}, bf16[16,256,256]{2,1,0:T(8,128)(2,1)}, u32[]{:S(2)}) %copy-start.3) | copy-done | bytes 2097176
  131.6 11.2 %residual.1 = bf16[256,8192]{1,0:T(8,128)(2,1)} custom-call(s32[1]{0:T(128)} %bitcast.par_ref.core_ref, bf16[16,256,256]{2,1,0:T(8,128)(2,1)S(1)} %copy-done.3, bf16[16,256,256]{2,1,0:T(8,128)(2,1)} %get-tuple-element.17.b_ref, bf16[256,32]{1,0:T(8,128)(2,1)S(1)} %get-tuple-element.25.low_ref, bf16[16,32,256]{2,1,0:T(8,128)(2,1)S(1)} %all_to_all.30.fa_ref, ...), custom_call_target="tpu_custom_call" | custom-call | flops 134217728 | bytes 8388608 | tf_op jit(solution)/shard_map/residual/pallas_call | solution.py:303
  (9 shorter events, 0.1 us)
Async XLA Ops:
  0.6 1.0 copy-start
  1.7 10.2 %copy-start.1 = (bf16[1,32,8192]{2,1,0:T(8,128)(2,1)S(1)}, bf16[1,32,8192]{2,1,0:T(8,128)(2,1)}, u32[]{:S(2)}) copy-start(bf16[1,32,8192]{2,1,0:T(8,128)(2,1)} %param.5) | copy-start | bytes 1572868
  8.6 16.0 %collective-permute-start = (bf16[16,256,256]{2,1,0:T(8,128)(2,1)}, bf16[16,256,256]{2,1,0:T(8,128)(2,1)}, u32[]{:S(2)}, u32[]{:S(2)}) collective-permute-start(bf16[16,256,256]{2,1,0:T(8,128)(2,1)} %get-tuple-element.17.b_ref), channel_id=1, source_target_pairs={{0,8},{8,0},{1,9},{9,1},{2,10},{10,2},{3,11},{11,3},{4,12},{12,4},... | collective-permute-start | bytes 6291464 | tf_op jit(solution)/shard_map/ppermute | solution.py:319
  17.4 10.1 %copy-start.2 = (bf16[16,256,256]{2,1,0:T(8,128)(2,1)}, bf16[16,256,256]{2,1,0:T(8,128)(2,1)S(1)}, u32[]{:S(2)}) copy-start(bf16[16,256,256]{2,1,0:T(8,128)(2,1)S(1)} %get-tuple-element.16.a_ref) | copy-start | bytes 6291460
  17.5 1.3 collective-permute-start.1
  19.6 15.2 %all-to-all-start.1 = ((f32[16,32,256]{2,1,0:T(8,128)}), f32[16,32,256]{2,1,0:T(8,128)S(1)}, u32[]{:S(2)}, u32[]{:S(2)}) async-start(f32[16,32,256]{2,1,0:T(8,128)} %broadcast_in_dim.10), calls=%async_computation.1 | async-start | bytes 1048576 | tf_op jit(solution)/shard_map/all_to_all | solution.py:323
  27.5 1.3 copy-start.4
  34.8 29.8 %all-to-all-start = ((bf16[16,256,256]{2,1,0:T(8,128)(2,1)}), bf16[16,256,256]{2,1,0:T(8,128)(2,1)S(1)}, u32[]{:S(2)}, u32[]{:S(2)}) async-start(bf16[16,256,256]{2,1,0:T(8,128)(2,1)} %copy-done.4), calls=%async_computation | async-start | bytes 4194304 | tf_op jit(solution)/shard_map/all_to_all | solution.py:342
  65.8 6.0 %collective-permute-start.2 = (f32[32,256]{1,0:T(8,128)S(1)}, f32[32,256]{1,0:T(8,128)S(1)}, u32[]{:S(2)}, u32[]{:S(2)}) collective-permute-start(f32[32,256]{1,0:T(8,128)S(1)} %get-tuple-element.21), channel_id=1, source_target_pairs={{0,8},{8,0},{1,9},{9,1},{2,10},{10,2},{3,11},{11,3},{4,12},{12,4},... | collective-permute-start | bytes 98312 | tf_op jit(solution)/shard_map/ppermute | solution.py:319
  100.2 29.8 %collective-permute-start.3 = (bf16[16,32,256]{2,1,0:T(8,128)(2,1)S(1)}, bf16[16,32,256]{2,1,0:T(8,128)(2,1)S(1)}, u32[]{:S(2)}, u32[]{:S(2)}) collective-permute-start(bf16[16,32,256]{2,1,0:T(8,128)(2,1)S(1)} %all_to_all.30.fa_ref), channel_id=1, source_target_pairs={{0,8},{8,0},{1,9},{9,1},{2,10},{10,2},{3,11},{11,3},{4,12},{12,4},... | collective-permute-start | bytes 786440 | tf_op jit(solution)/shard_map/ppermute | solution.py:319
  103.1 0.8 copy-start.5
  130.0 1.6 %copy-start.3 = (bf16[16,256,256]{2,1,0:T(8,128)(2,1)S(1)}, bf16[16,256,256]{2,1,0:T(8,128)(2,1)}, u32[]{:S(2)}) copy-start(bf16[16,256,256]{2,1,0:T(8,128)(2,1)} %copy-done.2) | copy-start | bytes 6291460

commit v2 on v0

v2 whole, which is shorter than its diff:
```python
import jax
import jax.numpy as jnp
import numpy as np
from jax import lax
from jax.experimental import pallas as pl
from jax.experimental.pallas import tpu as pltpu
from jax.sharding import Mesh
from jax.sharding import PartitionSpec as P

F32 = jnp.float32
BF16 = jnp.bfloat16
HIGHEST = lax.Precision.HIGHEST
CHIPS = ("x", "y")
ALL = ("x", "y", "core", "expert")

NN = (((1,), (0,)), ((), ()))
NT = (((1,), (1,)), ((), ()))
TN = (((0,), (0,)), ((), ()))


def call(body, name, flops, moved, vmem=8, **kw):
    return pl.pallas_call(
        body,
        name=name,
        compiler_params=pltpu.CompilerParams(vmem_limit_bytes=vmem * 1024 * 1024),
        cost_estimate=pl.CostEstimate(flops=flops, bytes_accessed=moved, transcendentals=0),
        **kw,
    )


IN_VMEM = pl.BlockSpec(memory_space=pltpu.VMEM)
IN_SMEM = pl.BlockSpec(memory_space=pltpu.SMEM)
IN_HBM = pl.BlockSpec(memory_space=pltpu.HBM)


def combine(grad, error, core, first, rows, vmem):
    ff = grad.shape[1]
    width = 256
    pairs = ff // (2 * width)
    step = 32

    def body(core_ref, g_hbm, e_hbm, c_ref, s_ref, g_ref, e_ref, sems):
        core = core_ref[0]
        cuts = [pl.ds(r, step) for r in range(0, rows, step)]
        copies = []
        for i, cut in enumerate(cuts):
            there = pl.ds(first + i * step, step)
            copies.append(
                (
                    pltpu.make_async_copy(g_hbm.at[there], g_ref.at[cut], sems.at[0, i]),
                    pltpu.make_async_copy(e_hbm.at[there], e_ref.at[cut], sems.at[1, i]),
                )
            )
            for copy in copies[-1]:
                copy.start()
        for copy, cut in zip(copies, cuts):
            finish(copy)
            for i in range(pairs):
                for parity, ref in ((core, c_ref), (1 - core, s_ref)):
                    own = pl.ds(pl.multiple_of((2 * i + parity) * width, width), width)
                    ref[i, cut] = (g_ref[cut, own].astype(F32) + e_ref[cut, own].astype(F32)).astype(BF16)

    blocks = jax.ShapeDtypeStruct((pairs, rows, width), BF16)
    return call(
        body,
        f"combine_{first}",
        rows * ff,
        6 * rows * ff,
        vmem=vmem,
        in_specs=[IN_SMEM, IN_HBM, IN_HBM],
        out_specs=[IN_VMEM] * 2,
        out_shape=[blocks, blocks],
        scratch_shapes=[
            pltpu.VMEM((rows, ff), BF16),
            pltpu.VMEM((rows, ff), BF16),
            pltpu.SemaphoreType.DMA((2, rows // step)),
        ],
    )(core, grad, error)


def project(mine, sent, q_init, core):
    runs = len(mine)
    pairs, rows, width = mine[0].shape
    rank = q_init.shape[0]
    half = rank // 2

    def body(core_ref, q_ref, *refs):
        a_refs, b_refs, (keep_ref, send_ref, p_ref) = refs[:runs], refs[runs : 2 * runs], refs[2 * runs :]
        core = core_ref[0]
        for r in range(runs):
            part = jnp.zeros((rows, rank), F32)
            for i in range(pairs):
                for parity, ref in ((core, a_refs[r]), (1 - core, b_refs[r])):
                    columns = pl.ds(pl.multiple_of((2 * i + parity) * width, width), width)
                    part += lax.dot_general(ref[i], q_ref[:, columns], NT, preferred_element_type=F32)
            p_ref[:, r * rows : (r + 1) * rows] = part.T
        keep_ref[...] = p_ref[pl.ds(pl.multiple_of(core * half, half), half)]
        send_ref[...] = p_ref[pl.ds(pl.multiple_of((1 - core) * half, half), half)]

    return call(
        body,
        "project",
        2 * rank * runs * rows * q_init.shape[1],
        4 * runs * mine[0].size,
        in_specs=[IN_SMEM] + [IN_VMEM] * (1 + 2 * runs),
        out_specs=[IN_VMEM] * 2,
        out_shape=[jax.ShapeDtypeStruct((half, runs * rows), F32)] * 2,
        scratch_shapes=[pltpu.VMEM((rank, runs * rows), F32)],
    )(core, q_init, *mine, *sent)


def finish(copies):
    for copy in copies:
        copy.wait()


def lanes_of(x):
    x = x.reshape(x.shape[0] // 8, 8, x.shape[1])
    x = jnp.sum(x, axis=0)
    return x[:, :128] + x[:, 128:]


def high_low(x):
    high = x.astype(BF16)
    return high, (x - high.astype(F32)).astype(BF16)


def pair_sum(mine, other, place, first, rest):
    pairs, rows, width = mine.shape
    side = int(round(np.sqrt(pairs)))
    full = 2 * rows
    half = 16
    height = side * full + 2 * half

    def body(place_ref, a_ref, b_ref, *refs):
        outs, d_ref = refs[-side - 1 : -1], refs[-1]
        core, own = place_ref[2], jnp.where(place_ref[2] == 0, place_ref[0], place_ref[1])
        total = jnp.zeros((8, 128), F32)
        for k in range(side):
            group = lax.rem(own + k, side)

            def step(j, total, k=k, group=group):
                i = jnp.where(core == 0, side * group + j, side * j + group)
                a, b = a_ref[i].astype(F32), b_ref[i].astype(F32)
                outs[k][pl.ds(pl.multiple_of(j * full + first, rows), rows)] = (a + b).astype(BF16)
                d = a - b
                return total + lanes_of(d * d)

            total = lax.fori_loop(0, side, step, total, unroll=True)
        total = 0.5 * total
        if rest:
            before_ref, p_ref, o_ref = refs[side : side + 3]
            d_ref[...] = total + before_ref[...]
            high, low = high_low(p_ref[...] + o_ref[...])
            for out in outs:
                out[side * full : side * full + half] = high
                out[side * full + half :] = low
        else:
            d_ref[...] = total

    return call(
        body,
        f"pair_sum_{first}",
        6 * mine.size,
        6 * mine.size,
        in_specs=[IN_SMEM] + [IN_VMEM] * (2 + len(rest)),
        out_specs=[IN_VMEM] * (side + 1),
        out_shape=[jax.ShapeDtypeStruct((height, width), BF16)] * side + [jax.ShapeDtypeStruct((8, 128), F32)],
        input_output_aliases={3 + k: k for k in range(side)} if rest else {},
    )(place, mine, other, *rest)


def two_terms(x):
    half = x.shape[0] // 2
    return x[:half].astype(F32) + x[half:].astype(F32)


def merge(parts, place, rows):
    side = len(parts)
    height, width = parts[0].shape
    more = height - side * rows

    def body(place_ref, *refs):
        ins, outs = refs[:side], refs[side:]
        own = jnp.where(place_ref[2] == 0, place_ref[1], place_ref[0])
        left = sum(two_terms(ref[side * rows :]) for ref in ins)
        high, low = high_low(left)
        for k in range(side):
            block = pl.multiple_of(lax.rem(own + k, side) * rows, rows)
            for r in range(0, rows, 64):
                part = pl.ds(block + r, 64)
                outs[k][r : r + 64] = sum(ref[part].astype(F32) for ref in ins).astype(BF16)
            outs[k][rows : rows + more // 2] = high
            outs[k][rows + more // 2 :] = low

    return call(
        body,
        "merge",
        side * height * width,
        4 * side * height * width,
        in_specs=[IN_SMEM] + [IN_VMEM] * side,
        out_specs=[IN_VMEM] * side,
        out_shape=[jax.ShapeDtypeStruct((rows + more, width), BF16)] * side,
    )(place, *parts)


def spread(parts, rows, weight, before):
    side = len(parts)

    def body(*refs):
        ins, before_ref, out_ref = refs[:side], refs[side], refs[side + 1]

        def step(r, total):
            part = pl.ds(pl.multiple_of(r * 64, 64), 64)
            values = [ref[part].astype(F32) for ref in ins]
            mean = sum(values) * (1.0 / side)
            for value in values:
                d = value - mean
                total += lanes_of(d * d)
            return total

        total = lax.fori_loop(0, rows // 64, step, jnp.zeros((8, 128), F32))
        out_ref[...] = before_ref[...] + weight * total

    return call(
        body,
        "spread",
        3 * side * rows * parts[0].shape[1],
        2 * side * rows * parts[0].shape[1],
        in_specs=[IN_VMEM] * (side + 1),
        out_specs=IN_VMEM,
        out_shape=jax.ShapeDtypeStruct((8, 128), F32),
    )(*parts, before)


def left_sum(parts, rows, after):
    side = len(parts)
    height, width = parts[0].shape

    def body(*refs):
        refs[-1][...] = sum(two_terms(ref[rows:]) for ref in refs[:side])

    return call(
        body,
        "left_sum",
        side * (height - rows) * width,
        2 * side * (height - rows) * width,
        in_specs=[IN_VMEM] * (side + 1),
        out_specs=IN_VMEM,
        out_shape=jax.ShapeDtypeStruct(((height - rows) // 2, width), F32),
    )(*parts, after)


def mean_of(parts, rows, replicas):
    side = len(parts)
    width = parts[0].shape[1]

    def body(*refs):
        refs[side][...] = sum(ref[:rows].astype(F32) for ref in refs[:side]) * (1.0 / replicas)

    return call(
        body,
        "mean",
        side * rows * width,
        2 * side * rows * width,
        in_specs=[IN_VMEM] * side,
        out_specs=IN_VMEM,
        out_shape=jax.ShapeDtypeStruct((rows, width), F32),
    )(*parts)


def eliminate(p):
    rank = p.shape[0]
    block = 4
    g = lax.dot_general(p, p, NT, precision=HIGHEST, preferred_element_type=F32)
    row = lax.broadcasted_iota(jnp.int32, (rank, 128), 0)
    pivots = jnp.ones((rank, 128), F32)
    for first in range(0, rank, block):
        columns = [jnp.broadcast_to(g[:, k : k + 1], (rank, 128)) for k in range(first, first + block)]
        for b in range(block):
            k = first + b
            pivot = columns[b][k : k + 1]
            pivots = jnp.where(row == k, pivot, pivots)
            factor = jnp.where(row > k, columns[b] / pivot, 0.0)
            for c in range(b + 1, block):
                columns[c] = columns[c] - factor * columns[c][k : k + 1]
            g = g - factor[:, :rank] * g[k : k + 1]
            p = jnp.concatenate(
                [p[:, l : l + 128] - factor * p[k : k + 1, l : l + 128] for l in range(0, p.shape[1], 128)], axis=1
            )
    scale = 1.0 / jnp.sqrt(pivots)
    return jnp.concatenate([p[:, l : l + 128] * scale for l in range(0, p.shape[1], 128)], axis=1)


def first_right(left, other_left, mean, core, replicas, after):
    half, rows = left.shape

    def body(core_ref, a_ref, b_ref, m_ref, after_ref, out_ref, p_ref):
        core = core_ref[0]
        p_ref[pl.ds(pl.multiple_of(core * half, half), half)] = a_ref[...]
        p_ref[pl.ds(pl.multiple_of((1 - core) * half, half), half)] = b_ref[...]
        ortho_low = eliminate(p_ref[...] * (1.0 / replicas)).astype(BF16).astype(F32)
        mean = m_ref[...]
        q = lax.dot_general(ortho_low, mean, NN, precision=HIGHEST, preferred_element_type=F32)
        low = q.astype(BF16).astype(F32)
        out_ref[...] = lax.dot_general(low, mean, NT, precision=HIGHEST, preferred_element_type=F32)

    return call(
        body,
        "first_right",
        8 * half * mean.size,
        4 * mean.size,
        in_specs=[IN_SMEM] + [IN_VMEM] * 4,
        out_specs=IN_VMEM,
        out_shape=jax.ShapeDtypeStruct((2 * half, rows), F32),
        scratch_shapes=[pltpu.VMEM((2 * half, rows), F32)],
    )(core, left, other_left, mean, after)


def add_copies(a, b, copies):
    def body(a_ref, b_ref, out_ref):
        out_ref[...] = jnp.broadcast_to((a_ref[...] + b_ref[...])[None], out_ref.shape)

    return call(
        body,
        "add_copies",
        a.size,
        4 * a.size * copies,
        in_specs=[IN_VMEM] * 2,
        out_specs=IN_VMEM,
        out_shape=jax.ShapeDtypeStruct((copies,) + a.shape, F32),
    )(a, b)


def second_right(parts, mean, spread_sum, replicas):
    chips, rank, rows = parts.shape
    width = mean.shape[1]
    more = 16

    def body(p_ref, m_ref, s_ref, o_ref, low_ref, q_ref, f_ref):
        total = p_ref[0]
        for i in range(1, chips):
            total += p_ref[i]
        ortho_t = eliminate(total)
        o_ref[...] = ortho_t
        low_t = ortho_t.astype(BF16)
        low = low_t.astype(F32).T.astype(BF16)
        low_ref[...] = low
        mean = m_ref[...]
        q = lax.dot_general(low_t.astype(F32), mean, NN, precision=HIGHEST, preferred_element_type=F32)
        q_ref[...] = q
        f = q.astype(BF16)
        d = mean - lax.dot_general(low, f, NN, preferred_element_type=F32)
        lanes = jnp.sum(s_ref[...] + replicas * lanes_of(d * d), axis=0, keepdims=True)
        high, rest = high_low(lanes)
        rest = lanes - high.astype(F32)
        middle, last = high_low(rest)
        row = lax.broadcasted_iota(jnp.int32, (more, 128), 0)
        terms = jnp.zeros((more, 128), F32)
        for i, term in enumerate((high, middle, last)):
            terms = jnp.where(row == i, term.astype(F32), terms)
        terms = jnp.concatenate([terms, jnp.zeros_like(terms)], axis=1).astype(BF16)
        f_ref[...] = jnp.broadcast_to(jnp.concatenate([f, terms], axis=0)[None], f_ref.shape)

    return call(
        body,
        "second_right",
        4 * rank * rows * width,
        4 * parts.size,
        in_specs=[IN_VMEM] * 3,
        out_specs=[IN_VMEM] * 4,
        out_shape=(
            jax.ShapeDtypeStruct((rank, rows), F32),
            jax.ShapeDtypeStruct((rows, rank), BF16),
            jax.ShapeDtypeStruct((rank, width), F32),
            jax.ShapeDtypeStruct((chips, rank + more, width), BF16),
        ),
    )(parts, mean, spread_sum)


def square_sum(f_mine, f_other, rank, copies):
    def body(a_ref, b_ref, out_ref):
        terms = a_ref[:, rank:].astype(F32) + b_ref[:, rank:].astype(F32)
        lanes = jnp.sum(jnp.sum(terms, axis=0), axis=0, keepdims=True)
        row = lax.broadcasted_iota(jnp.int32, (8, 128), 0)
        out_ref[...] = jnp.broadcast_to(jnp.where(row == 0, lanes[:, :128], 0.0)[None], out_ref.shape)

    return call(
        body,
        "square_sum",
        2 * f_mine.size,
        4 * f_mine.size,
        in_specs=[IN_VMEM] * 2,
        out_specs=IN_VMEM,
        out_shape=jax.ShapeDtypeStruct((copies, 8, 128), F32),
    )(f_mine, f_other)


def residual(mine, sent, low, f_mine, f_other, core):
    runs = len(mine)
    pairs, run, width = mine[0].shape
    rows, rank = low.shape
    ff = 2 * pairs * width

    def body(core_ref, low_ref, fa_ref, fb_ref, *refs):
        a_refs, b_refs, (out_hbm, out_ref, sems) = refs[:runs], refs[runs : 2 * runs], refs[2 * runs :]
        core = core_ref[0]
        low = low_ref[...]
        copies = []
        for i in range(pairs):
            for parity, c_refs, f_ref in ((core, a_refs, fa_ref), (1 - core, b_refs, fb_ref)):
                approx = lax.dot_general(low, f_ref[i, :rank], NN, preferred_element_type=F32)
                own = pl.ds(pl.multiple_of(parity * width, width), width)
                for r in range(runs):
                    cut = slice(r * run, (r + 1) * run)
                    out_ref[i, cut, own] = (c_refs[r][i].astype(F32) - approx[cut]).astype(BF16)
            columns = pl.ds(2 * i * width, 2 * width)
            copies.append(pltpu.make_async_copy(out_ref.at[i], out_hbm.at[:, columns], sems.at[i]))
            copies[-1].start()
        finish(copies)

    return call(
        body,
        "residual",
        2 * rank * rows * ff,
        4 * rows * ff,
        vmem=8,
        in_specs=[IN_SMEM] + [IN_VMEM] * (3 + 2 * runs),
        out_specs=IN_HBM,
        out_shape=jax.ShapeDtypeStruct((rows, ff), BF16),
        scratch_shapes=[pltpu.VMEM((pairs, rows, 2 * width), BF16), pltpu.SemaphoreType.DMA((pairs,))],
    )(core, low, f_mine, f_other, *mine, *sent)


def swap(x):
    return lax.ppermute(x, "core", [(0, 1), (1, 0)])


def shifted(parts, phase):
    side = len(parts)
    out = [parts[0]]
    for k in range(1, side):
        pairs = []
        for x in range(side):
            for y in range(side):
                for core in range(2):
                    to = ((x + k) % side, y) if core == phase else (x, (y + k) % side)
                    pairs.append(((x * side + y) * 2 + core, (to[0] * side + to[1]) * 2 + core))
        out.append(lax.ppermute(parts[k], ("x", "y", "core"), pairs))
    return out


def local(grad, error, q_init):
    grad, error, q_init = grad[0, 0], error[0, 0], q_init[0]
    rows, ff = grad.shape
    rank = q_init.shape[0]
    side, experts = lax.axis_size("x"), lax.axis_size("expert")
    chips = side * side
    replicas = 2 * chips
    place = jnp.stack([lax.axis_index(a) for a in ("x", "y", "core")]).astype(jnp.int32)
    core = jnp.reshape(lax.axis_index("core"), (1,)).astype(jnp.int32)

    run = rows // 2
    mine_a, sent_a = combine(grad, error, core, 0, run, 48)
    came_a = swap(sent_a)
    mine_b, sent_b = combine(grad, error, core, run, run, 46)
    came_b = swap(sent_b)
    left, left_sent = project([mine_a, mine_b], [sent_a, sent_b], q_init, core)
    before = pair_sum(mine_a, came_a, place, 0, ())
    *parts, squares = pair_sum(mine_b, came_b, place, run, (*before, left, swap(left_sent)))

    parts = shifted(parts, 0)
    before = spread(parts, side * rows, 0.5, squares)
    parts = shifted(merge(parts, place, rows), 1)
    squares = spread(parts, rows, 1.0 / (2 * side), before)

    left = left_sum(parts, rows, before)
    other_left = swap(left)
    mean = mean_of(parts, rows, replicas)
    left = first_right(left, other_left, mean, core, replicas, squares)
    parts = lax.all_to_all(add_copies(left, swap(left), chips), CHIPS, 0, 0)
    ortho_t, low, q, f = second_right(parts, mean, squares, replicas)

    f_mine = lax.all_to_all(f, CHIPS, 0, 0)
    f_other = swap(f_mine)
    total = lax.all_to_all(square_sum(f_mine, f_other, rank, experts), "expert", 0, 0)
    new_error = residual([mine_a, mine_b], [sent_a, sent_b], low, f_mine, f_other, core)
    error_norm = jnp.sqrt(jnp.sum(total) / (rows * ff * replicas * experts))
    return (ortho_t.T[None], q[None], new_error[None, None], error_norm)


def solution(mesh):
    x = y = int(round(np.sqrt(mesh.shape["dp"] // 2)))
    fine = Mesh(mesh.devices.reshape(x, y, 2, mesh.shape["expert"]), ALL)
    dp = ("x", "y", "core")
    placed = (P("expert", dp, None, None), P("expert", dp, None, None), P("expert", None, None))
    return jax.shard_map(
        local,
        mesh=fine,
        in_specs=placed,
        out_specs=(
            P("expert", None, None),
            P("expert", None, dp),
            P("expert", dp, None, None),
            P(),
        ),
        check_vma=False,
    )
```

time: 613 us -> 102 us (0.17)
  blocking collectives: 323 us -> 27.6 us
  waiting for transfers between devices: 232 us -> 20.5 us
  starting transfers between devices: 0.08 us -> 24.8 us
  Pallas kernels: 0 us -> 21.3 us
  matrix products: 19.9 us -> 0 us
  other arithmetic: 18.5 us -> 1.45 us
  between operations: 16 us -> 2.6 us
    psum x3 -> x0, blocking collectives: 323 us -> none  [the longest x2 246 us: local(): projected = lax.psum(partial_value, 'dp') / replicas]
    psum x2 -> x0, waiting for transfers between devices: 232 us -> none  [local(): lax.psum(right_part.astype(jnp.bfloat16), 'dp').astype(jnp.float32)]
    all_to_all x0 -> x2, blocking collectives: none -> 27.6 us  [the longest x1 16 us: local(): parts = lax.all_to_all(add_copies(left, swap(left), chips), CHIPS, 0, 0)]
    pallas_call x0 -> x15, Pallas kernels: none -> 21.3 us  [the longest x2 5.23 us: combine(): call(body, f'combine_{first}', rows * ff, 6 * rows * ff, vmem=vmem, in_sp...]
    dot_general x7 -> x0, matrix products: 19.4 us -> none  [the longest x2 7.68 us: local(): jnp.einsum('erk,erf->ekf', ortho_low, combined, preferred_element_type=jn...]
    ppermute x0 -> x12, waiting for transfers between devices: none -> 18.8 us  [the longest x6 16.1 us: shifted(): out.append(lax.ppermute(parts[k], ('x', 'y', 'core'), pairs))]
    ppermute x0 -> x12, starting transfers between devices: none -> 17.3 us  [the longest x6 10.5 us: swap(): return lax.ppermute(x, 'core', [(0, 1), (1, 0)])]
    another operation x10 -> x1, other arithmetic: 13.4 us -> 0.08 us  [local(): jnp.stack([lax.axis_index(a) for a in ('x', 'y', 'core')]).astype(jnp.int32)]
  transfers between devices with their start and end apart: 2 -> 13, of which waited for: 2 -> 8; matrix products, arithmetic and copies ran while one was open for 0% -> 0% of each run, Pallas kernels for 0% -> 12%
where the time goes in v2:
time: 102 us; the launch traced here: 101 us
  blocking collectives  27.6 us (27%)
  starting transfers between devices  24.8 us (24%)
  Pallas kernels  21.3 us (21%)
  waiting for transfers between devices  20.5 us (20%)
  local copies, waits for them, and re-layouts  3.18 us (3%)
  between operations  2.6 us (3%)
  other arithmetic  1.45 us (1%)
    ppermute x6, waiting for transfers between devices, shifted(): out.append(lax.ppermute(parts[k], ('x', 'y', 'core'), pairs))  16.1 us
    all_to_all x1, blocking collectives, local(): parts = lax.all_to_all(add_copies(left, swap(left), chips), CHIPS, 0, 0)  16 us
    all_to_all x1, blocking collectives, local(): f_mine = lax.all_to_all(f, CHIPS, 0, 0)  11.6 us
    ppermute x6, starting transfers between devices, swap(): return lax.ppermute(x, 'core', [(0, 1), (1, 0)])  10.5 us
    all_to_all x1, starting transfers between devices, local(): lax.all_to_all(square_sum(f_mine, f_other, rank, experts), 'expert', 0, 0)  7.55 us
    ppermute x6, starting transfers between devices, shifted(): out.append(lax.ppermute(parts[k], ('x', 'y', 'core'), pairs))  6.79 us
    pallas_call x2, Pallas kernels, combine(): call(body, f'combine_{first}', rows * ff, 6 * rows * ff, vmem=vmem, in_sp...  5.23 us
    pallas_call x1, Pallas kernels, residual(): call(body, 'residual', 2 * rank * rows * ff, 4 * rows * ff, vmem=8, in_sp...  3.56 us
  transfers between devices with their start and end apart: 13, of which 8 were waited for; matrix products, arithmetic and copies ran while one was open for 0% of the time, Pallas kernels for 12%

profile of v2, /device:TPU:1, one launch (start us, length us, event | category | flops | bytes accessed | tf_op | source)
XLA Modules:
  0.0 101.4 jit_solution(6459720752720568070)
XLA Ops:
  0.6 2.5 %combine_0.1 = (bf16[16,128,256]{2,1,0:T(8,128)(2,1)S(1)}, bf16[16,128,256]{2,1,0:T(8,128)(2,1)S(1)}) custom-call(s32[1]{0:T(128)} %bitcast.core_ref, bf16[256,8192]{1,0:T(8,128)(2,1)} %bitcast.11, bf16[256,8192]{1,0:T(8,128)(2,1)} %bitcast.14), custom_call_target="tpu_custom_call" | custom-call | flops 1048576 | bytes 6291456 | tf_op jit(solution)/shard_map/combine_0/pallas_call | solution.py:64
  3.2 3.3 %collective-permute-start.1 = (bf16[16,128,256]{2,1,0:T(8,128)(2,1)S(1)}, bf16[16,128,256]{2,1,0:T(8,128)(2,1)}, u32[]{:S(2)}, u32[]{:S(2)}) collective-permute-start(bf16[16,128,256]{2,1,0:T(8,128)(2,1)S(1)} %get-tuple-element.31.refs_2_), channel_id=1, source_target_pairs={{0,8},{8,0},{1,9},{9,1},{2,10},{10,2},{3,11},{11,3},{4,12},{12,4},... | collective-permute-start | bytes 3145736 | tf_op jit(solution)/shard_map/ppermute | solution.py:436
  6.5 2.7 %combine_128.1 = (bf16[16,128,256]{2,1,0:T(8,128)(2,1)S(1)}, bf16[16,128,256]{2,1,0:T(8,128)(2,1)}) custom-call(s32[1]{0:T(128)} %bitcast.core_ref, bf16[256,8192]{1,0:T(8,128)(2,1)S(1)} %bitcast.12, bf16[256,8192]{1,0:T(8,128)(2,1)} %bitcast.15), custom_call_target="tpu_custom_call" | custom-call | flops 1048576 | bytes 6291456 | tf_op jit(solution)/shard_map/combine_128/pallas_call | solution.py:64
  9.2 0.9 collective-permute-start
  10.1 2.5 %project.1 = (f32[16,256]{1,0:T(8,128)S(1)}, f32[16,256]{1,0:T(8,128)S(1)}) custom-call(s32[1]{0:T(128)} %bitcast.core_ref, bf16[32,8192]{1,0:T(8,128)(2,1)S(1)} %bitcast.13, bf16[16,128,256]{2,1,0:T(8,128)(2,1)S(1)} %get-tuple-element.30.a_ref.refs_0_, bf16[16,128,256]{2,1,0:T(8,128)(2,1)S(1)} %get-tuple-element.28.refs_1_.a_ref, ...), custom_call_target="tpu_custom_call" | custom-call | flops 134217728 | bytes 4194304 | tf_op jit(solution)/shard_map/project/pallas_call | solution.py:100
  12.8 1.7 %pair_sum_0.1 = (bf16[1056,256]{1,0:T(8,128)(2,1)S(1)}, bf16[1056,256]{1,0:T(8,128)(2,1)S(1)}, bf16[1056,256]{1,0:T(8,128)(2,1)S(1)}, bf16[1056,256]{1,0:T(8,128)(2,1)S(1)}, f32[8,128]{1,0:T(8,128)S(1)}) custom-call(s32[3]{0:T(128)S(1)} %pad_add_fusion.place_ref, bf16[16,128,256]{2,1,0:T(8,128)(2,1)S(1)} %get-tuple-element.30.a_ref.refs_0_, ...), custom_call_target="tpu_custom_call" | custom-call | flops 3145728 | bytes 3145728 | tf_op jit(solution)/shard_map/pair_sum_0/pallas_call | solution.py:161
  14.5 1.7 %pair_sum_128.1 = (bf16[1056,256]{1,0:T(8,128)(2,1)S(1)}, bf16[1056,256]{1,0:T(8,128)(2,1)S(1)}, bf16[1056,256]{1,0:T(8,128)(2,1)S(1)}, bf16[1056,256]{1,0:T(8,128)(2,1)S(1)}, f32[8,128]{1,0:T(8,128)S(1)}) custom-call(s32[3]{0:T(128)S(1)} %pad_add_fusion.place_ref, ...), custom_call_target="tpu_custom_call", output_to_operand_aliasing={{0}: (3, {}), {1}: (4, {}), {2}: (5, {}), {3}: (6, {})} | custom-call | flops 3145728 | bytes 3145728 | tf_op jit(solution)/shard_map/pair_sum_128/pallas_call | solution.py:161
  16.3 2.2 %collective-permute-start.4 = (bf16[1056,256]{1,0:T(8,128)(2,1)S(1)}, bf16[1056,256]{1,0:T(8,128)(2,1)S(1)}, u32[]{:S(2)}, u32[]{:S(2)}) collective-permute-start(bf16[1056,256]{1,0:T(8,128)(2,1)S(1)} %get-tuple-element.41), channel_id=1, source_target_pairs={{0,128},{8,40},{16,144},{24,56},{32,160},{40,8},{48,176},{56,24},{... | collective-permute-start | bytes 1622024 | tf_op jit(solution)/shard_map/ppermute | solution.py:449
  18.5 1.1 %collective-permute-start.5 = (bf16[1056,256]{1,0:T(8,128)(2,1)S(1)}, bf16[1056,256]{1,0:T(8,128)(2,1)S(1)}, u32[]{:S(2)}, u32[]{:S(2)}) collective-permute-start(bf16[1056,256]{1,0:T(8,128)(2,1)S(1)} %get-tuple-element.42), channel_id=1, source_target_pairs={{0,192},{8,56},{16,208},{24,8},{32,224},{40,24},{48,240},{56,40},{... | collective-permute-start | bytes 1622024 | tf_op jit(solution)/shard_map/ppermute | solution.py:449
  19.5 12.3 %collective-permute-done.3.refs_1_ = bf16[1056,256]{1,0:T(8,128)(2,1)S(1)} collective-permute-done((bf16[1056,256]{1,0:T(8,128)(2,1)S(1)}, bf16[1056,256]{1,0:T(8,128)(2,1)S(1)}, u32[]{:S(2)}, u32[]{:S(2)}) %collective-permute-start.3) | collective-permute-done | bytes 540704 | tf_op jit(solution)/shard_map/ppermute | solution.py:449
  31.8 0.6 collective-permute-done.5.refs_3_
  32.4 0.8 merge.1
  33.3 2.2 %collective-permute-start.7 = (bf16[288,256]{1,0:T(8,128)(2,1)S(1)}, bf16[288,256]{1,0:T(8,128)(2,1)S(1)}, u32[]{:S(2)}, u32[]{:S(2)}) collective-permute-start(bf16[288,256]{1,0:T(8,128)(2,1)S(1)} %get-tuple-element.45), channel_id=1, source_target_pairs={{0,32},{8,136},{16,48},{24,152},{32,0},{40,168},{48,16},{56,184},{... | collective-permute-start | bytes 442376 | tf_op jit(solution)/shard_map/ppermute | solution.py:449
  35.6 1.2 %collective-permute-start.8 = (bf16[288,256]{1,0:T(8,128)(2,1)S(1)}, bf16[288,256]{1,0:T(8,128)(2,1)S(1)}, u32[]{:S(2)}, u32[]{:S(2)}) collective-permute-start(bf16[288,256]{1,0:T(8,128)(2,1)S(1)} %get-tuple-element.46), channel_id=1, source_target_pairs={{0,48},{8,200},{16,0},{24,216},{32,16},{40,232},{48,32},{56,248},{... | collective-permute-start | bytes 442376 | tf_op jit(solution)/shard_map/ppermute | solution.py:449
  36.7 1.0 %spread.2.refs_4_ = f32[8,128]{1,0:T(8,128)S(1)} custom-call(bf16[1056,256]{1,0:T(8,128)(2,1)S(1)} %get-tuple-element.39.refs_0_, bf16[1056,256]{1,0:T(8,128)(2,1)S(1)} %collective-permute-done.3.refs_1_, bf16[1056,256]{1,0:T(8,128)(2,1)S(1)} %collective-permute-done.4.refs_2_, bf16[1056,256]{1,0:T(8,128)(2,1)S(1)} %collective-permute-done.5.refs_3_, ...), custom_call_target="tpu_custom_call" | custom-call | flops 3145728 | bytes 2097152 | tf_op jit(solution)/shard_map/spread/pallas_call | solution.py:225
  37.7 2.7 %collective-permute-done.6.refs_1_ = bf16[288,256]{1,0:T(8,128)(2,1)S(1)} collective-permute-done((bf16[288,256]{1,0:T(8,128)(2,1)S(1)}, bf16[288,256]{1,0:T(8,128)(2,1)S(1)}, u32[]{:S(2)}, u32[]{:S(2)}) %collective-permute-start.6) | collective-permute-done | bytes 147488 | tf_op jit(solution)/shard_map/ppermute | solution.py:449
  41.0 2.8 %collective-permute-start.9 = (f32[16,256]{1,0:T(8,128)S(1)}, f32[16,256]{1,0:T(8,128)S(1)}, u32[]{:S(2)}, u32[]{:S(2)}) collective-permute-start(f32[16,256]{1,0:T(8,128)S(1)} %left_sum.1.a_ref), channel_id=1, source_target_pairs={{0,8},{8,0},{1,9},{9,1},{2,10},{10,2},{3,11},{11,3},{4,12},{12,4},... | collective-permute-start | bytes 49160 | tf_op jit(solution)/shard_map/ppermute | solution.py:436
  44.7 2.0 %first_right.1.a_ref = f32[32,256]{1,0:T(8,128)S(1)} custom-call(s32[1]{0:T(128)} %bitcast.core_ref, f32[16,256]{1,0:T(8,128)S(1)} %left_sum.1.a_ref, f32[16,256]{1,0:T(8,128)S(1)} %collective-permute-done.9.b_ref, f32[256,256]{1,0:T(8,128)S(1)} %mean.1.m_ref, f32[8,128]{1,0:T(8,128)S(1)} %spread.3.after_ref.s_ref), custom_call_target="tpu_custom_call" | custom-call | flops 8388608 | bytes 262144 | tf_op jit(solution)/shard_map/first_right/pallas_call | solution.py:308
  47.1 0.9 collective-permute-done.10.b_ref
  48.0 16.0 %all_to_all.15.p_ref = f32[16,32,256]{2,1,0:T(8,128)S(1)} all-to-all(f32[16,32,256]{2,1,0:T(8,128)S(1)} %add_copies.1), channel_id=1, replica_groups=mesh['x'=4,'y'=4,'core'=2,'expert'=8] {'x','y'}, dimensions={0} | all-to-all | bytes 1048576 | tf_op jit(solution)/shard_map/all_to_all | solution.py:481
  64.0 2.3 %second_right.1 = (f32[32,256]{1,0:T(8,128)}, bf16[256,32]{1,0:T(8,128)(2,1)S(1)}, f32[32,256]{1,0:T(8,128)}, bf16[16,48,256]{2,1,0:T(8,128)(2,1)S(1)}) custom-call(f32[16,32,256]{2,1,0:T(8,128)S(1)} %all_to_all.15.p_ref, f32[256,256]{1,0:T(8,128)S(1)} %mean.1.m_ref, f32[8,128]{1,0:T(8,128)S(1)} %spread.3.after_ref.s_ref), custom_call_target="tpu_custom_call" | custom-call | flops 8388608 | bytes 524288 | tf_op jit(solution)/shard_map/second_right/pallas_call | solution.py:365
  66.4 11.6 %all_to_all.16.fa_ref.a_ref = bf16[16,48,256]{2,1,0:T(8,128)(2,1)S(1)} all-to-all(bf16[16,48,256]{2,1,0:T(8,128)(2,1)S(1)} %get-tuple-element.51), channel_id=1, replica_groups=mesh['x'=4,'y'=4,'core'=2,'expert'=8] {'x','y'}, dimensions={0} | all-to-all | bytes 786432 | tf_op jit(solution)/shard_map/all_to_all | solution.py:484
  77.9 2.9 %collective-permute-start.11 = (bf16[16,48,256]{2,1,0:T(8,128)(2,1)S(1)}, bf16[16,48,256]{2,1,0:T(8,128)(2,1)S(1)}, u32[]{:S(2)}, u32[]{:S(2)}) collective-permute-start(bf16[16,48,256]{2,1,0:T(8,128)(2,1)S(1)} %all_to_all.16.fa_ref.a_ref), channel_id=1, source_target_pairs={{0,8},{8,0},{1,9},{9,1},{2,10},{10,2},{3,11},{11,3},{4,12},{12,4},... | collective-permute-start | bytes 1179656 | tf_op jit(solution)/shard_map/ppermute | solution.py:436
  80.8 1.3 %collective-permute-done.11.fb_ref.b_ref = bf16[16,48,256]{2,1,0:T(8,128)(2,1)S(1)} collective-permute-done((bf16[16,48,256]{2,1,0:T(8,128)(2,1)S(1)}, bf16[16,48,256]{2,1,0:T(8,128)(2,1)S(1)}, u32[]{:S(2)}, u32[]{:S(2)}) %collective-permute-start.11) | collective-permute-done | bytes 393248 | tf_op jit(solution)/shard_map/ppermute | solution.py:436
  82.2 0.7 copy-done.1
  83.0 0.6 copy-done.4
  83.6 7.6 %all-to-all-start.2 = ((f32[8,8,128]{2,1,0:T(8,128)}), f32[8,8,128]{2,1,0:T(8,128)}, u32[]{:S(2)}, u32[]{:S(2)}) async-start(f32[8,8,128]{2,1,0:T(8,128)} %copy-done.4), calls=%async_computation.2 | async-start | bytes 65536 | tf_op jit(solution)/shard_map/all_to_all | solution.py:486
  91.1 1.0 copy-done.2
  92.1 0.8 copy-done.6
  92.9 3.6 %residual.1 = bf16[256,8192]{1,0:T(8,128)(2,1)} custom-call(s32[1]{0:T(128)} %bitcast.core_ref, bf16[256,32]{1,0:T(8,128)(2,1)S(1)} %copy-done.6, bf16[16,48,256]{2,1,0:T(8,128)(2,1)S(1)} %all_to_all.16.fa_ref.a_ref, bf16[16,48,256]{2,1,0:T(8,128)(2,1)S(1)} %copy-done.2, bf16[16,128,256]{2,1,0:T(8,128)(2,1)S(1)} %get-tuple-element.30.a_ref.refs_0_, ...), custom_call_target="tpu_custom_call" | custom-call | flops 134217728 | bytes 8388608 | tf_op jit(solution)/shard_map/residual/pallas_call | solution.py:422
  96.5 1.6 %all-to-all-done.2 = f32[8,8,128]{2,1,0:T(8,128)} async-done(((f32[8,8,128]{2,1,0:T(8,128)}), f32[8,8,128]{2,1,0:T(8,128)}, u32[]{:S(2)}, u32[]{:S(2)}) %all-to-all-start.2) | async-done | bytes 32800 | tf_op jit(solution)/shard_map/all_to_all | solution.py:486
  98.2 1.4 %reduce_sum.9 = f32[]{:T(128)} reduce(f32[8,8,128]{2,1,0:T(8,128)} %all-to-all-done.2, f32[]{:T(128)} %constant.18.clone.1), dimensions={0,1,2}, to_apply=%region_0.0 | reduce | flops 8191 | bytes 32776 | tf_op jit(solution)/shard_map/reduce_sum | solution.py:488
  (27 shorter events, 2.3 us)
Async XLA Ops:
  0.6 5.9 %copy-start = (bf16[1,1,256,8192]{3,2,1,0:T(8,128)(2,1)S(1)}, bf16[1,1,256,8192]{3,2,1,0:T(8,128)(2,1)}, u32[]{:S(2)}) copy-start(bf16[1,1,256,8192]{3,2,1,0:T(8,128)(2,1)} %param.3) | copy-start | bytes 12582916
  3.2 7.0 %copy-start.3 = (bf16[1,32,8192]{2,1,0:T(8,128)(2,1)S(1)}, bf16[1,32,8192]{2,1,0:T(8,128)(2,1)}, u32[]{:S(2)}) copy-start(bf16[1,32,8192]{2,1,0:T(8,128)(2,1)} %param.5) | copy-start | bytes 1572868
  3.2 9.6 %collective-permute-start.1 = (bf16[16,128,256]{2,1,0:T(8,128)(2,1)S(1)}, bf16[16,128,256]{2,1,0:T(8,128)(2,1)}, u32[]{:S(2)}, u32[]{:S(2)}) collective-permute-start(bf16[16,128,256]{2,1,0:T(8,128)(2,1)S(1)} %get-tuple-element.31.refs_2_), channel_id=1, source_target_pairs={{0,8},{8,0},{1,9},{9,1},{2,10},{10,2},{3,11},{11,3},{4,12},{12,4},... | collective-permute-start | bytes 3145736 | tf_op jit(solution)/shard_map/ppermute | solution.py:436
  9.2 5.3 %collective-permute-start = (bf16[16,128,256]{2,1,0:T(8,128)(2,1)}, bf16[16,128,256]{2,1,0:T(8,128)(2,1)}, u32[]{:S(2)}, u32[]{:S(2)}) collective-permute-start(bf16[16,128,256]{2,1,0:T(8,128)(2,1)} %get-tuple-element.29.refs_3_), channel_id=1, source_target_pairs={{0,8},{8,0},{1,9},{9,1},{2,10},{10,2},{3,11},{11,3},{4,12},{12,4},... | collective-permute-start | bytes 3145736 | tf_op jit(solution)/shard_map/ppermute | solution.py:436
  12.6 1.9 %collective-permute-start.2 = (f32[16,256]{1,0:T(8,128)S(1)}, f32[16,256]{1,0:T(8,128)S(1)}, u32[]{:S(2)}, u32[]{:S(2)}) collective-permute-start(f32[16,256]{1,0:T(8,128)S(1)} %get-tuple-element.38), channel_id=1, source_target_pairs={{0,8},{8,0},{1,9},{9,1},{2,10},{10,2},{3,11},{11,3},{4,12},{12,4},... | collective-permute-start | bytes 49160 | tf_op jit(solution)/shard_map/ppermute | solution.py:436
  16.2 15.6 %collective-permute-start.3 = (bf16[1056,256]{1,0:T(8,128)(2,1)S(1)}, bf16[1056,256]{1,0:T(8,128)(2,1)S(1)}, u32[]{:S(2)}, u32[]{:S(2)}) collective-permute-start(bf16[1056,256]{1,0:T(8,128)(2,1)S(1)} %get-tuple-element.40), channel_id=1, source_target_pairs={{0,64},{8,24},{16,80},{24,40},{32,96},{40,56},{48,112},{56,8},{64,... | collective-permute-start | bytes 1622024 | tf_op jit(solution)/shard_map/ppermute | solution.py:449
  16.3 15.5 %collective-permute-start.4 = (bf16[1056,256]{1,0:T(8,128)(2,1)S(1)}, bf16[1056,256]{1,0:T(8,128)(2,1)S(1)}, u32[]{:S(2)}, u32[]{:S(2)}) collective-permute-start(bf16[1056,256]{1,0:T(8,128)(2,1)S(1)} %get-tuple-element.41), channel_id=1, source_target_pairs={{0,128},{8,40},{16,144},{24,56},{32,160},{40,8},{48,176},{56,24},{... | collective-permute-start | bytes 1622024 | tf_op jit(solution)/shard_map/ppermute | solution.py:449
  18.5 14.0 %collective-permute-start.5 = (bf16[1056,256]{1,0:T(8,128)(2,1)S(1)}, bf16[1056,256]{1,0:T(8,128)(2,1)S(1)}, u32[]{:S(2)}, u32[]{:S(2)}) collective-permute-start(bf16[1056,256]{1,0:T(8,128)(2,1)S(1)} %get-tuple-element.42), channel_id=1, source_target_pairs={{0,192},{8,56},{16,208},{24,8},{32,224},{40,24},{48,240},{56,40},{... | collective-permute-start | bytes 1622024 | tf_op jit(solution)/shard_map/ppermute | solution.py:449
  33.2 7.2 %collective-permute-start.6 = (bf16[288,256]{1,0:T(8,128)(2,1)S(1)}, bf16[288,256]{1,0:T(8,128)(2,1)S(1)}, u32[]{:S(2)}, u32[]{:S(2)}) collective-permute-start(bf16[288,256]{1,0:T(8,128)(2,1)S(1)} %get-tuple-element.44), channel_id=1, source_target_pairs={{0,16},{8,72},{16,32},{24,88},{32,48},{40,104},{48,0},{56,120},{64... | collective-permute-start | bytes 442376 | tf_op jit(solution)/shard_map/ppermute | solution.py:449
  33.3 7.1 %collective-permute-start.7 = (bf16[288,256]{1,0:T(8,128)(2,1)S(1)}, bf16[288,256]{1,0:T(8,128)(2,1)S(1)}, u32[]{:S(2)}, u32[]{:S(2)}) collective-permute-start(bf16[288,256]{1,0:T(8,128)(2,1)S(1)} %get-tuple-element.45), channel_id=1, source_target_pairs={{0,32},{8,136},{16,48},{24,152},{32,0},{40,168},{48,16},{56,184},{... | collective-permute-start | bytes 442376 | tf_op jit(solution)/shard_map/ppermute | solution.py:449
  35.6 5.4 %collective-permute-start.8 = (bf16[288,256]{1,0:T(8,128)(2,1)S(1)}, bf16[288,256]{1,0:T(8,128)(2,1)S(1)}, u32[]{:S(2)}, u32[]{:S(2)}) collective-permute-start(bf16[288,256]{1,0:T(8,128)(2,1)S(1)} %get-tuple-element.46), channel_id=1, source_target_pairs={{0,48},{8,200},{16,0},{24,216},{32,16},{40,232},{48,32},{56,248},{... | collective-permute-start | bytes 442376 | tf_op jit(solution)/shard_map/ppermute | solution.py:449
  41.0 3.7 %collective-permute-start.9 = (f32[16,256]{1,0:T(8,128)S(1)}, f32[16,256]{1,0:T(8,128)S(1)}, u32[]{:S(2)}, u32[]{:S(2)}) collective-permute-start(f32[16,256]{1,0:T(8,128)S(1)} %left_sum.1.a_ref), channel_id=1, source_target_pairs={{0,8},{8,0},{1,9},{9,1},{2,10},{10,2},{3,11},{11,3},{4,12},{12,4},... | collective-permute-start | bytes 49160 | tf_op jit(solution)/shard_map/ppermute | solution.py:436
  46.7 1.3 %collective-permute-start.10 = (f32[32,256]{1,0:T(8,128)S(1)}, f32[32,256]{1,0:T(8,128)S(1)}, u32[]{:S(2)}, u32[]{:S(2)}) collective-permute-start(f32[32,256]{1,0:T(8,128)S(1)} %first_right.1.a_ref), channel_id=1, source_target_pairs={{0,8},{8,0},{1,9},{9,1},{2,10},{10,2},{3,11},{11,3},{4,12},{12,4},... | collective-permute-start | bytes 98312 | tf_op jit(solution)/shard_map/ppermute | solution.py:436
  66.4 15.8 %copy-start.5 = (bf16[256,32]{1,0:T(8,128)(2,1)}, bf16[256,32]{1,0:T(8,128)(2,1)S(1)}, u32[]{:S(2)}) copy-start(bf16[256,32]{1,0:T(8,128)(2,1)S(1)} %get-tuple-element.50.low_ref) | copy-start | bytes 49156
  77.9 4.2 %collective-permute-start.11 = (bf16[16,48,256]{2,1,0:T(8,128)(2,1)S(1)}, bf16[16,48,256]{2,1,0:T(8,128)(2,1)S(1)}, u32[]{:S(2)}, u32[]{:S(2)}) collective-permute-start(bf16[16,48,256]{2,1,0:T(8,128)(2,1)S(1)} %all_to_all.16.fa_ref.a_ref), channel_id=1, source_target_pairs={{0,8},{8,0},{1,9},{9,1},{2,10},{10,2},{3,11},{11,3},{4,12},{12,4},... | collective-permute-start | bytes 1179656 | tf_op jit(solution)/shard_map/ppermute | solution.py:436
  82.2 0.7 copy-start.1
  83.0 0.6 copy-start.4
  83.6 14.6 %all-to-all-start.2 = ((f32[8,8,128]{2,1,0:T(8,128)}), f32[8,8,128]{2,1,0:T(8,128)}, u32[]{:S(2)}, u32[]{:S(2)}) async-start(f32[8,8,128]{2,1,0:T(8,128)} %copy-done.4), calls=%async_computation.2 | async-start | bytes 65536 | tf_op jit(solution)/shard_map/all_to_all | solution.py:486
  91.1 1.0 copy-start.2
  92.1 0.8 copy-start.6

commit v3 on v2

--- a/solution.py
+++ b/solution.py
@@ -18,7 +18,7 @@
 TN = (((0,), (0,)), ((), ()))
 
 
-def call(body, name, flops, moved, vmem=8, **kw):
+def call(body, name, flops, moved, vmem=4, **kw):
     return pl.pallas_call(
         body,
         name=name,
@@ -33,13 +33,14 @@
 IN_HBM = pl.BlockSpec(memory_space=pltpu.HBM)
 
 
-def combine(grad, error, core, first, rows, vmem):
+def combine(grad, error, core, first, rows, vmem, after=()):
     ff = grad.shape[1]
     width = 256
     pairs = ff // (2 * width)
     step = 32
 
-    def body(core_ref, g_hbm, e_hbm, c_ref, s_ref, g_ref, e_ref, sems):
+    def body(core_ref, g_hbm, e_hbm, *refs):
+        c_ref, s_ref, g_ref, e_ref, sems = refs[len(after) :]
         core = core_ref[0]
         cuts = [pl.ds(r, step) for r in range(0, rows, step)]
         copies = []
@@ -67,7 +68,7 @@
         rows * ff,
         6 * rows * ff,
         vmem=vmem,
-        in_specs=[IN_SMEM, IN_HBM, IN_HBM],
+        in_specs=[IN_SMEM, IN_HBM, IN_HBM] + [IN_VMEM] * len(after),
         out_specs=[IN_VMEM] * 2,
         out_shape=[blocks, blocks],
         scratch_shapes=[
@@ -75,7 +76,7 @@
             pltpu.VMEM((rows, ff), BF16),
             pltpu.SemaphoreType.DMA((2, rows // step)),
         ],
-    )(core, grad, error)
+    )(core, grad, error, *after)
 
 
 def project(mine, sent, q_init, core):
@@ -85,15 +86,20 @@
     half = rank // 2
 
     def body(core_ref, q_ref, *refs):
-        a_refs, b_refs, (keep_ref, send_ref, p_ref) = refs[:runs], refs[runs : 2 * runs], refs[2 * runs :]
+        a_refs, b_refs = refs[:runs], refs[runs : 2 * runs]
+        keep_ref, send_ref, p_ref, s_ref, sem = refs[2 * runs :]
         core = core_ref[0]
-        for r in range(runs):
-            part = jnp.zeros((rows, rank), F32)
+        copy = pltpu.make_async_copy(b_refs[-1], s_ref, sem)
+        copy.start()
+        parts = [jnp.zeros((rows, rank), F32)] * runs
+        for parity, c_refs in ((core, a_refs), (1 - core, [*b_refs[:-1], s_ref])):
+            if c_refs[-1] is s_ref:
+                copy.wait()
             for i in range(pairs):
-                for parity, ref in ((core, a_refs[r]), (1 - core, b_refs[r])):
-                    columns = pl.ds(pl.multiple_of((2 * i + parity) * width, width), width)
-                    part += lax.dot_general(ref[i], q_ref[:, columns], NT, preferred_element_type=F32)
-            p_ref[:, r * rows : (r + 1) * rows] = part.T
+                columns = pl.ds(pl.multiple_of((2 * i + parity) * width, width), width)
+                for r in range(runs):
+                    parts[r] += lax.dot_general(c_refs[r][i], q_ref[:, columns], NT, preferred_element_type=F32)
+        p_ref[...] = jnp.concatenate([part.T for part in parts], axis=1)
         keep_ref[...] = p_ref[pl.ds(pl.multiple_of(core * half, half), half)]
         send_ref[...] = p_ref[pl.ds(pl.multiple_of((1 - core) * half, half), half)]
 
@@ -102,10 +108,14 @@
         "project",
         2 * rank * runs * rows * q_init.shape[1],
         4 * runs * mine[0].size,
-        in_specs=[IN_SMEM] + [IN_VMEM] * (1 + 2 * runs),
+        in_specs=[IN_SMEM] + [IN_VMEM] * (2 * runs) + [IN_HBM],
         out_specs=[IN_VMEM] * 2,
         out_shape=[jax.ShapeDtypeStruct((half, runs * rows), F32)] * 2,
-        scratch_shapes=[pltpu.VMEM((rank, runs * rows), F32)],
+        scratch_shapes=[
+            pltpu.VMEM((rank, runs * rows), F32),
+            pltpu.VMEM((pairs, rows, width), BF16),
+            pltpu.SemaphoreType.DMA,
+        ],
     )(core, q_init, *mine, *sent)
 
 
@@ -125,49 +135,78 @@
     return high, (x - high.astype(F32)).astype(BF16)
 
 
-def pair_sum(mine, other, place, first, rest):
-    pairs, rows, width = mine.shape
+def pair_sum(mine, other, place, left):
+    runs = len(mine)
+    pairs, rows, width = mine[0].shape
     side = int(round(np.sqrt(pairs)))
-    full = 2 * rows
-    half = 16
+    half = left[0].shape[0]
+    full = runs * rows
     height = side * full + 2 * half
 
-    def body(place_ref, a_ref, b_ref, *refs):
-        outs, d_ref = refs[-side - 1 : -1], refs[-1]
+    def body(place_ref, *refs):
+        a_refs, b_refs, p_refs = refs[:runs], refs[runs : 2 * runs], refs[2 * runs : 2 * runs + 2]
+        outs, t_ref, sems = refs[2 * runs + 2 : -2], refs[-2], refs[-1]
         core, own = place_ref[2], jnp.where(place_ref[2] == 0, place_ref[0], place_ref[1])
+        copies = [pltpu.make_async_copy(b_refs[r], t_ref.at[r], sems.at[r]) for r in range(runs)]
+        for copy in copies:
+            copy.start()
+        high, low = high_low(p_refs[0][...] + p_refs[1][...])
+        for out in outs:
+            out[side * full : side * full + half] = high
+            out[side * full + half :] = low
+        for r in range(runs):
+            copies[r].wait()
+            for k in range(side):
+                group = lax.rem(own + k, side)
+                for j in range(side):
+                    i = jnp.where(core == 0, side * group + j, side * j + group)
+                    there = j * full + r * rows
+                    outs[k][there : there + rows] = a_refs[r][i] + t_ref[r, i]
+
+    return call(
+        body,
+        "pair_sum",
+        6 * runs * mine[0].size,
+        6 * runs * mine[0].size,
+        vmem=6,
+        in_specs=[IN_SMEM] + [IN_VMEM] * runs + [IN_HBM] * runs + [IN_VMEM] * 2,
+        out_specs=[IN_VMEM] * side,
+        out_shape=[jax.ShapeDtypeStruct((height, width), BF16)] * side,
+        scratch_shapes=[pltpu.VMEM((runs, pairs, rows, width), BF16), pltpu.SemaphoreType.DMA((runs,))],
+    )(place, *mine, *other, *left)
+
+
+def pair_spread(mine, other):
+    runs = len(mine)
+    pairs, rows, width = mine[0].shape
+
+    def body(*refs):
+        a_refs, b_refs, out_ref, t_ref, sems = refs[:runs], refs[runs : 2 * runs], refs[-3], refs[-2], refs[-1]
+        copies = [pltpu.make_async_copy(b_refs[r], t_ref.at[r], sems.at[r]) for r in range(runs)]
+        for copy in copies:
+            copy.start()
         total = jnp.zeros((8, 128), F32)
-        for k in range(side):
-            group = lax.rem(own + k, side)
-
-            def step(j, total, k=k, group=group):
-                i = jnp.where(core == 0, side * group + j, side * j + group)
-                a, b = a_ref[i].astype(F32), b_ref[i].astype(F32)
-                outs[k][pl.ds(pl.multiple_of(j * full + first, rows), rows)] = (a + b).astype(BF16)
-                d = a - b
+        for r in range(runs):
+            copies[r].wait()
+
+            def step(i, total, r=r):
+                d = a_refs[r][i].astype(F32) - t_ref[r, i].astype(F32)
                 return total + lanes_of(d * d)
 
-            total = lax.fori_loop(0, side, step, total, unroll=True)
-        total = 0.5 * total
-        if rest:
-            before_ref, p_ref, o_ref = refs[side : side + 3]
-            d_ref[...] = total + before_ref[...]
-            high, low = high_low(p_ref[...] + o_ref[...])
-            for out in outs:
-                out[side * full : side * full + half] = high
-                out[side * full + half :] = low
-        else:
-            d_ref[...] = total
-
-    return call(
-        body,
-        f"pair_sum_{first}",
-        6 * mine.size,
-        6 * mine.size,
-        in_specs=[IN_SMEM] + [IN_VMEM] * (2 + len(rest)),
-        out_specs=[IN_VMEM] * (side + 1),
-        out_shape=[jax.ShapeDtypeStruct((height, width), BF16)] * side + [jax.ShapeDtypeStruct((8, 128), F32)],
-        input_output_aliases={3 + k: k for k in range(side)} if rest else {},
-    )(place, mine, other, *rest)
+            total = lax.fori_loop(0, pairs, step, total)
+        out_ref[...] = 0.5 * total
+
+    return call(
+        body,
+        "pair_spread",
+        3 * runs * mine[0].size,
+        4 * runs * mine[0].size,
+        vmem=6,
+        in_specs=[IN_VMEM] * runs + [IN_HBM] * runs,
+        out_specs=IN_VMEM,
+        out_shape=jax.ShapeDtypeStruct((8, 128), F32),
+        scratch_shapes=[pltpu.VMEM((runs, pairs, rows, width), BF16), pltpu.SemaphoreType.DMA((runs,))],
+    )(*mine, *other)
 
 
 def two_terms(x):
@@ -175,40 +214,41 @@
     return x[:half].astype(F32) + x[half:].astype(F32)
 
 
-def merge(parts, place, rows):
+def merge(parts, place, rows, after):
     side = len(parts)
     height, width = parts[0].shape
     more = height - side * rows
 
     def body(place_ref, *refs):
-        ins, outs = refs[:side], refs[side:]
+        ins, outs = refs[:side], refs[side + 1 :]
         own = jnp.where(place_ref[2] == 0, place_ref[1], place_ref[0])
-        left = sum(two_terms(ref[side * rows :]) for ref in ins)
-        high, low = high_low(left)
+        if more:
+            high, low = high_low(sum(two_terms(ref[side * rows :]) for ref in ins))
         for k in range(side):
             block = pl.multiple_of(lax.rem(own + k, side) * rows, rows)
             for r in range(0, rows, 64):
                 part = pl.ds(block + r, 64)
                 outs[k][r : r + 64] = sum(ref[part].astype(F32) for ref in ins).astype(BF16)
-            outs[k][rows : rows + more // 2] = high
-            outs[k][rows + more // 2 :] = low
-
-    return call(
-        body,
-        "merge",
+            if more:
+                outs[k][rows : rows + more // 2] = high
+                outs[k][rows + more // 2 :] = low
+
+    return call(
+        body,
+        "merge_left" if more else "merge",
         side * height * width,
         4 * side * height * width,
-        in_specs=[IN_SMEM] + [IN_VMEM] * side,
+        in_specs=[IN_SMEM] + [IN_VMEM] * (side + 1),
         out_specs=[IN_VMEM] * side,
         out_shape=[jax.ShapeDtypeStruct((rows + more, width), BF16)] * side,
-    )(place, *parts)
+    )(place, *parts, after)
 
 
 def spread(parts, rows, weight, before):
-    side = len(parts)
+    side, more = len(parts), len(before)
 
     def body(*refs):
-        ins, before_ref, out_ref = refs[:side], refs[side], refs[side + 1]
+        ins, befores, out_ref = refs[:side], refs[side : side + more], refs[-1]
 
         def step(r, total):
             part = pl.ds(pl.multiple_of(r * 64, 64), 64)
@@ -220,17 +260,17 @@
             return total
 
         total = lax.fori_loop(0, rows // 64, step, jnp.zeros((8, 128), F32))
-        out_ref[...] = before_ref[...] + weight * total
+        out_ref[...] = sum(ref[...] for ref in befores) + weight * total
 
     return call(
         body,
         "spread",
         3 * side * rows * parts[0].shape[1],
         2 * side * rows * parts[0].shape[1],
-        in_specs=[IN_VMEM] * (side + 1),
+        in_specs=[IN_VMEM] * (side + more),
         out_specs=IN_VMEM,
         out_shape=jax.ShapeDtypeStruct((8, 128), F32),
-    )(*parts, before)
+    )(*parts, *before)
 
 
 def left_sum(parts, rows, after):
@@ -251,27 +291,28 @@
     )(*parts, after)
 
 
-def mean_of(parts, rows, replicas):
-    side = len(parts)
-    width = parts[0].shape[1]
+def mean_of(runs, rows, replicas):
+    side, width = len(runs[0]), runs[0][0].shape[1]
 
     def body(*refs):
-        refs[side][...] = sum(ref[:rows].astype(F32) for ref in refs[:side]) * (1.0 / replicas)
+        for r in range(len(runs)):
+            ins = refs[r * side : (r + 1) * side]
+            refs[-1][r * rows : (r + 1) * rows] = sum(ref[:rows].astype(F32) for ref in ins) * (1.0 / replicas)
 
     return call(
         body,
         "mean",
-        side * rows * width,
-        2 * side * rows * width,
-        in_specs=[IN_VMEM] * side,
-        out_specs=IN_VMEM,
-        out_shape=jax.ShapeDtypeStruct((rows, width), F32),
-    )(*parts)
+        len(runs) * side * rows * width,
+        2 * len(runs) * side * rows * width,
+        in_specs=[IN_VMEM] * (len(runs) * side),
+        out_specs=IN_VMEM,
+        out_shape=jax.ShapeDtypeStruct((len(runs) * rows, width), F32),
+    )(*(part for parts in runs for part in parts))
 
 
 def eliminate(p):
     rank = p.shape[0]
-    block = 4
+    block = 8
     g = lax.dot_general(p, p, NT, precision=HIGHEST, preferred_element_type=F32)
     row = lax.broadcasted_iota(jnp.int32, (rank, 128), 0)
     pivots = jnp.ones((rank, 128), F32)
@@ -345,7 +386,7 @@
         o_ref[...] = ortho_t
         low_t = ortho_t.astype(BF16)
         low = low_t.astype(F32).T.astype(BF16)
-        low_ref[...] = low
+        low_ref[...] = low_t
         mean = m_ref[...]
         q = lax.dot_general(low_t.astype(F32), mean, NN, precision=HIGHEST, preferred_element_type=F32)
         q_ref[...] = q
@@ -371,7 +412,7 @@
         out_specs=[IN_VMEM] * 4,
         out_shape=(
             jax.ShapeDtypeStruct((rank, rows), F32),
-            jax.ShapeDtypeStruct((rows, rank), BF16),
+            jax.ShapeDtypeStruct((rank, rows), BF16),
             jax.ShapeDtypeStruct((rank, width), F32),
             jax.ShapeDtypeStruct((chips, rank + more, width), BF16),
         ),
@@ -379,44 +420,80 @@
 
 
 def square_sum(f_mine, f_other, rank, copies):
-    def body(a_ref, b_ref, out_ref):
-        terms = a_ref[:, rank:].astype(F32) + b_ref[:, rank:].astype(F32)
+    chips, height, width = f_mine.shape
+    more = height - rank
+
+    def body(a_ref, b_hbm, out_hbm, b_ref, out_ref, sems):
+        copy = pltpu.make_async_copy(b_hbm.at[:, pl.ds(rank, more)], b_ref, sems.at[0])
+        copy.start()
+        copy.wait()
+        terms = a_ref[:, rank:].astype(F32) + b_ref[...].astype(F32)
         lanes = jnp.sum(jnp.sum(terms, axis=0), axis=0, keepdims=True)
         row = lax.broadcasted_iota(jnp.int32, (8, 128), 0)
         out_ref[...] = jnp.broadcast_to(jnp.where(row == 0, lanes[:, :128], 0.0)[None], out_ref.shape)
+        copy = pltpu.make_async_copy(out_ref, out_hbm, sems.at[1])
+        copy.start()
+        copy.wait()
 
     return call(
         body,
         "square_sum",
         2 * f_mine.size,
         4 * f_mine.size,
-        in_specs=[IN_VMEM] * 2,
-        out_specs=IN_VMEM,
+        in_specs=[IN_VMEM, IN_HBM],
+        out_specs=IN_HBM,
         out_shape=jax.ShapeDtypeStruct((copies, 8, 128), F32),
+        scratch_shapes=[
+            pltpu.VMEM((chips, more, width), BF16),
+            pltpu.VMEM((copies, 8, 128), F32),
+            pltpu.SemaphoreType.DMA((2,)),
+        ],
     )(f_mine, f_other)
 
 
-def residual(mine, sent, low, f_mine, f_other, core):
+def root_mean(total, count):
+    def body(t_ref, out_ref):
+        out_ref[...] = jnp.sqrt(jnp.sum(t_ref[...], keepdims=True)[0] * (1.0 / count))
+
+    return call(
+        body,
+        "root_mean",
+        total.size,
+        4 * total.size,
+        in_specs=[IN_VMEM],
+        out_specs=IN_VMEM,
+        out_shape=jax.ShapeDtypeStruct((1, 1), F32),
+    )(total)[0, 0]
+
+
+def residual(mine, sent, low_t, f_mine, f_other, core):
     runs = len(mine)
     pairs, run, width = mine[0].shape
-    rows, rank = low.shape
+    rank, rows = low_t.shape
     ff = 2 * pairs * width
 
     def body(core_ref, low_ref, fa_ref, fb_ref, *refs):
-        a_refs, b_refs, (out_hbm, out_ref, sems) = refs[:runs], refs[runs : 2 * runs], refs[2 * runs :]
+        a_refs, b_refs = refs[:runs], list(refs[runs : 2 * runs])
+        out_hbm, out_ref, s_ref, sems, s_sem = refs[2 * runs :]
         core = core_ref[0]
-        low = low_ref[...]
+        arrive = pltpu.make_async_copy(b_refs[-1], s_ref, s_sem)
+        arrive.start()
+        b_refs[-1] = s_ref
+        low = low_ref[...].astype(F32).T.astype(BF16)
+        arrive.wait()
         copies = []
-        for i in range(pairs):
-            for parity, c_refs, f_ref in ((core, a_refs, fa_ref), (1 - core, b_refs, fb_ref)):
-                approx = lax.dot_general(low, f_ref[i, :rank], NN, preferred_element_type=F32)
-                own = pl.ds(pl.multiple_of(parity * width, width), width)
-                for r in range(runs):
-                    cut = slice(r * run, (r + 1) * run)
-                    out_ref[i, cut, own] = (c_refs[r][i].astype(F32) - approx[cut]).astype(BF16)
-            columns = pl.ds(2 * i * width, 2 * width)
-            copies.append(pltpu.make_async_copy(out_ref.at[i], out_hbm.at[:, columns], sems.at[i]))
-            copies[-1].start()
+        for first in range(0, pairs, 4):
+            for i in range(first, first + 4):
+                for parity, c_refs, f_ref in ((core, a_refs, fa_ref), (1 - core, b_refs, fb_ref)):
+                    approx = lax.dot_general(low, f_ref[i, :rank], NN, preferred_element_type=F32)
+                    own = pl.ds(pl.multiple_of(parity * width, width), width)
+                    for r in range(runs):
+                        cut = slice(r * run, (r + 1) * run)
+                        out_ref[i, cut, own] = (c_refs[r][i].astype(F32) - approx[cut]).astype(BF16)
+            for i in range(first, first + 4):
+                columns = pl.ds(2 * i * width, 2 * width)
+                copies.append(pltpu.make_async_copy(out_ref.at[i], out_hbm.at[:, columns], sems.at[i]))
+                copies[-1].start()
         finish(copies)
 
     return call(
@@ -425,11 +502,16 @@
         2 * rank * rows * ff,
         4 * rows * ff,
         vmem=8,
-        in_specs=[IN_SMEM] + [IN_VMEM] * (3 + 2 * runs),
+        in_specs=[IN_SMEM] + [IN_VMEM] * (2 + 2 * runs) + [IN_HBM],
         out_specs=IN_HBM,
         out_shape=jax.ShapeDtypeStruct((rows, ff), BF16),
-        scratch_shapes=[pltpu.VMEM((pairs, rows, 2 * width), BF16), pltpu.SemaphoreType.DMA((pairs,))],
-    )(core, low, f_mine, f_other, *mine, *sent)
+        scratch_shapes=[
+            pltpu.VMEM((pairs, rows, 2 * width), BF16),
+            pltpu.VMEM((pairs, run, width), BF16),
+            pltpu.SemaphoreType.DMA((pairs,)),
+            pltpu.SemaphoreType.DMA,
+        ],
+    )(core, low_t, f_mine, f_other, *mine, *sent)
 
 
 def swap(x):
@@ -463,20 +545,20 @@
     run = rows // 2
     mine_a, sent_a = combine(grad, error, core, 0, run, 48)
     came_a = swap(sent_a)
-    mine_b, sent_b = combine(grad, error, core, run, run, 46)
+    mine_b, sent_b = combine(grad, error, core, run, run, 46, (mine_a,))
     came_b = swap(sent_b)
     left, left_sent = project([mine_a, mine_b], [sent_a, sent_b], q_init, core)
-    before = pair_sum(mine_a, came_a, place, 0, ())
-    *parts, squares = pair_sum(mine_b, came_b, place, run, (*before, left, swap(left_sent)))
+    parts = pair_sum([mine_a, mine_b], [came_a, came_b], place, (left, swap(left_sent)))
 
     parts = shifted(parts, 0)
-    before = spread(parts, side * rows, 0.5, squares)
-    parts = shifted(merge(parts, place, rows), 1)
-    squares = spread(parts, rows, 1.0 / (2 * side), before)
+    squares = pair_spread([mine_a, mine_b], [came_a, came_b])
+    before = spread(parts, side * rows, 0.5, [squares])
+    parts = shifted(merge(parts, place, rows, squares), 1)
+    squares = spread(parts, rows, 1.0 / (2 * side), [before])
 
     left = left_sum(parts, rows, before)
     other_left = swap(left)
-    mean = mean_of(parts, rows, replicas)
+    mean = mean_of([parts], rows, replicas)
     left = first_right(left, other_left, mean, core, replicas, squares)
     parts = lax.all_to_all(add_copies(left, swap(left), chips), CHIPS, 0, 0)
     ortho_t, low, q, f = second_right(parts, mean, squares, replicas)
@@ -485,7 +567,7 @@
     f_other = swap(f_mine)
     total = lax.all_to_all(square_sum(f_mine, f_other, rank, experts), "expert", 0, 0)
     new_error = residual([mine_a, mine_b], [sent_a, sent_b], low, f_mine, f_other, core)
-    error_norm = jnp.sqrt(jnp.sum(total) / (rows * ff * replicas * experts))
+    error_norm = root_mean(total, rows * ff * replicas * experts)
     return (ortho_t.T[None], q[None], new_error[None, None], error_norm)
 
 

time: 102 us -> 98.5 us (0.966)
  between operations: 2.6 us -> 0.77 us
  other arithmetic: 1.45 us -> 0.08 us
  Pallas kernels: 21.3 us -> 22.6 us
    pallas_call x4 -> x5, Pallas kernels: 4.26 us -> 6.6 us  [the longest x1 2.21 us: pair_sum(): call(body, 'pair_sum', 6 * runs * mine[0].size, 6 * runs * mine[0].size,...]
    ppermute x6, waiting for transfers between devices: 16.1 us -> 14 us  [shifted(): out.append(lax.ppermute(parts[k], ('x', 'y', 'core'), pairs))]
    reduce_sum x1 -> x0, other arithmetic: 1.37 us -> none  [local(): error_norm = jnp.sqrt(jnp.sum(total) / (rows * ff * replicas * experts))]
    ppermute x6, waiting for transfers between devices: 2.72 us -> 3.79 us  [swap(): return lax.ppermute(x, 'core', [(0, 1), (1, 0)])]
    unnamed x14 -> x10, local copies, waits for them, and re-layouts: 3.18 us -> 2.36 us
  transfers between devices with their start and end apart: 13 -> 13, of which waited for: 8 -> 9; matrix products, arithmetic and copies ran while one was open for 0% -> 0% of each run, Pallas kernels for 12% -> 12%
where the time goes in v3:
time: 98.5 us; the launch traced here: 98 us
  blocking collectives  27.6 us (28%)
  starting transfers between devices  24.6 us (25%)
  Pallas kernels  22.6 us (23%)
  waiting for transfers between devices  20 us (20%)
  local copies, waits for them, and re-layouts  2.36 us (2%)
    all_to_all x1, blocking collectives, local(): parts = lax.all_to_all(add_copies(left, swap(left), chips), CHIPS, 0, 0)  16 us
    ppermute x6, waiting for transfers between devices, shifted(): out.append(lax.ppermute(parts[k], ('x', 'y', 'core'), pairs))  14 us
    all_to_all x1, blocking collectives, local(): f_mine = lax.all_to_all(f, CHIPS, 0, 0)  11.6 us
    ppermute x6, starting transfers between devices, swap(): return lax.ppermute(x, 'core', [(0, 1), (1, 0)])  10.2 us
    all_to_all x1, starting transfers between devices, local(): lax.all_to_all(square_sum(f_mine, f_other, rank, experts), 'expert', 0, 0)  7.57 us
    ppermute x6, starting transfers between devices, shifted(): out.append(lax.ppermute(parts[k], ('x', 'y', 'core'), pairs))  6.82 us
    pallas_call x2, Pallas kernels, combine(): call(body, f'combine_{first}', rows * ff, 6 * rows * ff, vmem=vmem, in_sp...  5.25 us
    ppermute x6, waiting for transfers between devices, swap(): return lax.ppermute(x, 'core', [(0, 1), (1, 0)])  3.79 us
  transfers between devices with their start and end apart: 13, of which 9 were waited for; matrix products, arithmetic and copies ran while one was open for 0% of the time, Pallas kernels for 12%

profile of v3, /device:TPU:1, one launch (start us, length us, event | category | flops | bytes accessed | tf_op | source)
XLA Modules:
  0.0 98.0 jit_solution(1979167593320006770)
XLA Ops:
  0.6 2.5 %combine_0.1 = (bf16[16,128,256]{2,1,0:T(8,128)(2,1)S(1)}, bf16[16,128,256]{2,1,0:T(8,128)(2,1)S(1)}) custom-call(s32[1]{0:T(128)} %bitcast.core_ref, bf16[256,8192]{1,0:T(8,128)(2,1)} %bitcast.12, bf16[256,8192]{1,0:T(8,128)(2,1)} %bitcast.15), custom_call_target="tpu_custom_call" | custom-call | flops 1048576 | bytes 6291456 | tf_op jit(solution)/shard_map/combine_0/pallas_call | solution.py:65
  3.2 3.3 %collective-permute-start = (bf16[16,128,256]{2,1,0:T(8,128)(2,1)S(1)}, bf16[16,128,256]{2,1,0:T(8,128)(2,1)}, u32[]{:S(2)}, u32[]{:S(2)}) collective-permute-start(bf16[16,128,256]{2,1,0:T(8,128)(2,1)S(1)} %get-tuple-element.24.refs_2_), channel_id=1, source_target_pairs={{0,8},{8,0},{1,9},{9,1},{2,10},{10,2},{3,11},{11,3},{4,12},{12,4},... | collective-permute-start | bytes 3145736 | tf_op jit(solution)/shard_map/ppermute | solution.py:518
  6.5 2.7 %combine_128.1 = (bf16[16,128,256]{2,1,0:T(8,128)(2,1)S(1)}, bf16[16,128,256]{2,1,0:T(8,128)(2,1)}) custom-call(s32[1]{0:T(128)} %bitcast.core_ref, bf16[256,8192]{1,0:T(8,128)(2,1)S(1)} %bitcast.13, bf16[256,8192]{1,0:T(8,128)(2,1)} %bitcast.16, bf16[16,128,256]{2,1,0:T(8,128)(2,1)S(1)} %get-tuple-element.22.refs_0_), custom_call_target="tpu_custom_call" | custom-call | flops 1048576 | bytes 6291456 | tf_op jit(solution)/shard_map/combine_128/pallas_call | solution.py:65
  9.2 0.9 collective-permute-start.1
  10.2 2.1 %project.1 = (f32[16,256]{1,0:T(8,128)S(1)}, f32[16,256]{1,0:T(8,128)S(1)}) custom-call(s32[1]{0:T(128)} %bitcast.core_ref, bf16[32,8192]{1,0:T(8,128)(2,1)S(1)} %bitcast.14, bf16[16,128,256]{2,1,0:T(8,128)(2,1)S(1)} %get-tuple-element.22.refs_0_, bf16[16,128,256]{2,1,0:T(8,128)(2,1)S(1)} %get-tuple-element.23.refs_1_, ...), custom_call_target="tpu_custom_call" | custom-call | flops 134217728 | bytes 4194304 | tf_op jit(solution)/shard_map/project/pallas_call | solution.py:106
  12.5 1.1 %collective-permute-done.2.refs_5_ = f32[16,256]{1,0:T(8,128)S(1)} collective-permute-done((f32[16,256]{1,0:T(8,128)S(1)}, f32[16,256]{1,0:T(8,128)S(1)}, u32[]{:S(2)}, u32[]{:S(2)}) %collective-permute-start.2) | collective-permute-done | bytes 16416 | tf_op jit(solution)/shard_map/ppermute | solution.py:518
  13.6 2.2 %pair_sum.1 = (bf16[1056,256]{1,0:T(8,128)(2,1)S(1)}, bf16[1056,256]{1,0:T(8,128)(2,1)S(1)}, bf16[1056,256]{1,0:T(8,128)(2,1)S(1)}, bf16[1056,256]{1,0:T(8,128)(2,1)S(1)}) custom-call(s32[3]{0:T(128)S(1)} %pad_add_fusion.place_ref, bf16[16,128,256]{2,1,0:T(8,128)(2,1)S(1)} %get-tuple-element.22.refs_0_, bf16[16,128,256]{2,1,0:T(8,128)(2,1)S(1)} %get-tuple-element.23.refs_1_, ...), custom_call_target="tpu_custom_call" | custom-call | flops 6291456 | bytes 6291456 | tf_op jit(solution)/shard_map/pair_sum/pallas_call | solution.py:166
  15.9 2.2 %collective-permute-start.4 = (bf16[1056,256]{1,0:T(8,128)(2,1)S(1)}, bf16[1056,256]{1,0:T(8,128)(2,1)S(1)}, u32[]{:S(2)}, u32[]{:S(2)}) collective-permute-start(bf16[1056,256]{1,0:T(8,128)(2,1)S(1)} %get-tuple-element.30), channel_id=1, source_target_pairs={{0,128},{8,40},{16,144},{24,56},{32,160},{40,8},{48,176},{56,24},{... | collective-permute-start | bytes 1622024 | tf_op jit(solution)/shard_map/ppermute | solution.py:531
  18.0 1.1 %collective-permute-start.5 = (bf16[1056,256]{1,0:T(8,128)(2,1)S(1)}, bf16[1056,256]{1,0:T(8,128)(2,1)S(1)}, u32[]{:S(2)}, u32[]{:S(2)}) collective-permute-start(bf16[1056,256]{1,0:T(8,128)(2,1)S(1)} %get-tuple-element.31), channel_id=1, source_target_pairs={{0,192},{8,56},{16,208},{24,8},{32,224},{40,24},{48,240},{56,40},{... | collective-permute-start | bytes 1622024 | tf_op jit(solution)/shard_map/ppermute | solution.py:531
  19.1 2.1 %pair_spread.1.refs_4_ = f32[8,128]{1,0:T(8,128)S(1)} custom-call(bf16[16,128,256]{2,1,0:T(8,128)(2,1)S(1)} %get-tuple-element.22.refs_0_, bf16[16,128,256]{2,1,0:T(8,128)(2,1)S(1)} %get-tuple-element.23.refs_1_, bf16[16,128,256]{2,1,0:T(8,128)(2,1)} %collective-permute-done.refs_2_, bf16[16,128,256]{2,1,0:T(8,128)(2,1)} %collective-permute-done.1.refs_3_), custom_call_target="tpu_custom_call" | custom-call | flops 3145728 | bytes 4194304 | tf_op jit(solution)/shard_map/pair_spread/pallas_call | solution.py:199
  21.2 10.1 %collective-permute-done.3.refs_1_ = bf16[1056,256]{1,0:T(8,128)(2,1)S(1)} collective-permute-done((bf16[1056,256]{1,0:T(8,128)(2,1)S(1)}, bf16[1056,256]{1,0:T(8,128)(2,1)S(1)}, u32[]{:S(2)}, u32[]{:S(2)}) %collective-permute-start.3) | collective-permute-done | bytes 540704 | tf_op jit(solution)/shard_map/ppermute | solution.py:531
  31.4 0.6 collective-permute-done.5.refs_3_
  32.0 0.8 merge_left.1
  32.9 2.2 %collective-permute-start.7 = (bf16[288,256]{1,0:T(8,128)(2,1)S(1)}, bf16[288,256]{1,0:T(8,128)(2,1)S(1)}, u32[]{:S(2)}, u32[]{:S(2)}) collective-permute-start(bf16[288,256]{1,0:T(8,128)(2,1)S(1)} %get-tuple-element.34), channel_id=1, source_target_pairs={{0,32},{8,136},{16,48},{24,152},{32,0},{40,168},{48,16},{56,184},{... | collective-permute-start | bytes 442376 | tf_op jit(solution)/shard_map/ppermute | solution.py:531
  35.1 1.2 %collective-permute-start.8 = (bf16[288,256]{1,0:T(8,128)(2,1)S(1)}, bf16[288,256]{1,0:T(8,128)(2,1)S(1)}, u32[]{:S(2)}, u32[]{:S(2)}) collective-permute-start(bf16[288,256]{1,0:T(8,128)(2,1)S(1)} %get-tuple-element.35), channel_id=1, source_target_pairs={{0,48},{8,200},{16,0},{24,216},{32,16},{40,232},{48,32},{56,248},{... | collective-permute-start | bytes 442376 | tf_op jit(solution)/shard_map/ppermute | solution.py:531
  36.3 1.0 %spread.2.refs_4_ = f32[8,128]{1,0:T(8,128)S(1)} custom-call(bf16[1056,256]{1,0:T(8,128)(2,1)S(1)} %get-tuple-element.28.refs_0_, bf16[1056,256]{1,0:T(8,128)(2,1)S(1)} %collective-permute-done.3.refs_1_, bf16[1056,256]{1,0:T(8,128)(2,1)S(1)} %collective-permute-done.4.refs_2_, bf16[1056,256]{1,0:T(8,128)(2,1)S(1)} %collective-permute-done.5.refs_3_, ...), custom_call_target="tpu_custom_call" | custom-call | flops 3145728 | bytes 2097152 | tf_op jit(solution)/shard_map/spread/pallas_call | solution.py:265
  37.3 2.6 %collective-permute-done.6.refs_1_ = bf16[288,256]{1,0:T(8,128)(2,1)S(1)} collective-permute-done((bf16[288,256]{1,0:T(8,128)(2,1)S(1)}, bf16[288,256]{1,0:T(8,128)(2,1)S(1)}, u32[]{:S(2)}, u32[]{:S(2)}) %collective-permute-start.6) | collective-permute-done | bytes 147488 | tf_op jit(solution)/shard_map/ppermute | solution.py:531
  40.5 2.5 %collective-permute-start.9 = (f32[16,256]{1,0:T(8,128)S(1)}, f32[16,256]{1,0:T(8,128)S(1)}, u32[]{:S(2)}, u32[]{:S(2)}) collective-permute-start(f32[16,256]{1,0:T(8,128)S(1)} %left_sum.1.a_ref), channel_id=1, source_target_pairs={{0,8},{8,0},{1,9},{9,1},{2,10},{10,2},{3,11},{11,3},{4,12},{12,4},... | collective-permute-start | bytes 49160 | tf_op jit(solution)/shard_map/ppermute | solution.py:518
  43.9 1.6 %first_right.1.a_ref = f32[32,256]{1,0:T(8,128)S(1)} custom-call(s32[1]{0:T(128)} %bitcast.core_ref, f32[16,256]{1,0:T(8,128)S(1)} %left_sum.1.a_ref, f32[16,256]{1,0:T(8,128)S(1)} %collective-permute-done.9.b_ref, f32[256,256]{1,0:T(8,128)S(1)} %mean.1.m_ref, f32[8,128]{1,0:T(8,128)S(1)} %spread.3.after_ref.s_ref), custom_call_target="tpu_custom_call" | custom-call | flops 8388608 | bytes 262144 | tf_op jit(solution)/shard_map/first_right/pallas_call | solution.py:349
  45.9 0.9 collective-permute-done.10.b_ref
  46.8 16.0 %all_to_all.15.p_ref = f32[16,32,256]{2,1,0:T(8,128)S(1)} all-to-all(f32[16,32,256]{2,1,0:T(8,128)S(1)} %add_copies.1), channel_id=1, replica_groups=mesh['x'=4,'y'=4,'core'=2,'expert'=8] {'x','y'}, dimensions={0} | all-to-all | bytes 1048576 | tf_op jit(solution)/shard_map/all_to_all | solution.py:563
  62.8 1.9 %second_right.1 = (f32[32,256]{1,0:T(8,128)}, bf16[32,256]{1,0:T(8,128)(2,1)S(1)}, f32[32,256]{1,0:T(8,128)}, bf16[16,48,256]{2,1,0:T(8,128)(2,1)S(1)}) custom-call(f32[16,32,256]{2,1,0:T(8,128)S(1)} %all_to_all.15.p_ref, f32[256,256]{1,0:T(8,128)S(1)} %mean.1.m_ref, f32[8,128]{1,0:T(8,128)S(1)} %spread.3.after_ref.s_ref), custom_call_target="tpu_custom_call" | custom-call | flops 8388608 | bytes 524288 | tf_op jit(solution)/shard_map/second_right/pallas_call | solution.py:406
  64.7 11.6 %all_to_all.16.fa_ref.a_ref = bf16[16,48,256]{2,1,0:T(8,128)(2,1)S(1)} all-to-all(bf16[16,48,256]{2,1,0:T(8,128)(2,1)S(1)} %get-tuple-element.39), channel_id=1, replica_groups=mesh['x'=4,'y'=4,'core'=2,'expert'=8] {'x','y'}, dimensions={0} | all-to-all | bytes 786432 | tf_op jit(solution)/shard_map/all_to_all | solution.py:566
  76.2 2.9 %collective-permute-start.11 = (bf16[16,48,256]{2,1,0:T(8,128)(2,1)S(1)}, bf16[16,48,256]{2,1,0:T(8,128)(2,1)S(1)}, u32[]{:S(2)}, u32[]{:S(2)}) collective-permute-start(bf16[16,48,256]{2,1,0:T(8,128)(2,1)S(1)} %all_to_all.16.fa_ref.a_ref), channel_id=1, source_target_pairs={{0,8},{8,0},{1,9},{9,1},{2,10},{10,2},{3,11},{11,3},{4,12},{12,4},... | collective-permute-start | bytes 1179656 | tf_op jit(solution)/shard_map/ppermute | solution.py:518
  79.1 1.3 %collective-permute-done.11.fb_ref.b_hbm = bf16[16,48,256]{2,1,0:T(8,128)(2,1)S(1)} collective-permute-done((bf16[16,48,256]{2,1,0:T(8,128)(2,1)S(1)}, bf16[16,48,256]{2,1,0:T(8,128)(2,1)S(1)}, u32[]{:S(2)}, u32[]{:S(2)}) %collective-permute-start.11) | collective-permute-done | bytes 393248 | tf_op jit(solution)/shard_map/ppermute | solution.py:518
  80.6 0.7 copy-done.1
  81.3 0.6 copy-done.4
  82.0 7.6 %all-to-all-start.2 = ((f32[8,8,128]{2,1,0:T(8,128)}), f32[8,8,128]{2,1,0:T(8,128)}, u32[]{:S(2)}, u32[]{:S(2)}) async-start(f32[8,8,128]{2,1,0:T(8,128)} %copy-done.4), calls=%async_computation.2 | async-start | bytes 65536 | tf_op jit(solution)/shard_map/all_to_all | solution.py:568
  89.5 1.0 %copy-done.2 = bf16[16,48,256]{2,1,0:T(8,128)(2,1)S(1)} copy-done((bf16[16,48,256]{2,1,0:T(8,128)(2,1)S(1)}, bf16[16,48,256]{2,1,0:T(8,128)(2,1)}, u32[]{:S(2)}) %copy-start.2) | copy-done | bytes 393240
  90.5 3.8 %residual.1 = bf16[256,8192]{1,0:T(8,128)(2,1)} custom-call(s32[1]{0:T(128)} %bitcast.core_ref, bf16[32,256]{1,0:T(8,128)(2,1)S(1)} %get-tuple-element.38.low_ref, bf16[16,48,256]{2,1,0:T(8,128)(2,1)S(1)} %all_to_all.16.fa_ref.a_ref, bf16[16,48,256]{2,1,0:T(8,128)(2,1)S(1)} %copy-done.2, bf16[16,128,256]{2,1,0:T(8,128)(2,1)S(1)} %get-tuple-element.22.refs_0_, ...), custom_call_target="tpu_custom_call" | custom-call | flops 134217728 | bytes 8388608 | tf_op jit(solution)/shard_map/residual/pallas_call | solution.py:499
  94.3 2.3 %all-to-all-done.2.t_ref = f32[8,8,128]{2,1,0:T(8,128)} async-done(((f32[8,8,128]{2,1,0:T(8,128)}), f32[8,8,128]{2,1,0:T(8,128)}, u32[]{:S(2)}, u32[]{:S(2)}) %all-to-all-start.2) | async-done | bytes 32800 | tf_op jit(solution)/shard_map/all_to_all | solution.py:568
  96.6 1.4 %root_mean.1 = f32[1,1]{1,0:T(1,128)} custom-call(f32[8,8,128]{2,1,0:T(8,128)} %all-to-all-done.2.t_ref), custom_call_target="tpu_custom_call" | custom-call | flops 8192 | bytes 32768 | tf_op jit(solution)/shard_map/root_mean/pallas_call | solution.py:458
  (23 shorter events, 2.4 us)
Async XLA Ops:
  0.6 5.9 %copy-start = (bf16[1,1,256,8192]{3,2,1,0:T(8,128)(2,1)S(1)}, bf16[1,1,256,8192]{3,2,1,0:T(8,128)(2,1)}, u32[]{:S(2)}) copy-start(bf16[1,1,256,8192]{3,2,1,0:T(8,128)(2,1)} %param.3) | copy-start | bytes 12582916
  3.2 10.4 %collective-permute-start = (bf16[16,128,256]{2,1,0:T(8,128)(2,1)S(1)}, bf16[16,128,256]{2,1,0:T(8,128)(2,1)}, u32[]{:S(2)}, u32[]{:S(2)}) collective-permute-start(bf16[16,128,256]{2,1,0:T(8,128)(2,1)S(1)} %get-tuple-element.24.refs_2_), channel_id=1, source_target_pairs={{0,8},{8,0},{1,9},{9,1},{2,10},{10,2},{3,11},{11,3},{4,12},{12,4},... | collective-permute-start | bytes 3145736 | tf_op jit(solution)/shard_map/ppermute | solution.py:518
  6.5 3.7 %copy-start.3 = (bf16[1,32,8192]{2,1,0:T(8,128)(2,1)S(1)}, bf16[1,32,8192]{2,1,0:T(8,128)(2,1)}, u32[]{:S(2)}) copy-start(bf16[1,32,8192]{2,1,0:T(8,128)(2,1)} %param.5) | copy-start | bytes 1572868
  9.2 4.3 %collective-permute-start.1 = (bf16[16,128,256]{2,1,0:T(8,128)(2,1)}, bf16[16,128,256]{2,1,0:T(8,128)(2,1)}, u32[]{:S(2)}, u32[]{:S(2)}) collective-permute-start(bf16[16,128,256]{2,1,0:T(8,128)(2,1)} %get-tuple-element.25.refs_3_), channel_id=1, source_target_pairs={{0,8},{8,0},{1,9},{9,1},{2,10},{10,2},{3,11},{11,3},{4,12},{12,4},... | collective-permute-start | bytes 3145736 | tf_op jit(solution)/shard_map/ppermute | solution.py:518
  12.3 1.3 %collective-permute-start.2 = (f32[16,256]{1,0:T(8,128)S(1)}, f32[16,256]{1,0:T(8,128)S(1)}, u32[]{:S(2)}, u32[]{:S(2)}) collective-permute-start(f32[16,256]{1,0:T(8,128)S(1)} %get-tuple-element.27), channel_id=1, source_target_pairs={{0,8},{8,0},{1,9},{9,1},{2,10},{10,2},{3,11},{11,3},{4,12},{12,4},... | collective-permute-start | bytes 49160 | tf_op jit(solution)/shard_map/ppermute | solution.py:518
  15.8 15.6 %collective-permute-start.3 = (bf16[1056,256]{1,0:T(8,128)(2,1)S(1)}, bf16[1056,256]{1,0:T(8,128)(2,1)S(1)}, u32[]{:S(2)}, u32[]{:S(2)}) collective-permute-start(bf16[1056,256]{1,0:T(8,128)(2,1)S(1)} %get-tuple-element.29), channel_id=1, source_target_pairs={{0,64},{8,24},{16,80},{24,40},{32,96},{40,56},{48,112},{56,8},{64,... | collective-permute-start | bytes 1622024 | tf_op jit(solution)/shard_map/ppermute | solution.py:531
  15.9 15.5 %collective-permute-start.4 = (bf16[1056,256]{1,0:T(8,128)(2,1)S(1)}, bf16[1056,256]{1,0:T(8,128)(2,1)S(1)}, u32[]{:S(2)}, u32[]{:S(2)}) collective-permute-start(bf16[1056,256]{1,0:T(8,128)(2,1)S(1)} %get-tuple-element.30), channel_id=1, source_target_pairs={{0,128},{8,40},{16,144},{24,56},{32,160},{40,8},{48,176},{56,24},{... | collective-permute-start | bytes 1622024 | tf_op jit(solution)/shard_map/ppermute | solution.py:531
  18.0 13.9 %collective-permute-start.5 = (bf16[1056,256]{1,0:T(8,128)(2,1)S(1)}, bf16[1056,256]{1,0:T(8,128)(2,1)S(1)}, u32[]{:S(2)}, u32[]{:S(2)}) collective-permute-start(bf16[1056,256]{1,0:T(8,128)(2,1)S(1)} %get-tuple-element.31), channel_id=1, source_target_pairs={{0,192},{8,56},{16,208},{24,8},{32,224},{40,24},{48,240},{56,40},{... | collective-permute-start | bytes 1622024 | tf_op jit(solution)/shard_map/ppermute | solution.py:531
  32.8 7.2 %collective-permute-start.6 = (bf16[288,256]{1,0:T(8,128)(2,1)S(1)}, bf16[288,256]{1,0:T(8,128)(2,1)S(1)}, u32[]{:S(2)}, u32[]{:S(2)}) collective-permute-start(bf16[288,256]{1,0:T(8,128)(2,1)S(1)} %get-tuple-element.33), channel_id=1, source_target_pairs={{0,16},{8,72},{16,32},{24,88},{32,48},{40,104},{48,0},{56,120},{64... | collective-permute-start | bytes 442376 | tf_op jit(solution)/shard_map/ppermute | solution.py:531
  32.9 7.1 %collective-permute-start.7 = (bf16[288,256]{1,0:T(8,128)(2,1)S(1)}, bf16[288,256]{1,0:T(8,128)(2,1)S(1)}, u32[]{:S(2)}, u32[]{:S(2)}) collective-permute-start(bf16[288,256]{1,0:T(8,128)(2,1)S(1)} %get-tuple-element.34), channel_id=1, source_target_pairs={{0,32},{8,136},{16,48},{24,152},{32,0},{40,168},{48,16},{56,184},{... | collective-permute-start | bytes 442376 | tf_op jit(solution)/shard_map/ppermute | solution.py:531
  35.1 5.4 %collective-permute-start.8 = (bf16[288,256]{1,0:T(8,128)(2,1)S(1)}, bf16[288,256]{1,0:T(8,128)(2,1)S(1)}, u32[]{:S(2)}, u32[]{:S(2)}) collective-permute-start(bf16[288,256]{1,0:T(8,128)(2,1)S(1)} %get-tuple-element.35), channel_id=1, source_target_pairs={{0,48},{8,200},{16,0},{24,216},{32,16},{40,232},{48,32},{56,248},{... | collective-permute-start | bytes 442376 | tf_op jit(solution)/shard_map/ppermute | solution.py:531
  40.5 3.4 %collective-permute-start.9 = (f32[16,256]{1,0:T(8,128)S(1)}, f32[16,256]{1,0:T(8,128)S(1)}, u32[]{:S(2)}, u32[]{:S(2)}) collective-permute-start(f32[16,256]{1,0:T(8,128)S(1)} %left_sum.1.a_ref), channel_id=1, source_target_pairs={{0,8},{8,0},{1,9},{9,1},{2,10},{10,2},{3,11},{11,3},{4,12},{12,4},... | collective-permute-start | bytes 49160 | tf_op jit(solution)/shard_map/ppermute | solution.py:518
  45.5 1.3 %collective-permute-start.10 = (f32[32,256]{1,0:T(8,128)S(1)}, f32[32,256]{1,0:T(8,128)S(1)}, u32[]{:S(2)}, u32[]{:S(2)}) collective-permute-start(f32[32,256]{1,0:T(8,128)S(1)} %first_right.1.a_ref), channel_id=1, source_target_pairs={{0,8},{8,0},{1,9},{9,1},{2,10},{10,2},{3,11},{11,3},{4,12},{12,4},... | collective-permute-start | bytes 98312 | tf_op jit(solution)/shard_map/ppermute | solution.py:518
  76.2 4.2 %collective-permute-start.11 = (bf16[16,48,256]{2,1,0:T(8,128)(2,1)S(1)}, bf16[16,48,256]{2,1,0:T(8,128)(2,1)S(1)}, u32[]{:S(2)}, u32[]{:S(2)}) collective-permute-start(bf16[16,48,256]{2,1,0:T(8,128)(2,1)S(1)} %all_to_all.16.fa_ref.a_ref), channel_id=1, source_target_pairs={{0,8},{8,0},{1,9},{9,1},{2,10},{10,2},{3,11},{11,3},{4,12},{12,4},... | collective-permute-start | bytes 1179656 | tf_op jit(solution)/shard_map/ppermute | solution.py:518
  80.6 0.7 copy-start.1
  81.3 0.6 copy-start.4
  82.0 14.6 %all-to-all-start.2 = ((f32[8,8,128]{2,1,0:T(8,128)}), f32[8,8,128]{2,1,0:T(8,128)}, u32[]{:S(2)}, u32[]{:S(2)}) async-start(f32[8,8,128]{2,1,0:T(8,128)} %copy-done.4), calls=%async_computation.2 | async-start | bytes 65536 | tf_op jit(solution)/shard_map/all_to_all | solution.py:568
  89.5 1.0 %copy-start.2 = (bf16[16,48,256]{2,1,0:T(8,128)(2,1)S(1)}, bf16[16,48,256]{2,1,0:T(8,128)(2,1)}, u32[]{:S(2)}) copy-start(bf16[16,48,256]{2,1,0:T(8,128)(2,1)} %copy-done.1) | copy-start | bytes 1179652

commit v4 on v3

--- a/solution.py
+++ b/solution.py
@@ -135,25 +135,22 @@
     return high, (x - high.astype(F32)).astype(BF16)
 
 
-def pair_sum(mine, other, place, left):
+def pair_sum(mine, other, place, more):
     runs = len(mine)
     pairs, rows, width = mine[0].shape
     side = int(round(np.sqrt(pairs)))
-    half = left[0].shape[0]
     full = runs * rows
-    height = side * full + 2 * half
+    height = side * full + more
 
     def body(place_ref, *refs):
-        a_refs, b_refs, p_refs = refs[:runs], refs[runs : 2 * runs], refs[2 * runs : 2 * runs + 2]
-        outs, t_ref, sems = refs[2 * runs + 2 : -2], refs[-2], refs[-1]
+        a_refs, b_refs = refs[:runs], refs[runs : 2 * runs]
+        outs, t_ref, sems = refs[2 * runs : -2], refs[-2], refs[-1]
         core, own = place_ref[2], jnp.where(place_ref[2] == 0, place_ref[0], place_ref[1])
         copies = [pltpu.make_async_copy(b_refs[r], t_ref.at[r], sems.at[r]) for r in range(runs)]
         for copy in copies:
             copy.start()
-        high, low = high_low(p_refs[0][...] + p_refs[1][...])
         for out in outs:
-            out[side * full : side * full + half] = high
-            out[side * full + half :] = low
+            out[side * full :] = jnp.zeros((more, width), BF16)
         for r in range(runs):
             copies[r].wait()
             for k in range(side):
@@ -169,11 +166,34 @@
         6 * runs * mine[0].size,
         6 * runs * mine[0].size,
         vmem=6,
-        in_specs=[IN_SMEM] + [IN_VMEM] * runs + [IN_HBM] * runs + [IN_VMEM] * 2,
+        in_specs=[IN_SMEM] + [IN_VMEM] * runs + [IN_HBM] * runs,
         out_specs=[IN_VMEM] * side,
         out_shape=[jax.ShapeDtypeStruct((height, width), BF16)] * side,
         scratch_shapes=[pltpu.VMEM((runs, pairs, rows, width), BF16), pltpu.SemaphoreType.DMA((runs,))],
-    )(place, *mine, *other, *left)
+    )(place, *mine, *other)
+
+
+def put_left(parts, a, b):
+    side = len(parts)
+    half = a.shape[0]
+    height = parts[0].shape[0]
+
+    def body(a_ref, b_ref, *refs):
+        high, low = high_low(a_ref[...] + b_ref[...])
+        for out in refs[side:]:
+            out[height - 2 * half : height - half] = high
+            out[height - half :] = low
+
+    return call(
+        body,
+        "put_left",
+        side * a.size,
+        4 * side * a.size,
+        in_specs=[IN_VMEM] * (2 + side),
+        out_specs=[IN_VMEM] * side,
+        out_shape=[jax.ShapeDtypeStruct(part.shape, BF16) for part in parts],
+        input_output_aliases={2 + k: k for k in range(side)},
+    )(a, b, *parts)
 
 
 def pair_spread(mine, other):
@@ -291,23 +311,39 @@
     )(*parts, after)
 
 
-def mean_of(runs, rows, replicas):
-    side, width = len(runs[0]), runs[0][0].shape[1]
+def mean_of(parts, rows, replicas):
+    side, width = len(parts), parts[0].shape[1]
 
     def body(*refs):
-        for r in range(len(runs)):
-            ins = refs[r * side : (r + 1) * side]
-            refs[-1][r * rows : (r + 1) * rows] = sum(ref[:rows].astype(F32) for ref in ins) * (1.0 / replicas)
+        mean_ref, terms_ref, flipped_ref = refs[side:]
+        mean = sum(ref[:rows].astype(F32) for ref in refs[:side]) * (1.0 / replicas)
+        mean_ref[...] = mean
+        high, low = high_low(mean)
+        terms_ref[0] = high
+        terms_ref[1] = low
+        high, low = high_low(mean.T)
+        flipped_ref[0] = high
+        flipped_ref[1] = low
 
     return call(
         body,
         "mean",
-        len(runs) * side * rows * width,
-        2 * len(runs) * side * rows * width,
-        in_specs=[IN_VMEM] * (len(runs) * side),
-        out_specs=IN_VMEM,
-        out_shape=jax.ShapeDtypeStruct((len(runs) * rows, width), F32),
-    )(*(part for parts in runs for part in parts))
+        side * rows * width,
+        2 * side * rows * width,
+        in_specs=[IN_VMEM] * side,
+        out_specs=[IN_VMEM] * 3,
+        out_shape=(
+            jax.ShapeDtypeStruct((rows, width), F32),
+            jax.ShapeDtypeStruct((2, rows, width), BF16),
+            jax.ShapeDtypeStruct((2, width, rows), BF16),
+        ),
+    )(*parts)
+
+
+def product(x, terms_ref):
+    return lax.dot_general(x, terms_ref[0], NN, preferred_element_type=F32) + lax.dot_general(
+        x, terms_ref[1], NN, preferred_element_type=F32
+    )
 
 
 def eliminate(p):
@@ -333,29 +369,26 @@
     return jnp.concatenate([p[:, l : l + 128] * scale for l in range(0, p.shape[1], 128)], axis=1)
 
 
-def first_right(left, other_left, mean, core, replicas, after):
+def first_right(left, other_left, terms, flipped, core, replicas, after):
     half, rows = left.shape
 
-    def body(core_ref, a_ref, b_ref, m_ref, after_ref, out_ref, p_ref):
+    def body(core_ref, a_ref, b_ref, m_ref, t_ref, after_ref, out_ref, p_ref):
         core = core_ref[0]
         p_ref[pl.ds(pl.multiple_of(core * half, half), half)] = a_ref[...]
         p_ref[pl.ds(pl.multiple_of((1 - core) * half, half), half)] = b_ref[...]
-        ortho_low = eliminate(p_ref[...] * (1.0 / replicas)).astype(BF16).astype(F32)
-        mean = m_ref[...]
-        q = lax.dot_general(ortho_low, mean, NN, precision=HIGHEST, preferred_element_type=F32)
-        low = q.astype(BF16).astype(F32)
-        out_ref[...] = lax.dot_general(low, mean, NT, precision=HIGHEST, preferred_element_type=F32)
+        ortho_low = eliminate(p_ref[...] * (1.0 / replicas)).astype(BF16)
+        out_ref[...] = product(product(ortho_low, m_ref).astype(BF16), t_ref)
 
     return call(
         body,
         "first_right",
-        8 * half * mean.size,
-        4 * mean.size,
-        in_specs=[IN_SMEM] + [IN_VMEM] * 4,
+        8 * half * terms.size,
+        4 * terms.size,
+        in_specs=[IN_SMEM] + [IN_VMEM] * 5,
         out_specs=IN_VMEM,
         out_shape=jax.ShapeDtypeStruct((2 * half, rows), F32),
         scratch_shapes=[pltpu.VMEM((2 * half, rows), F32)],
-    )(core, left, other_left, mean, after)
+    )(core, left, other_left, terms, flipped, after)
 
 
 def add_copies(a, b, copies):
@@ -373,12 +406,12 @@
     )(a, b)
 
 
-def second_right(parts, mean, spread_sum, replicas):
+def second_right(parts, mean, terms, spread_sum, replicas):
     chips, rank, rows = parts.shape
     width = mean.shape[1]
     more = 16
 
-    def body(p_ref, m_ref, s_ref, o_ref, low_ref, q_ref, f_ref):
+    def body(p_ref, m_ref, t_ref, s_ref, o_ref, low_ref, q_ref, f_ref):
         total = p_ref[0]
         for i in range(1, chips):
             total += p_ref[i]
@@ -388,7 +421,7 @@
         low = low_t.astype(F32).T.astype(BF16)
         low_ref[...] = low_t
         mean = m_ref[...]
-        q = lax.dot_general(low_t.astype(F32), mean, NN, precision=HIGHEST, preferred_element_type=F32)
+        q = product(low_t, t_ref)
         q_ref[...] = q
         f = q.astype(BF16)
         d = mean - lax.dot_general(low, f, NN, preferred_element_type=F32)
@@ -408,7 +441,7 @@
         "second_right",
         4 * rank * rows * width,
         4 * parts.size,
-        in_specs=[IN_VMEM] * 3,
+        in_specs=[IN_VMEM] * 4,
         out_specs=[IN_VMEM] * 4,
         out_shape=(
             jax.ShapeDtypeStruct((rank, rows), F32),
@@ -416,7 +449,7 @@
             jax.ShapeDtypeStruct((rank, width), F32),
             jax.ShapeDtypeStruct((chips, rank + more, width), BF16),
         ),
-    )(parts, mean, spread_sum)
+    )(parts, mean, terms, spread_sum)
 
 
 def square_sum(f_mine, f_other, rank, copies):
@@ -548,9 +581,9 @@
     mine_b, sent_b = combine(grad, error, core, run, run, 46, (mine_a,))
     came_b = swap(sent_b)
     left, left_sent = project([mine_a, mine_b], [sent_a, sent_b], q_init, core)
-    parts = pair_sum([mine_a, mine_b], [came_a, came_b], place, (left, swap(left_sent)))
-
-    parts = shifted(parts, 0)
+    came_left = swap(left_sent)
+    parts = pair_sum([mine_a, mine_b], [came_a, came_b], place, rank)
+    parts = shifted(put_left(parts, left, came_left), 0)
     squares = pair_spread([mine_a, mine_b], [came_a, came_b])
     before = spread(parts, side * rows, 0.5, [squares])
     parts = shifted(merge(parts, place, rows, squares), 1)
@@ -558,10 +591,10 @@
 
     left = left_sum(parts, rows, before)
     other_left = swap(left)
-    mean = mean_of([parts], rows, replicas)
-    left = first_right(left, other_left, mean, core, replicas, squares)
+    mean, terms, flipped = mean_of(parts, rows, replicas)
+    left = first_right(left, other_left, terms, flipped, core, replicas, squares)
     parts = lax.all_to_all(add_copies(left, swap(left), chips), CHIPS, 0, 0)
-    ortho_t, low, q, f = second_right(parts, mean, squares, replicas)
+    ortho_t, low, q, f = second_right(parts, mean, terms, squares, replicas)
 
     f_mine = lax.all_to_all(f, CHIPS, 0, 0)
     f_other = swap(f_mine)

time: 98.5 us -> 97.4 us (0.989)
  transfers between devices with their start and end apart: 13 -> 13, of which waited for: 9 -> 9; matrix products, arithmetic and copies ran while one was open for 0% -> 0% of each run, Pallas kernels for 12% -> 15%
where the time goes in v4:
time: 97.4 us; the launch traced here: 97 us
  blocking collectives  27.6 us (28%)
  starting transfers between devices  24.7 us (25%)
  Pallas kernels  22.3 us (23%)
  waiting for transfers between devices  19.2 us (20%)
  local copies, waits for them, and re-layouts  2.35 us (2%)
    all_to_all x1, blocking collectives, local(): parts = lax.all_to_all(add_copies(left, swap(left), chips), CHIPS, 0, 0)  16 us
    ppermute x6, waiting for transfers between devices, shifted(): out.append(lax.ppermute(parts[k], ('x', 'y', 'core'), pairs))  14 us
    all_to_all x1, blocking collectives, local(): f_mine = lax.all_to_all(f, CHIPS, 0, 0)  11.6 us
    ppermute x6, starting transfers between devices, swap(): return lax.ppermute(x, 'core', [(0, 1), (1, 0)])  10.3 us
    all_to_all x1, starting transfers between devices, local(): lax.all_to_all(square_sum(f_mine, f_other, rank, experts), 'expert', 0, 0)  7.57 us
    ppermute x6, starting transfers between devices, shifted(): out.append(lax.ppermute(parts[k], ('x', 'y', 'core'), pairs))  6.8 us
    pallas_call x2, Pallas kernels, combine(): call(body, f'combine_{first}', rows * ff, 6 * rows * ff, vmem=vmem, in_sp...  5.28 us
    pallas_call x1, Pallas kernels, residual(): call(body, 'residual', 2 * rank * rows * ff, 4 * rows * ff, vmem=8, in_sp...  3.78 us
  transfers between devices with their start and end apart: 13, of which 9 were waited for; matrix products, arithmetic and copies ran while one was open for 0% of the time, Pallas kernels for 15%

profile of v4, /device:TPU:1, one launch (start us, length us, event | category | flops | bytes accessed | tf_op | source)
XLA Modules:
  0.0 97.0 jit_solution(10639729971305938955)
XLA Ops:
  0.6 2.5 %combine_0.1 = (bf16[16,128,256]{2,1,0:T(8,128)(2,1)S(1)}, bf16[16,128,256]{2,1,0:T(8,128)(2,1)S(1)}) custom-call(s32[1]{0:T(128)} %bitcast.core_ref, bf16[256,8192]{1,0:T(8,128)(2,1)} %bitcast.12, bf16[256,8192]{1,0:T(8,128)(2,1)} %bitcast.15), custom_call_target="tpu_custom_call" | custom-call | flops 1048576 | bytes 6291456 | tf_op jit(solution)/shard_map/combine_0/pallas_call | solution.py:65
  3.2 3.3 %collective-permute-start.1 = (bf16[16,128,256]{2,1,0:T(8,128)(2,1)S(1)}, bf16[16,128,256]{2,1,0:T(8,128)(2,1)}, u32[]{:S(2)}, u32[]{:S(2)}) collective-permute-start(bf16[16,128,256]{2,1,0:T(8,128)(2,1)S(1)} %get-tuple-element.31.refs_2_), channel_id=1, source_target_pairs={{0,8},{8,0},{1,9},{9,1},{2,10},{10,2},{3,11},{11,3},{4,12},{12,4},... | collective-permute-start | bytes 3145736 | tf_op jit(solution)/shard_map/ppermute | solution.py:551
  6.5 2.8 %combine_128.1 = (bf16[16,128,256]{2,1,0:T(8,128)(2,1)S(1)}, bf16[16,128,256]{2,1,0:T(8,128)(2,1)}) custom-call(s32[1]{0:T(128)} %bitcast.core_ref, bf16[256,8192]{1,0:T(8,128)(2,1)S(1)} %bitcast.13, bf16[256,8192]{1,0:T(8,128)(2,1)} %bitcast.16, bf16[16,128,256]{2,1,0:T(8,128)(2,1)S(1)} %get-tuple-element.29.refs_0_), custom_call_target="tpu_custom_call" | custom-call | flops 1048576 | bytes 6291456 | tf_op jit(solution)/shard_map/combine_128/pallas_call | solution.py:65
  9.3 0.9 collective-permute-start.2
  10.2 2.1 %project.1 = (f32[16,256]{1,0:T(8,128)S(1)}, f32[16,256]{1,0:T(8,128)S(1)}) custom-call(s32[1]{0:T(128)} %bitcast.core_ref, bf16[32,8192]{1,0:T(8,128)(2,1)S(1)} %bitcast.14, bf16[16,128,256]{2,1,0:T(8,128)(2,1)S(1)} %get-tuple-element.29.refs_0_, bf16[16,128,256]{2,1,0:T(8,128)(2,1)S(1)} %get-tuple-element.30.refs_1_, ...), custom_call_target="tpu_custom_call" | custom-call | flops 134217728 | bytes 4194304 | tf_op jit(solution)/shard_map/project/pallas_call | solution.py:106
  12.8 2.2 %pair_sum.1 = (bf16[1056,256]{1,0:T(8,128)(2,1)S(1)}, bf16[1056,256]{1,0:T(8,128)(2,1)S(1)}, bf16[1056,256]{1,0:T(8,128)(2,1)S(1)}, bf16[1056,256]{1,0:T(8,128)(2,1)S(1)}) custom-call(s32[3]{0:T(128)S(1)} %pad_add_fusion.place_ref, bf16[16,128,256]{2,1,0:T(8,128)(2,1)S(1)} %get-tuple-element.29.refs_0_, bf16[16,128,256]{2,1,0:T(8,128)(2,1)S(1)} %get-tuple-element.30.refs_1_, ...), custom_call_target="tpu_custom_call" | custom-call | flops 6291456 | bytes 6291456 | tf_op jit(solution)/shard_map/pair_sum/pallas_call | solution.py:163
  15.2 2.2 %collective-permute-start.4 = (bf16[1056,256]{1,0:T(8,128)(2,1)S(1)}, bf16[1056,256]{1,0:T(8,128)(2,1)S(1)}, u32[]{:S(2)}, u32[]{:S(2)}) collective-permute-start(bf16[1056,256]{1,0:T(8,128)(2,1)S(1)} %get-tuple-element.41), channel_id=1, source_target_pairs={{0,128},{8,40},{16,144},{24,56},{32,160},{40,8},{48,176},{56,24},{... | collective-permute-start | bytes 1622024 | tf_op jit(solution)/shard_map/ppermute | solution.py:564
  17.3 1.1 %collective-permute-start.5 = (bf16[1056,256]{1,0:T(8,128)(2,1)S(1)}, bf16[1056,256]{1,0:T(8,128)(2,1)S(1)}, u32[]{:S(2)}, u32[]{:S(2)}) collective-permute-start(bf16[1056,256]{1,0:T(8,128)(2,1)S(1)} %get-tuple-element.42), channel_id=1, source_target_pairs={{0,192},{8,56},{16,208},{24,8},{32,224},{40,24},{48,240},{56,40},{... | collective-permute-start | bytes 1622024 | tf_op jit(solution)/shard_map/ppermute | solution.py:564
  18.4 2.1 %pair_spread.1.refs_4_ = f32[8,128]{1,0:T(8,128)S(1)} custom-call(bf16[16,128,256]{2,1,0:T(8,128)(2,1)S(1)} %get-tuple-element.29.refs_0_, bf16[16,128,256]{2,1,0:T(8,128)(2,1)S(1)} %get-tuple-element.30.refs_1_, bf16[16,128,256]{2,1,0:T(8,128)(2,1)} %collective-permute-done.1.refs_2_, bf16[16,128,256]{2,1,0:T(8,128)(2,1)} %collective-permute-done.2.refs_3_), custom_call_target="tpu_custom_call" | custom-call | flops 3145728 | bytes 4194304 | tf_op jit(solution)/shard_map/pair_spread/pallas_call | solution.py:219
  20.5 10.1 %collective-permute-done.3.refs_1_ = bf16[1056,256]{1,0:T(8,128)(2,1)S(1)} collective-permute-done((bf16[1056,256]{1,0:T(8,128)(2,1)S(1)}, bf16[1056,256]{1,0:T(8,128)(2,1)S(1)}, u32[]{:S(2)}, u32[]{:S(2)}) %collective-permute-start.3) | collective-permute-done | bytes 540704 | tf_op jit(solution)/shard_map/ppermute | solution.py:564
  30.7 0.6 collective-permute-done.5.refs_3_
  31.3 0.8 merge_left.1
  32.2 2.2 %collective-permute-start.7 = (bf16[288,256]{1,0:T(8,128)(2,1)S(1)}, bf16[288,256]{1,0:T(8,128)(2,1)S(1)}, u32[]{:S(2)}, u32[]{:S(2)}) collective-permute-start(bf16[288,256]{1,0:T(8,128)(2,1)S(1)} %get-tuple-element.45), channel_id=1, source_target_pairs={{0,32},{8,136},{16,48},{24,152},{32,0},{40,168},{48,16},{56,184},{... | collective-permute-start | bytes 442376 | tf_op jit(solution)/shard_map/ppermute | solution.py:564
  34.4 1.2 %collective-permute-start.8 = (bf16[288,256]{1,0:T(8,128)(2,1)S(1)}, bf16[288,256]{1,0:T(8,128)(2,1)S(1)}, u32[]{:S(2)}, u32[]{:S(2)}) collective-permute-start(bf16[288,256]{1,0:T(8,128)(2,1)S(1)} %get-tuple-element.46), channel_id=1, source_target_pairs={{0,48},{8,200},{16,0},{24,216},{32,16},{40,232},{48,32},{56,248},{... | collective-permute-start | bytes 442376 | tf_op jit(solution)/shard_map/ppermute | solution.py:564
  35.6 1.0 %spread.2.refs_4_ = f32[8,128]{1,0:T(8,128)S(1)} custom-call(bf16[1056,256]{1,0:T(8,128)(2,1)S(1)} %get-tuple-element.39.refs_0_, bf16[1056,256]{1,0:T(8,128)(2,1)S(1)} %collective-permute-done.3.refs_1_, bf16[1056,256]{1,0:T(8,128)(2,1)S(1)} %collective-permute-done.4.refs_2_, bf16[1056,256]{1,0:T(8,128)(2,1)S(1)} %collective-permute-done.5.refs_3_, ...), custom_call_target="tpu_custom_call" | custom-call | flops 3145728 | bytes 2097152 | tf_op jit(solution)/shard_map/spread/pallas_call | solution.py:285
  36.6 2.7 %collective-permute-done.6.refs_1_ = bf16[288,256]{1,0:T(8,128)(2,1)S(1)} collective-permute-done((bf16[288,256]{1,0:T(8,128)(2,1)S(1)}, bf16[288,256]{1,0:T(8,128)(2,1)S(1)}, u32[]{:S(2)}, u32[]{:S(2)}) %collective-permute-start.6) | collective-permute-done | bytes 147488 | tf_op jit(solution)/shard_map/ppermute | solution.py:564
  39.2 0.6 collective-permute-done.8.refs_3_
  39.8 2.7 %collective-permute-start.9 = (f32[16,256]{1,0:T(8,128)S(1)}, f32[16,256]{1,0:T(8,128)S(1)}, u32[]{:S(2)}, u32[]{:S(2)}) collective-permute-start(f32[16,256]{1,0:T(8,128)S(1)} %left_sum.1.a_ref), channel_id=1, source_target_pairs={{0,8},{8,0},{1,9},{9,1},{2,10},{10,2},{3,11},{11,3},{4,12},{12,4},... | collective-permute-start | bytes 49160 | tf_op jit(solution)/shard_map/ppermute | solution.py:551
  43.4 1.2 %first_right.1.a_ref = f32[32,256]{1,0:T(8,128)S(1)} custom-call(s32[1]{0:T(128)} %bitcast.core_ref, f32[16,256]{1,0:T(8,128)S(1)} %left_sum.1.a_ref, f32[16,256]{1,0:T(8,128)S(1)} %collective-permute-done.9.b_ref, bf16[2,256,256]{2,1,0:T(8,128)(2,1)S(1)} %get-tuple-element.47.m_ref.t_ref, bf16[2,256,256]{2,1,0:T(8,128)(2,1)S(1)} %get-tuple-element.48.t_ref, ...), custom_call_target="tpu_custom_call" | custom-call | flops 16777216 | bytes 524288 | tf_op jit(solution)/shard_map/first_right/pallas_call | solution.py:382
  45.0 0.9 collective-permute-done.10.b_ref
  45.9 16.0 %all_to_all.15.p_ref = f32[16,32,256]{2,1,0:T(8,128)S(1)} all-to-all(f32[16,32,256]{2,1,0:T(8,128)S(1)} %add_copies.1), channel_id=1, replica_groups=mesh['x'=4,'y'=4,'core'=2,'expert'=8] {'x','y'}, dimensions={0} | all-to-all | bytes 1048576 | tf_op jit(solution)/shard_map/all_to_all | solution.py:596
  61.9 1.8 %second_right.1 = (f32[32,256]{1,0:T(8,128)}, bf16[32,256]{1,0:T(8,128)(2,1)S(1)}, f32[32,256]{1,0:T(8,128)}, bf16[16,48,256]{2,1,0:T(8,128)(2,1)S(1)}) custom-call(f32[16,32,256]{2,1,0:T(8,128)S(1)} %all_to_all.15.p_ref, f32[256,256]{1,0:T(8,128)S(1)} %get-tuple-element.49.m_ref, bf16[2,256,256]{2,1,0:T(8,128)(2,1)S(1)} %get-tuple-element.47.m_ref.t_ref, ...), custom_call_target="tpu_custom_call" | custom-call | flops 8388608 | bytes 524288 | tf_op jit(solution)/shard_map/second_right/pallas_call | solution.py:439
  63.7 11.6 %all_to_all.16.fa_ref.a_ref = bf16[16,48,256]{2,1,0:T(8,128)(2,1)S(1)} all-to-all(bf16[16,48,256]{2,1,0:T(8,128)(2,1)S(1)} %get-tuple-element.53), channel_id=1, replica_groups=mesh['x'=4,'y'=4,'core'=2,'expert'=8] {'x','y'}, dimensions={0} | all-to-all | bytes 786432 | tf_op jit(solution)/shard_map/all_to_all | solution.py:599
  75.2 2.9 %collective-permute-start.11 = (bf16[16,48,256]{2,1,0:T(8,128)(2,1)S(1)}, bf16[16,48,256]{2,1,0:T(8,128)(2,1)S(1)}, u32[]{:S(2)}, u32[]{:S(2)}) collective-permute-start(bf16[16,48,256]{2,1,0:T(8,128)(2,1)S(1)} %all_to_all.16.fa_ref.a_ref), channel_id=1, source_target_pairs={{0,8},{8,0},{1,9},{9,1},{2,10},{10,2},{3,11},{11,3},{4,12},{12,4},... | collective-permute-start | bytes 1179656 | tf_op jit(solution)/shard_map/ppermute | solution.py:551
  78.1 1.3 %collective-permute-done.11.fb_ref.b_hbm = bf16[16,48,256]{2,1,0:T(8,128)(2,1)S(1)} collective-permute-done((bf16[16,48,256]{2,1,0:T(8,128)(2,1)S(1)}, bf16[16,48,256]{2,1,0:T(8,128)(2,1)S(1)}, u32[]{:S(2)}, u32[]{:S(2)}) %collective-permute-start.11) | collective-permute-done | bytes 393248 | tf_op jit(solution)/shard_map/ppermute | solution.py:551
  79.6 0.7 copy-done.1
  80.3 0.6 copy-done.4
  80.9 7.6 %all-to-all-start.2 = ((f32[8,8,128]{2,1,0:T(8,128)}), f32[8,8,128]{2,1,0:T(8,128)}, u32[]{:S(2)}, u32[]{:S(2)}) async-start(f32[8,8,128]{2,1,0:T(8,128)} %copy-done.4), calls=%async_computation.2 | async-start | bytes 65536 | tf_op jit(solution)/shard_map/all_to_all | solution.py:601
  88.5 1.0 %copy-done.2 = bf16[16,48,256]{2,1,0:T(8,128)(2,1)S(1)} copy-done((bf16[16,48,256]{2,1,0:T(8,128)(2,1)S(1)}, bf16[16,48,256]{2,1,0:T(8,128)(2,1)}, u32[]{:S(2)}) %copy-start.2) | copy-done | bytes 393240
  89.5 3.8 %residual.1 = bf16[256,8192]{1,0:T(8,128)(2,1)} custom-call(s32[1]{0:T(128)} %bitcast.core_ref, bf16[32,256]{1,0:T(8,128)(2,1)S(1)} %get-tuple-element.52.low_ref, bf16[16,48,256]{2,1,0:T(8,128)(2,1)S(1)} %all_to_all.16.fa_ref.a_ref, bf16[16,48,256]{2,1,0:T(8,128)(2,1)S(1)} %copy-done.2, bf16[16,128,256]{2,1,0:T(8,128)(2,1)S(1)} %get-tuple-element.29.refs_0_, ...), custom_call_target="tpu_custom_call" | custom-call | flops 134217728 | bytes 8388608 | tf_op jit(solution)/shard_map/residual/pallas_call | solution.py:532
  93.3 2.3 %all-to-all-done.2.t_ref = f32[8,8,128]{2,1,0:T(8,128)} async-done(((f32[8,8,128]{2,1,0:T(8,128)}), f32[8,8,128]{2,1,0:T(8,128)}, u32[]{:S(2)}, u32[]{:S(2)}) %all-to-all-start.2) | async-done | bytes 32800 | tf_op jit(solution)/shard_map/all_to_all | solution.py:601
  95.6 1.4 %root_mean.1 = f32[1,1]{1,0:T(1,128)} custom-call(f32[8,8,128]{2,1,0:T(8,128)} %all-to-all-done.2.t_ref), custom_call_target="tpu_custom_call" | custom-call | flops 8192 | bytes 32768 | tf_op jit(solution)/shard_map/root_mean/pallas_call | solution.py:491
  (24 shorter events, 2.0 us)
Async XLA Ops:
  0.6 5.9 %copy-start = (bf16[1,1,256,8192]{3,2,1,0:T(8,128)(2,1)S(1)}, bf16[1,1,256,8192]{3,2,1,0:T(8,128)(2,1)}, u32[]{:S(2)}) copy-start(bf16[1,1,256,8192]{3,2,1,0:T(8,128)(2,1)} %param.3) | copy-start | bytes 12582916
  3.2 9.4 %collective-permute-start.1 = (bf16[16,128,256]{2,1,0:T(8,128)(2,1)S(1)}, bf16[16,128,256]{2,1,0:T(8,128)(2,1)}, u32[]{:S(2)}, u32[]{:S(2)}) collective-permute-start(bf16[16,128,256]{2,1,0:T(8,128)(2,1)S(1)} %get-tuple-element.31.refs_2_), channel_id=1, source_target_pairs={{0,8},{8,0},{1,9},{9,1},{2,10},{10,2},{3,11},{11,3},{4,12},{12,4},... | collective-permute-start | bytes 3145736 | tf_op jit(solution)/shard_map/ppermute | solution.py:551
  6.5 3.7 %copy-start.3 = (bf16[1,32,8192]{2,1,0:T(8,128)(2,1)S(1)}, bf16[1,32,8192]{2,1,0:T(8,128)(2,1)}, u32[]{:S(2)}) copy-start(bf16[1,32,8192]{2,1,0:T(8,128)(2,1)} %param.5) | copy-start | bytes 1572868
  9.3 3.6 %collective-permute-start.2 = (bf16[16,128,256]{2,1,0:T(8,128)(2,1)}, bf16[16,128,256]{2,1,0:T(8,128)(2,1)}, u32[]{:S(2)}, u32[]{:S(2)}) collective-permute-start(bf16[16,128,256]{2,1,0:T(8,128)(2,1)} %get-tuple-element.32.refs_3_), channel_id=1, source_target_pairs={{0,8},{8,0},{1,9},{9,1},{2,10},{10,2},{3,11},{11,3},{4,12},{12,4},... | collective-permute-start | bytes 3145736 | tf_op jit(solution)/shard_map/ppermute | solution.py:551
  12.3 2.7 %collective-permute-start = (f32[16,256]{1,0:T(8,128)S(1)}, f32[16,256]{1,0:T(8,128)S(1)}, u32[]{:S(2)}, u32[]{:S(2)}) collective-permute-start(f32[16,256]{1,0:T(8,128)S(1)} %get-tuple-element.34), channel_id=1, source_target_pairs={{0,8},{8,0},{1,9},{9,1},{2,10},{10,2},{3,11},{11,3},{4,12},{12,4},... | collective-permute-start | bytes 49160 | tf_op jit(solution)/shard_map/ppermute | solution.py:551
  15.1 15.6 %collective-permute-start.3 = (bf16[1056,256]{1,0:T(8,128)(2,1)S(1)}, bf16[1056,256]{1,0:T(8,128)(2,1)S(1)}, u32[]{:S(2)}, u32[]{:S(2)}) collective-permute-start(bf16[1056,256]{1,0:T(8,128)(2,1)S(1)} %get-tuple-element.40), channel_id=1, source_target_pairs={{0,64},{8,24},{16,80},{24,40},{32,96},{40,56},{48,112},{56,8},{64,... | collective-permute-start | bytes 1622024 | tf_op jit(solution)/shard_map/ppermute | solution.py:564
  15.2 15.5 %collective-permute-start.4 = (bf16[1056,256]{1,0:T(8,128)(2,1)S(1)}, bf16[1056,256]{1,0:T(8,128)(2,1)S(1)}, u32[]{:S(2)}, u32[]{:S(2)}) collective-permute-start(bf16[1056,256]{1,0:T(8,128)(2,1)S(1)} %get-tuple-element.41), channel_id=1, source_target_pairs={{0,128},{8,40},{16,144},{24,56},{32,160},{40,8},{48,176},{56,24},{... | collective-permute-start | bytes 1622024 | tf_op jit(solution)/shard_map/ppermute | solution.py:564
  17.3 13.9 %collective-permute-start.5 = (bf16[1056,256]{1,0:T(8,128)(2,1)S(1)}, bf16[1056,256]{1,0:T(8,128)(2,1)S(1)}, u32[]{:S(2)}, u32[]{:S(2)}) collective-permute-start(bf16[1056,256]{1,0:T(8,128)(2,1)S(1)} %get-tuple-element.42), channel_id=1, source_target_pairs={{0,192},{8,56},{16,208},{24,8},{32,224},{40,24},{48,240},{56,40},{... | collective-permute-start | bytes 1622024 | tf_op jit(solution)/shard_map/ppermute | solution.py:564
  32.1 7.2 %collective-permute-start.6 = (bf16[288,256]{1,0:T(8,128)(2,1)S(1)}, bf16[288,256]{1,0:T(8,128)(2,1)S(1)}, u32[]{:S(2)}, u32[]{:S(2)}) collective-permute-start(bf16[288,256]{1,0:T(8,128)(2,1)S(1)} %get-tuple-element.44), channel_id=1, source_target_pairs={{0,16},{8,72},{16,32},{24,88},{32,48},{40,104},{48,0},{56,120},{64... | collective-permute-start | bytes 442376 | tf_op jit(solution)/shard_map/ppermute | solution.py:564
  32.2 7.1 %collective-permute-start.7 = (bf16[288,256]{1,0:T(8,128)(2,1)S(1)}, bf16[288,256]{1,0:T(8,128)(2,1)S(1)}, u32[]{:S(2)}, u32[]{:S(2)}) collective-permute-start(bf16[288,256]{1,0:T(8,128)(2,1)S(1)} %get-tuple-element.45), channel_id=1, source_target_pairs={{0,32},{8,136},{16,48},{24,152},{32,0},{40,168},{48,16},{56,184},{... | collective-permute-start | bytes 442376 | tf_op jit(solution)/shard_map/ppermute | solution.py:564
  34.4 5.4 %collective-permute-start.8 = (bf16[288,256]{1,0:T(8,128)(2,1)S(1)}, bf16[288,256]{1,0:T(8,128)(2,1)S(1)}, u32[]{:S(2)}, u32[]{:S(2)}) collective-permute-start(bf16[288,256]{1,0:T(8,128)(2,1)S(1)} %get-tuple-element.46), channel_id=1, source_target_pairs={{0,48},{8,200},{16,0},{24,216},{32,16},{40,232},{48,32},{56,248},{... | collective-permute-start | bytes 442376 | tf_op jit(solution)/shard_map/ppermute | solution.py:564
  39.8 3.6 %collective-permute-start.9 = (f32[16,256]{1,0:T(8,128)S(1)}, f32[16,256]{1,0:T(8,128)S(1)}, u32[]{:S(2)}, u32[]{:S(2)}) collective-permute-start(f32[16,256]{1,0:T(8,128)S(1)} %left_sum.1.a_ref), channel_id=1, source_target_pairs={{0,8},{8,0},{1,9},{9,1},{2,10},{10,2},{3,11},{11,3},{4,12},{12,4},... | collective-permute-start | bytes 49160 | tf_op jit(solution)/shard_map/ppermute | solution.py:551
  44.6 1.2 %collective-permute-start.10 = (f32[32,256]{1,0:T(8,128)S(1)}, f32[32,256]{1,0:T(8,128)S(1)}, u32[]{:S(2)}, u32[]{:S(2)}) collective-permute-start(f32[32,256]{1,0:T(8,128)S(1)} %first_right.1.a_ref), channel_id=1, source_target_pairs={{0,8},{8,0},{1,9},{9,1},{2,10},{10,2},{3,11},{11,3},{4,12},{12,4},... | collective-permute-start | bytes 98312 | tf_op jit(solution)/shard_map/ppermute | solution.py:551
  75.2 4.2 %collective-permute-start.11 = (bf16[16,48,256]{2,1,0:T(8,128)(2,1)S(1)}, bf16[16,48,256]{2,1,0:T(8,128)(2,1)S(1)}, u32[]{:S(2)}, u32[]{:S(2)}) collective-permute-start(bf16[16,48,256]{2,1,0:T(8,128)(2,1)S(1)} %all_to_all.16.fa_ref.a_ref), channel_id=1, source_target_pairs={{0,8},{8,0},{1,9},{9,1},{2,10},{10,2},{3,11},{11,3},{4,12},{12,4},... | collective-permute-start | bytes 1179656 | tf_op jit(solution)/shard_map/ppermute | solution.py:551
  79.6 0.7 copy-start.1
  80.3 0.6 copy-start.4
  80.9 14.6 %all-to-all-start.2 = ((f32[8,8,128]{2,1,0:T(8,128)}), f32[8,8,128]{2,1,0:T(8,128)}, u32[]{:S(2)}, u32[]{:S(2)}) async-start(f32[8,8,128]{2,1,0:T(8,128)} %copy-done.4), calls=%async_computation.2 | async-start | bytes 65536 | tf_op jit(solution)/shard_map/all_to_all | solution.py:601
  88.5 1.0 %copy-start.2 = (bf16[16,48,256]{2,1,0:T(8,128)(2,1)S(1)}, bf16[16,48,256]{2,1,0:T(8,128)(2,1)}, u32[]{:S(2)}) copy-start(bf16[16,48,256]{2,1,0:T(8,128)(2,1)} %copy-done.1) | copy-start | bytes 1179652

commit v5 on v4

--- a/solution.py
+++ b/solution.py
@@ -372,12 +372,14 @@
 def first_right(left, other_left, terms, flipped, core, replicas, after):
     half, rows = left.shape
 
-    def body(core_ref, a_ref, b_ref, m_ref, t_ref, after_ref, out_ref, p_ref):
+    def body(core_ref, a_ref, b_ref, m_ref, t_ref, after_ref, keep_ref, send_ref, p_ref):
         core = core_ref[0]
         p_ref[pl.ds(pl.multiple_of(core * half, half), half)] = a_ref[...]
         p_ref[pl.ds(pl.multiple_of((1 - core) * half, half), half)] = b_ref[...]
         ortho_low = eliminate(p_ref[...] * (1.0 / replicas)).astype(BF16)
-        out_ref[...] = product(product(ortho_low, m_ref).astype(BF16), t_ref)
+        p_ref[...] = product(product(ortho_low, m_ref).astype(BF16), t_ref)
+        keep_ref[...] = p_ref[pl.ds(pl.multiple_of(core * half, half), half)]
+        send_ref[...] = p_ref[pl.ds(pl.multiple_of((1 - core) * half, half), half)]
 
     return call(
         body,
@@ -385,8 +387,8 @@
         8 * half * terms.size,
         4 * terms.size,
         in_specs=[IN_SMEM] + [IN_VMEM] * 5,
-        out_specs=IN_VMEM,
-        out_shape=jax.ShapeDtypeStruct((2 * half, rows), F32),
+        out_specs=[IN_VMEM] * 2,
+        out_shape=[jax.ShapeDtypeStruct((half, rows), F32)] * 2,
         scratch_shapes=[pltpu.VMEM((2 * half, rows), F32)],
     )(core, left, other_left, terms, flipped, after)
 
@@ -406,16 +408,35 @@
     )(a, b)
 
 
-def second_right(parts, mean, terms, spread_sum, replicas):
-    chips, rank, rows = parts.shape
+def chip_sum(parts):
+    def body(p_ref, out_ref):
+        total = p_ref[0]
+        for i in range(1, parts.shape[0]):
+            total += p_ref[i]
+        out_ref[...] = total
+
+    return call(
+        body,
+        "chip_sum",
+        parts.size,
+        4 * parts.size,
+        in_specs=[IN_VMEM],
+        out_specs=IN_VMEM,
+        out_shape=jax.ShapeDtypeStruct(parts.shape[1:], F32),
+    )(parts)
+
+
+def second_right(left, other_left, mean, terms, spread_sum, core, chips, replicas):
+    half, rows = left.shape
+    rank = 2 * half
     width = mean.shape[1]
     more = 16
 
-    def body(p_ref, m_ref, t_ref, s_ref, o_ref, low_ref, q_ref, f_ref):
-        total = p_ref[0]
-        for i in range(1, chips):
-            total += p_ref[i]
-        ortho_t = eliminate(total)
+    def body(core_ref, a_ref, b_ref, m_ref, t_ref, s_ref, o_ref, low_ref, q_ref, f_ref, p_ref):
+        core = core_ref[0]
+        p_ref[pl.ds(pl.multiple_of(core * half, half), half)] = a_ref[...]
+        p_ref[pl.ds(pl.multiple_of((1 - core) * half, half), half)] = b_ref[...]
+        ortho_t = eliminate(p_ref[...])
         o_ref[...] = ortho_t
         low_t = ortho_t.astype(BF16)
         low = low_t.astype(F32).T.astype(BF16)
@@ -440,8 +461,8 @@
         body,
         "second_right",
         4 * rank * rows * width,
-        4 * parts.size,
-        in_specs=[IN_VMEM] * 4,
+        4 * chips * rank * width,
+        in_specs=[IN_SMEM] + [IN_VMEM] * 5,
         out_specs=[IN_VMEM] * 4,
         out_shape=(
             jax.ShapeDtypeStruct((rank, rows), F32),
@@ -449,7 +470,8 @@
             jax.ShapeDtypeStruct((rank, width), F32),
             jax.ShapeDtypeStruct((chips, rank + more, width), BF16),
         ),
-    )(parts, mean, terms, spread_sum)
+        scratch_shapes=[pltpu.VMEM((rank, rows), F32)],
+    )(core, left, other_left, mean, terms, spread_sum)
 
 
 def square_sum(f_mine, f_other, rank, copies):
@@ -592,9 +614,9 @@
     left = left_sum(parts, rows, before)
     other_left = swap(left)
     mean, terms, flipped = mean_of(parts, rows, replicas)
-    left = first_right(left, other_left, terms, flipped, core, replicas, squares)
-    parts = lax.all_to_all(add_copies(left, swap(left), chips), CHIPS, 0, 0)
-    ortho_t, low, q, f = second_right(parts, mean, terms, squares, replicas)
+    left, left_sent = first_right(left, other_left, terms, flipped, core, replicas, squares)
+    left = chip_sum(lax.all_to_all(add_copies(left, swap(left_sent), chips), CHIPS, 0, 0))
+    ortho_t, low, q, f = second_right(left, swap(left), mean, terms, squares, core, chips, replicas)
 
     f_mine = lax.all_to_all(f, CHIPS, 0, 0)
     f_other = swap(f_mine)

time: 97.4 us -> 97 us (level)
  blocking collectives: 27.6 us -> 25.6 us
    all_to_all x1, blocking collectives: 16 us -> 13.2 us  [local(): lax.all_to_all(add_copies(left, swap(left_sent), chips), CHIPS, 0, 0)]
    ppermute x6 -> x7, waiting for transfers between devices: 2.93 us -> 3.76 us  [swap(): return lax.ppermute(x, 'core', [(0, 1), (1, 0)])]
    ppermute x6 -> x7, starting transfers between devices: 10.3 us -> 11 us  [swap(): return lax.ppermute(x, 'core', [(0, 1), (1, 0)])]
  transfers between devices with their start and end apart: 13 -> 14, of which waited for: 9 -> 10; matrix products, arithmetic and copies ran while one was open for 0% -> 0% of each run, Pallas kernels for 15% -> 15%
where the time goes in v5:
time: 97 us; the launch traced here: 96.5 us
  blocking collectives  25.6 us (26%)
  starting transfers between devices  25.4 us (26%)
  Pallas kernels  22.3 us (23%)
  waiting for transfers between devices  20 us (21%)
  local copies, waits for them, and re-layouts  2.34 us (2%)
    ppermute x6, waiting for transfers between devices, shifted(): out.append(lax.ppermute(parts[k], ('x', 'y', 'core'), pairs))  14 us
    all_to_all x1, blocking collectives, local(): lax.all_to_all(add_copies(left, swap(left_sent), chips), CHIPS, 0, 0)  13.2 us
    all_to_all x1, blocking collectives, local(): f_mine = lax.all_to_all(f, CHIPS, 0, 0)  12.4 us
    ppermute x7, starting transfers between devices, swap(): return lax.ppermute(x, 'core', [(0, 1), (1, 0)])  11 us
    all_to_all x1, starting transfers between devices, local(): lax.all_to_all(square_sum(f_mine, f_other, rank, experts), 'expert', 0, 0)  7.56 us
    ppermute x6, starting transfers between devices, shifted(): out.append(lax.ppermute(parts[k], ('x', 'y', 'core'), pairs))  6.8 us
    pallas_call x2, Pallas kernels, combine(): call(body, f'combine_{first}', rows * ff, 6 * rows * ff, vmem=vmem, in_sp...  5.27 us
    pallas_call x1, Pallas kernels, residual(): call(body, 'residual', 2 * rank * rows * ff, 4 * rows * ff, vmem=8, in_sp...  3.78 us
  transfers between devices with their start and end apart: 14, of which 10 were waited for; matrix products, arithmetic and copies ran while one was open for 0% of the time, Pallas kernels for 15%

profile of v5, /device:TPU:1, one launch (start us, length us, event | category | flops | bytes accessed | tf_op | source)
XLA Modules:
  0.0 96.5 jit_solution(16252674216617954599)
XLA Ops:
  0.6 2.5 %combine_0.1 = (bf16[16,128,256]{2,1,0:T(8,128)(2,1)S(1)}, bf16[16,128,256]{2,1,0:T(8,128)(2,1)S(1)}) custom-call(s32[1]{0:T(128)} %bitcast.core_ref, bf16[256,8192]{1,0:T(8,128)(2,1)} %bitcast.12, bf16[256,8192]{1,0:T(8,128)(2,1)} %bitcast.15), custom_call_target="tpu_custom_call" | custom-call | flops 1048576 | bytes 6291456 | tf_op jit(solution)/shard_map/combine_0/pallas_call | solution.py:65
  3.2 3.3 %collective-permute-start.1 = (bf16[16,128,256]{2,1,0:T(8,128)(2,1)S(1)}, bf16[16,128,256]{2,1,0:T(8,128)(2,1)}, u32[]{:S(2)}, u32[]{:S(2)}) collective-permute-start(bf16[16,128,256]{2,1,0:T(8,128)(2,1)S(1)} %get-tuple-element.33.refs_2_), channel_id=1, source_target_pairs={{0,8},{8,0},{1,9},{9,1},{2,10},{10,2},{3,11},{11,3},{4,12},{12,4},... | collective-permute-start | bytes 3145736 | tf_op jit(solution)/shard_map/ppermute | solution.py:573
  6.5 2.8 %combine_128.1 = (bf16[16,128,256]{2,1,0:T(8,128)(2,1)S(1)}, bf16[16,128,256]{2,1,0:T(8,128)(2,1)}) custom-call(s32[1]{0:T(128)} %bitcast.core_ref, bf16[256,8192]{1,0:T(8,128)(2,1)S(1)} %bitcast.13, bf16[256,8192]{1,0:T(8,128)(2,1)} %bitcast.16, bf16[16,128,256]{2,1,0:T(8,128)(2,1)S(1)} %get-tuple-element.31.refs_0_), custom_call_target="tpu_custom_call" | custom-call | flops 1048576 | bytes 6291456 | tf_op jit(solution)/shard_map/combine_128/pallas_call | solution.py:65
  9.3 0.9 collective-permute-start.2
  10.2 2.1 %project.1 = (f32[16,256]{1,0:T(8,128)S(1)}, f32[16,256]{1,0:T(8,128)S(1)}) custom-call(s32[1]{0:T(128)} %bitcast.core_ref, bf16[32,8192]{1,0:T(8,128)(2,1)S(1)} %bitcast.14, bf16[16,128,256]{2,1,0:T(8,128)(2,1)S(1)} %get-tuple-element.31.refs_0_, bf16[16,128,256]{2,1,0:T(8,128)(2,1)S(1)} %get-tuple-element.32.refs_1_, ...), custom_call_target="tpu_custom_call" | custom-call | flops 134217728 | bytes 4194304 | tf_op jit(solution)/shard_map/project/pallas_call | solution.py:106
  12.8 2.2 %pair_sum.1 = (bf16[1056,256]{1,0:T(8,128)(2,1)S(1)}, bf16[1056,256]{1,0:T(8,128)(2,1)S(1)}, bf16[1056,256]{1,0:T(8,128)(2,1)S(1)}, bf16[1056,256]{1,0:T(8,128)(2,1)S(1)}) custom-call(s32[3]{0:T(128)S(1)} %pad_add_fusion.place_ref, bf16[16,128,256]{2,1,0:T(8,128)(2,1)S(1)} %get-tuple-element.31.refs_0_, bf16[16,128,256]{2,1,0:T(8,128)(2,1)S(1)} %get-tuple-element.32.refs_1_, ...), custom_call_target="tpu_custom_call" | custom-call | flops 6291456 | bytes 6291456 | tf_op jit(solution)/shard_map/pair_sum/pallas_call | solution.py:163
  15.2 2.2 %collective-permute-start.4 = (bf16[1056,256]{1,0:T(8,128)(2,1)S(1)}, bf16[1056,256]{1,0:T(8,128)(2,1)S(1)}, u32[]{:S(2)}, u32[]{:S(2)}) collective-permute-start(bf16[1056,256]{1,0:T(8,128)(2,1)S(1)} %get-tuple-element.43), channel_id=1, source_target_pairs={{0,128},{8,40},{16,144},{24,56},{32,160},{40,8},{48,176},{56,24},{... | collective-permute-start | bytes 1622024 | tf_op jit(solution)/shard_map/ppermute | solution.py:586
  17.3 1.1 %collective-permute-start.5 = (bf16[1056,256]{1,0:T(8,128)(2,1)S(1)}, bf16[1056,256]{1,0:T(8,128)(2,1)S(1)}, u32[]{:S(2)}, u32[]{:S(2)}) collective-permute-start(bf16[1056,256]{1,0:T(8,128)(2,1)S(1)} %get-tuple-element.44), channel_id=1, source_target_pairs={{0,192},{8,56},{16,208},{24,8},{32,224},{40,24},{48,240},{56,40},{... | collective-permute-start | bytes 1622024 | tf_op jit(solution)/shard_map/ppermute | solution.py:586
  18.4 2.1 %pair_spread.1.refs_4_ = f32[8,128]{1,0:T(8,128)S(1)} custom-call(bf16[16,128,256]{2,1,0:T(8,128)(2,1)S(1)} %get-tuple-element.31.refs_0_, bf16[16,128,256]{2,1,0:T(8,128)(2,1)S(1)} %get-tuple-element.32.refs_1_, bf16[16,128,256]{2,1,0:T(8,128)(2,1)} %collective-permute-done.1.refs_2_, bf16[16,128,256]{2,1,0:T(8,128)(2,1)} %collective-permute-done.2.refs_3_), custom_call_target="tpu_custom_call" | custom-call | flops 3145728 | bytes 4194304 | tf_op jit(solution)/shard_map/pair_spread/pallas_call | solution.py:219
  20.5 10.1 %collective-permute-done.3.refs_1_ = bf16[1056,256]{1,0:T(8,128)(2,1)S(1)} collective-permute-done((bf16[1056,256]{1,0:T(8,128)(2,1)S(1)}, bf16[1056,256]{1,0:T(8,128)(2,1)S(1)}, u32[]{:S(2)}, u32[]{:S(2)}) %collective-permute-start.3) | collective-permute-done | bytes 540704 | tf_op jit(solution)/shard_map/ppermute | solution.py:586
  30.6 0.6 collective-permute-done.5.refs_3_
  31.3 0.8 merge_left.1
  32.2 2.2 %collective-permute-start.7 = (bf16[288,256]{1,0:T(8,128)(2,1)S(1)}, bf16[288,256]{1,0:T(8,128)(2,1)S(1)}, u32[]{:S(2)}, u32[]{:S(2)}) collective-permute-start(bf16[288,256]{1,0:T(8,128)(2,1)S(1)} %get-tuple-element.47), channel_id=1, source_target_pairs={{0,32},{8,136},{16,48},{24,152},{32,0},{40,168},{48,16},{56,184},{... | collective-permute-start | bytes 442376 | tf_op jit(solution)/shard_map/ppermute | solution.py:586
  34.4 1.2 %collective-permute-start.8 = (bf16[288,256]{1,0:T(8,128)(2,1)S(1)}, bf16[288,256]{1,0:T(8,128)(2,1)S(1)}, u32[]{:S(2)}, u32[]{:S(2)}) collective-permute-start(bf16[288,256]{1,0:T(8,128)(2,1)S(1)} %get-tuple-element.48), channel_id=1, source_target_pairs={{0,48},{8,200},{16,0},{24,216},{32,16},{40,232},{48,32},{56,248},{... | collective-permute-start | bytes 442376 | tf_op jit(solution)/shard_map/ppermute | solution.py:586
  35.6 1.0 %spread.2.refs_4_ = f32[8,128]{1,0:T(8,128)S(1)} custom-call(bf16[1056,256]{1,0:T(8,128)(2,1)S(1)} %get-tuple-element.41.refs_0_, bf16[1056,256]{1,0:T(8,128)(2,1)S(1)} %collective-permute-done.3.refs_1_, bf16[1056,256]{1,0:T(8,128)(2,1)S(1)} %collective-permute-done.4.refs_2_, bf16[1056,256]{1,0:T(8,128)(2,1)S(1)} %collective-permute-done.5.refs_3_, ...), custom_call_target="tpu_custom_call" | custom-call | flops 3145728 | bytes 2097152 | tf_op jit(solution)/shard_map/spread/pallas_call | solution.py:285
  36.6 2.7 %collective-permute-done.6.refs_1_ = bf16[288,256]{1,0:T(8,128)(2,1)S(1)} collective-permute-done((bf16[288,256]{1,0:T(8,128)(2,1)S(1)}, bf16[288,256]{1,0:T(8,128)(2,1)S(1)}, u32[]{:S(2)}, u32[]{:S(2)}) %collective-permute-start.6) | collective-permute-done | bytes 147488 | tf_op jit(solution)/shard_map/ppermute | solution.py:586
  39.8 2.7 %collective-permute-start.9 = (f32[16,256]{1,0:T(8,128)S(1)}, f32[16,256]{1,0:T(8,128)S(1)}, u32[]{:S(2)}, u32[]{:S(2)}) collective-permute-start(f32[16,256]{1,0:T(8,128)S(1)} %left_sum.1.a_ref), channel_id=1, source_target_pairs={{0,8},{8,0},{1,9},{9,1},{2,10},{10,2},{3,11},{11,3},{4,12},{12,4},... | collective-permute-start | bytes 49160 | tf_op jit(solution)/shard_map/ppermute | solution.py:573
  43.4 1.2 %first_right.1 = (f32[16,256]{1,0:T(8,128)S(1)}, f32[16,256]{1,0:T(8,128)S(1)}) custom-call(s32[1]{0:T(128)} %bitcast.core_ref, f32[16,256]{1,0:T(8,128)S(1)} %left_sum.1.a_ref, f32[16,256]{1,0:T(8,128)S(1)} %collective-permute-done.9.b_ref, bf16[2,256,256]{2,1,0:T(8,128)(2,1)S(1)} %get-tuple-element.49.m_ref.t_ref, ...), custom_call_target="tpu_custom_call" | custom-call | flops 16777216 | bytes 524288 | tf_op jit(solution)/shard_map/first_right/pallas_call | solution.py:384
  45.1 0.8 collective-permute-done.10.b_ref
  45.9 13.2 %all_to_all.15.p_ref = f32[16,16,256]{2,1,0:T(8,128)S(1)} all-to-all(f32[16,16,256]{2,1,0:T(8,128)S(1)} %add_copies.1), channel_id=1, replica_groups=mesh['x'=4,'y'=4,'core'=2,'expert'=8] {'x','y'}, dimensions={0} | all-to-all | bytes 524288 | tf_op jit(solution)/shard_map/all_to_all | solution.py:618
  59.2 2.0 %collective-permute-start.11 = (f32[16,256]{1,0:T(8,128)S(1)}, f32[16,256]{1,0:T(8,128)S(1)}, u32[]{:S(2)}, u32[]{:S(2)}) collective-permute-start(f32[16,256]{1,0:T(8,128)S(1)} %chip_sum.1.a_ref), channel_id=1, source_target_pairs={{0,8},{8,0},{1,9},{9,1},{2,10},{10,2},{3,11},{11,3},{4,12},{12,4},... | collective-permute-start | bytes 49160 | tf_op jit(solution)/shard_map/ppermute | solution.py:573
  61.1 0.8 collective-permute-done.11.b_ref
  62.0 1.8 %second_right.1 = (f32[32,256]{1,0:T(8,128)}, bf16[32,256]{1,0:T(8,128)(2,1)S(1)}, f32[32,256]{1,0:T(8,128)}, bf16[16,48,256]{2,1,0:T(8,128)(2,1)S(1)}) custom-call(s32[1]{0:T(128)} %bitcast.core_ref, f32[16,256]{1,0:T(8,128)S(1)} %chip_sum.1.a_ref, f32[16,256]{1,0:T(8,128)S(1)} %collective-permute-done.11.b_ref, f32[256,256]{1,0:T(8,128)S(1)} %get-tuple-element.53.m_ref, ...), custom_call_target="tpu_custom_call" | custom-call | flops 8388608 | bytes 524288 | tf_op jit(solution)/shard_map/second_right/pallas_call | solution.py:460
  63.7 12.4 %all_to_all.16.fa_ref.a_ref = bf16[16,48,256]{2,1,0:T(8,128)(2,1)S(1)} all-to-all(bf16[16,48,256]{2,1,0:T(8,128)(2,1)S(1)} %get-tuple-element.57), channel_id=1, replica_groups=mesh['x'=4,'y'=4,'core'=2,'expert'=8] {'x','y'}, dimensions={0} | all-to-all | bytes 786432 | tf_op jit(solution)/shard_map/all_to_all | solution.py:621
  76.1 1.5 %collective-permute-start.12 = (bf16[16,48,256]{2,1,0:T(8,128)(2,1)S(1)}, bf16[16,48,256]{2,1,0:T(8,128)(2,1)S(1)}, u32[]{:S(2)}, u32[]{:S(2)}) collective-permute-start(bf16[16,48,256]{2,1,0:T(8,128)(2,1)S(1)} %all_to_all.16.fa_ref.a_ref), channel_id=1, source_target_pairs={{0,8},{8,0},{1,9},{9,1},{2,10},{10,2},{3,11},{11,3},{4,12},{12,4},... | collective-permute-start | bytes 1179656 | tf_op jit(solution)/shard_map/ppermute | solution.py:573
  77.6 1.3 %collective-permute-done.12.fb_ref.b_hbm = bf16[16,48,256]{2,1,0:T(8,128)(2,1)S(1)} collective-permute-done((bf16[16,48,256]{2,1,0:T(8,128)(2,1)S(1)}, bf16[16,48,256]{2,1,0:T(8,128)(2,1)S(1)}, u32[]{:S(2)}, u32[]{:S(2)}) %collective-permute-start.12) | collective-permute-done | bytes 393248 | tf_op jit(solution)/shard_map/ppermute | solution.py:573
  79.1 0.7 copy-done.1
  80.4 7.6 %all-to-all-start.2 = ((f32[8,8,128]{2,1,0:T(8,128)}), f32[8,8,128]{2,1,0:T(8,128)}, u32[]{:S(2)}, u32[]{:S(2)}) async-start(f32[8,8,128]{2,1,0:T(8,128)} %copy-done.4), calls=%async_computation.2 | async-start | bytes 65536 | tf_op jit(solution)/shard_map/all_to_all | solution.py:623
  88.0 1.0 %copy-done.2 = bf16[16,48,256]{2,1,0:T(8,128)(2,1)S(1)} copy-done((bf16[16,48,256]{2,1,0:T(8,128)(2,1)S(1)}, bf16[16,48,256]{2,1,0:T(8,128)(2,1)}, u32[]{:S(2)}) %copy-start.2) | copy-done | bytes 393240
  89.0 3.8 %residual.1 = bf16[256,8192]{1,0:T(8,128)(2,1)} custom-call(s32[1]{0:T(128)} %bitcast.core_ref, bf16[32,256]{1,0:T(8,128)(2,1)S(1)} %get-tuple-element.56.low_ref, bf16[16,48,256]{2,1,0:T(8,128)(2,1)S(1)} %all_to_all.16.fa_ref.a_ref, bf16[16,48,256]{2,1,0:T(8,128)(2,1)S(1)} %copy-done.2, bf16[16,128,256]{2,1,0:T(8,128)(2,1)S(1)} %get-tuple-element.31.refs_0_, ...), custom_call_target="tpu_custom_call" | custom-call | flops 134217728 | bytes 8388608 | tf_op jit(solution)/shard_map/residual/pallas_call | solution.py:554
  92.8 2.3 %all-to-all-done.2.t_ref = f32[8,8,128]{2,1,0:T(8,128)} async-done(((f32[8,8,128]{2,1,0:T(8,128)}), f32[8,8,128]{2,1,0:T(8,128)}, u32[]{:S(2)}, u32[]{:S(2)}) %all-to-all-start.2) | async-done | bytes 32800 | tf_op jit(solution)/shard_map/all_to_all | solution.py:623
  95.1 1.4 %root_mean.1 = f32[1,1]{1,0:T(1,128)} custom-call(f32[8,8,128]{2,1,0:T(8,128)} %all-to-all-done.2.t_ref), custom_call_target="tpu_custom_call" | custom-call | flops 8192 | bytes 32768 | tf_op jit(solution)/shard_map/root_mean/pallas_call | solution.py:513
  (27 shorter events, 3.3 us)
Async XLA Ops:
  0.6 5.9 %copy-start = (bf16[1,1,256,8192]{3,2,1,0:T(8,128)(2,1)S(1)}, bf16[1,1,256,8192]{3,2,1,0:T(8,128)(2,1)}, u32[]{:S(2)}) copy-start(bf16[1,1,256,8192]{3,2,1,0:T(8,128)(2,1)} %param.3) | copy-start | bytes 12582916
  3.2 9.3 %collective-permute-start.1 = (bf16[16,128,256]{2,1,0:T(8,128)(2,1)S(1)}, bf16[16,128,256]{2,1,0:T(8,128)(2,1)}, u32[]{:S(2)}, u32[]{:S(2)}) collective-permute-start(bf16[16,128,256]{2,1,0:T(8,128)(2,1)S(1)} %get-tuple-element.33.refs_2_), channel_id=1, source_target_pairs={{0,8},{8,0},{1,9},{9,1},{2,10},{10,2},{3,11},{11,3},{4,12},{12,4},... | collective-permute-start | bytes 3145736 | tf_op jit(solution)/shard_map/ppermute | solution.py:573
  6.5 3.7 %copy-start.3 = (bf16[1,32,8192]{2,1,0:T(8,128)(2,1)S(1)}, bf16[1,32,8192]{2,1,0:T(8,128)(2,1)}, u32[]{:S(2)}) copy-start(bf16[1,32,8192]{2,1,0:T(8,128)(2,1)} %param.5) | copy-start | bytes 1572868
  9.3 3.6 %collective-permute-start.2 = (bf16[16,128,256]{2,1,0:T(8,128)(2,1)}, bf16[16,128,256]{2,1,0:T(8,128)(2,1)}, u32[]{:S(2)}, u32[]{:S(2)}) collective-permute-start(bf16[16,128,256]{2,1,0:T(8,128)(2,1)} %get-tuple-element.34.refs_3_), channel_id=1, source_target_pairs={{0,8},{8,0},{1,9},{9,1},{2,10},{10,2},{3,11},{11,3},{4,12},{12,4},... | collective-permute-start | bytes 3145736 | tf_op jit(solution)/shard_map/ppermute | solution.py:573
  12.3 2.7 %collective-permute-start = (f32[16,256]{1,0:T(8,128)S(1)}, f32[16,256]{1,0:T(8,128)S(1)}, u32[]{:S(2)}, u32[]{:S(2)}) collective-permute-start(f32[16,256]{1,0:T(8,128)S(1)} %get-tuple-element.36), channel_id=1, source_target_pairs={{0,8},{8,0},{1,9},{9,1},{2,10},{10,2},{3,11},{11,3},{4,12},{12,4},... | collective-permute-start | bytes 49160 | tf_op jit(solution)/shard_map/ppermute | solution.py:573
  15.1 15.6 %collective-permute-start.3 = (bf16[1056,256]{1,0:T(8,128)(2,1)S(1)}, bf16[1056,256]{1,0:T(8,128)(2,1)S(1)}, u32[]{:S(2)}, u32[]{:S(2)}) collective-permute-start(bf16[1056,256]{1,0:T(8,128)(2,1)S(1)} %get-tuple-element.42), channel_id=1, source_target_pairs={{0,64},{8,24},{16,80},{24,40},{32,96},{40,56},{48,112},{56,8},{64,... | collective-permute-start | bytes 1622024 | tf_op jit(solution)/shard_map/ppermute | solution.py:586
  15.2 15.5 %collective-permute-start.4 = (bf16[1056,256]{1,0:T(8,128)(2,1)S(1)}, bf16[1056,256]{1,0:T(8,128)(2,1)S(1)}, u32[]{:S(2)}, u32[]{:S(2)}) collective-permute-start(bf16[1056,256]{1,0:T(8,128)(2,1)S(1)} %get-tuple-element.43), channel_id=1, source_target_pairs={{0,128},{8,40},{16,144},{24,56},{32,160},{40,8},{48,176},{56,24},{... | collective-permute-start | bytes 1622024 | tf_op jit(solution)/shard_map/ppermute | solution.py:586
  17.3 13.9 %collective-permute-start.5 = (bf16[1056,256]{1,0:T(8,128)(2,1)S(1)}, bf16[1056,256]{1,0:T(8,128)(2,1)S(1)}, u32[]{:S(2)}, u32[]{:S(2)}) collective-permute-start(bf16[1056,256]{1,0:T(8,128)(2,1)S(1)} %get-tuple-element.44), channel_id=1, source_target_pairs={{0,192},{8,56},{16,208},{24,8},{32,224},{40,24},{48,240},{56,40},{... | collective-permute-start | bytes 1622024 | tf_op jit(solution)/shard_map/ppermute | solution.py:586
  32.1 7.2 %collective-permute-start.6 = (bf16[288,256]{1,0:T(8,128)(2,1)S(1)}, bf16[288,256]{1,0:T(8,128)(2,1)S(1)}, u32[]{:S(2)}, u32[]{:S(2)}) collective-permute-start(bf16[288,256]{1,0:T(8,128)(2,1)S(1)} %get-tuple-element.46), channel_id=1, source_target_pairs={{0,16},{8,72},{16,32},{24,88},{32,48},{40,104},{48,0},{56,120},{64... | collective-permute-start | bytes 442376 | tf_op jit(solution)/shard_map/ppermute | solution.py:586
  32.2 7.1 %collective-permute-start.7 = (bf16[288,256]{1,0:T(8,128)(2,1)S(1)}, bf16[288,256]{1,0:T(8,128)(2,1)S(1)}, u32[]{:S(2)}, u32[]{:S(2)}) collective-permute-start(bf16[288,256]{1,0:T(8,128)(2,1)S(1)} %get-tuple-element.47), channel_id=1, source_target_pairs={{0,32},{8,136},{16,48},{24,152},{32,0},{40,168},{48,16},{56,184},{... | collective-permute-start | bytes 442376 | tf_op jit(solution)/shard_map/ppermute | solution.py:586
  34.4 5.4 %collective-permute-start.8 = (bf16[288,256]{1,0:T(8,128)(2,1)S(1)}, bf16[288,256]{1,0:T(8,128)(2,1)S(1)}, u32[]{:S(2)}, u32[]{:S(2)}) collective-permute-start(bf16[288,256]{1,0:T(8,128)(2,1)S(1)} %get-tuple-element.48), channel_id=1, source_target_pairs={{0,48},{8,200},{16,0},{24,216},{32,16},{40,232},{48,32},{56,248},{... | collective-permute-start | bytes 442376 | tf_op jit(solution)/shard_map/ppermute | solution.py:586
  39.8 3.6 %collective-permute-start.9 = (f32[16,256]{1,0:T(8,128)S(1)}, f32[16,256]{1,0:T(8,128)S(1)}, u32[]{:S(2)}, u32[]{:S(2)}) collective-permute-start(f32[16,256]{1,0:T(8,128)S(1)} %left_sum.1.a_ref), channel_id=1, source_target_pairs={{0,8},{8,0},{1,9},{9,1},{2,10},{10,2},{3,11},{11,3},{4,12},{12,4},... | collective-permute-start | bytes 49160 | tf_op jit(solution)/shard_map/ppermute | solution.py:573
  44.6 1.3 %collective-permute-start.10 = (f32[16,256]{1,0:T(8,128)S(1)}, f32[16,256]{1,0:T(8,128)S(1)}, u32[]{:S(2)}, u32[]{:S(2)}) collective-permute-start(f32[16,256]{1,0:T(8,128)S(1)} %get-tuple-element.52), channel_id=1, source_target_pairs={{0,8},{8,0},{1,9},{9,1},{2,10},{10,2},{3,11},{11,3},{4,12},{12,4},... | collective-permute-start | bytes 49160 | tf_op jit(solution)/shard_map/ppermute | solution.py:573
  59.2 2.8 %collective-permute-start.11 = (f32[16,256]{1,0:T(8,128)S(1)}, f32[16,256]{1,0:T(8,128)S(1)}, u32[]{:S(2)}, u32[]{:S(2)}) collective-permute-start(f32[16,256]{1,0:T(8,128)S(1)} %chip_sum.1.a_ref), channel_id=1, source_target_pairs={{0,8},{8,0},{1,9},{9,1},{2,10},{10,2},{3,11},{11,3},{4,12},{12,4},... | collective-permute-start | bytes 49160 | tf_op jit(solution)/shard_map/ppermute | solution.py:573
  76.1 2.9 %collective-permute-start.12 = (bf16[16,48,256]{2,1,0:T(8,128)(2,1)S(1)}, bf16[16,48,256]{2,1,0:T(8,128)(2,1)S(1)}, u32[]{:S(2)}, u32[]{:S(2)}) collective-permute-start(bf16[16,48,256]{2,1,0:T(8,128)(2,1)S(1)} %all_to_all.16.fa_ref.a_ref), channel_id=1, source_target_pairs={{0,8},{8,0},{1,9},{9,1},{2,10},{10,2},{3,11},{11,3},{4,12},{12,4},... | collective-permute-start | bytes 1179656 | tf_op jit(solution)/shard_map/ppermute | solution.py:573
  79.1 0.7 copy-start.1
  79.8 0.6 copy-start.4
  80.4 14.6 %all-to-all-start.2 = ((f32[8,8,128]{2,1,0:T(8,128)}), f32[8,8,128]{2,1,0:T(8,128)}, u32[]{:S(2)}, u32[]{:S(2)}) async-start(f32[8,8,128]{2,1,0:T(8,128)} %copy-done.4), calls=%async_computation.2 | async-start | bytes 65536 | tf_op jit(solution)/shard_map/all_to_all | solution.py:623
  88.0 1.0 %copy-start.2 = (bf16[16,48,256]{2,1,0:T(8,128)(2,1)S(1)}, bf16[16,48,256]{2,1,0:T(8,128)(2,1)}, u32[]{:S(2)}) copy-start(bf16[16,48,256]{2,1,0:T(8,128)(2,1)} %copy-done.1) | copy-start | bytes 1179652
